TPU v7x, 128 devices: a whole 4x4x4 slice. The times are simulated.
128 devices in a mesh: row: 64 (over z, y_lo, x, core), col: 2 (over y_hi).
Axes of the slice: x: 4, y: 4 (y_hi: 2, y_lo: 2; y = y_hi * 2 + y_lo), z: 4, core: 2. Of those that a mesh axis runs over, the one named last changes fastest.
Arguments:
- front_matrix: float32 [16384, 16384], P('row', 'col'), may hold values from -0.35 to 8.35, as said below
- row_map: int32 [64, 256], P('row'), may hold values from 0 to 16383, as said below
Outputs:
- factor_panels: float32 [16384, 768], P('row')
- parent_rows: float32 [16384, 16384], P('row', 'col')
Inputs may be any that keep to these rules, and one draw needn't show every extreme that they name: `row_map`: the rows of all blocks name every parent row exactly once. The 256 rows of one block go in runs of exactly 4 consecutive rows, each run to a different parent row block of 256 rows. `front_matrix`: Symmetric; its leading 3 * 256 x 3 * 256 block is positive definite.
All inputs are finite; a program needn't handle non-finite values.
Results may differ from a plain program's by a relative error of at most 0.0001.
Values sent between devices are 32-bit elements; how exact they have to be, the bound alone decides.
No kernel may reach another device: no remote copies, remote signals or barrier semaphores. Data moves between devices by JAX's collectives and lax.ppermute only.
A program may use at most 128 MiB of HBM per device.

v0:
```python
import jax
import jax.numpy as jnp
from jax import lax
from jax.sharding import PartitionSpec as P

NP = 3


exact_prec = lax.Precision.HIGHEST


def from_root(block, axis, holder):
    block = jnp.where(lax.axis_index(axis) == holder, block, jnp.zeros_like(block))
    return lax.psum(block, axis)


def times_rows(left_factor, piece_rows):
    return lax.dot_general(
        left_factor,
        piece_rows,
        (((1,), (1,)), ((), ())),
        precision=exact_prec,
        preferred_element_type=jnp.float32,
    )


def panel_factor(working, step_index, block_cols, row_index):
    panel_part = working[:, step_index * block_cols : (step_index + 1) * block_cols]
    panel_block = lax.all_gather(panel_part, "col", axis=1, tiled=True)
    diagonal = from_root(panel_block, "row", step_index)
    lower_factor = jnp.linalg.cholesky(diagonal)
    identity = jnp.eye(panel_block.shape[0], dtype=jnp.float32)
    inverse = lax.linalg.triangular_solve(lower_factor, identity, left_side=True, lower=True)
    result = lax.dot_general(
        panel_block,
        inverse,
        (((1,), (1,)), ((), ())),
        precision=exact_prec,
        preferred_element_type=jnp.float32,
    )
    return jnp.where(row_index >= step_index, result, 0.0)


def local(front_matrix, row_map):
    row_count, local_width = front_matrix.shape
    row_devices = lax.axis_size("row")
    block_cols = local_width // row_devices
    row_index = lax.axis_index("row")
    col_index = lax.axis_index("col")
    working = front_matrix
    panels = []
    for step_index in range(NP):
        current = panel_factor(working, step_index, block_cols, row_index)
        own_rows = lax.dynamic_slice_in_dim(current, col_index * block_cols, block_cols, 0)
        update = times_rows(current, lax.all_gather(own_rows, "row", axis=0, tiled=True))
        working = working - update
        panels.append(current)
    column_ids = lax.broadcasted_iota(jnp.int32, (1, local_width), 1)
    contribution = jnp.where((row_index >= NP) & (column_ids >= NP * block_cols), working, 0.0)
    capacity = max(1, row_count // row_devices)
    total_slots = row_devices * capacity
    targets = row_map[0] // row_count
    within = row_map[0] % row_count
    matches = (targets[:, None] == jnp.arange(row_devices, dtype=jnp.int32)[None, :]).astype(
        jnp.int32
    )
    earlier = jnp.sum((jnp.cumsum(matches, axis=0) - matches) * matches, axis=1)
    slot_ids = targets * capacity + earlier
    sources = (
        jnp.full((total_slots,), row_count, jnp.int32)
        .at[slot_ids]
        .set(jnp.arange(row_count, dtype=jnp.int32))
    )
    padded = jnp.concatenate([contribution, jnp.zeros((1, local_width), jnp.float32)], axis=0)
    outgoing = padded[sources].reshape(row_devices, capacity, local_width)
    out_index = (
        jnp.full((total_slots,), row_count, jnp.int32)
        .at[slot_ids]
        .set(within)
        .reshape(row_devices, capacity)
    )
    arrived, arrived_index = (
        lax.all_to_all(outgoing, "row", split_axis=0, concat_axis=0, tiled=True),
        lax.all_to_all(out_index, "row", split_axis=0, concat_axis=0, tiled=True),
    )
    assembled = (
        jnp.zeros((row_count + 1, local_width), jnp.float32)
        .at[arrived_index.reshape(-1)]
        .add(arrived.reshape(-1, local_width))
    )
    return (jnp.concatenate(panels, axis=1), assembled[:row_count])


def solution(mesh):
    placed = (P("row", "col"), P("row", None))
    return jax.shard_map(
        local,
        mesh=mesh,
        in_specs=placed,
        out_specs=(P("row", None), P("row", "col")),
        check_vma=False,
    )
```

profile of v0, /device:TPU:1, one launch (start us, length us, event | category | flops | bytes accessed | tf_op | source)
XLA Modules:
  0.0 2371.2 jit_solution(6497873733223411994)
XLA Ops:
  7.2 9.0 copy.27
  16.2 0.9 slice.104
  17.1 7.3 all_gather.18
  24.4 0.7 broadcast_select_fusion.2
  25.3 502.8 %all-reduce.6.cloned.1.call-done = f32[256,256]{0,1:T(8,128)} async-done(((f32[256,256]{0,1:T(8,128)}), f32[256,256]{0,1:T(8,128)}) %all-reduce.6.cloned.1.call-update) | async-done | bytes 262160 | tf_op jit(solution)/shard_map/psum | solution.py:14
  528.1 1.1 copy.28
  529.2 1.0 fusion.14
  530.2 11.7 cholesky.172
  541.9 9.8 custom-call.15
  552.3 11.7 cholesky.189
  564.0 0.7 compare_reduce_fusion.4
  566.2 4.6 while.6
  567.3 1.4 bitcast_dynamic-update-slice_fusion.6
  569.3 1.4 bitcast_dynamic-update-slice_fusion.6
  570.8 19.7 custom-call.16
  592.5 127.5 %all-gather.4.cloned.1.call-done = f32[8192,256]{0,1:T(8,128)} async-done(((f32[128,256]{0,1:T(8,128)}), f32[8192,256]{0,1:T(8,128)}) %all-gather.4.cloned.1.call-update) | async-done | bytes 8388624 | tf_op jit(solution)/shard_map/all_gather | solution.py:55
  720.0 16.9 convolution_subtract_fusion.2
  736.9 3.4 copy-done
  740.3 7.0 all_gather.20
  747.3 0.7 broadcast_select_fusion.1
  748.3 499.2 %all-reduce.8.cloned.1.call-done = f32[256,256]{0,1:T(8,128)} async-done(((f32[256,256]{0,1:T(8,128)}), f32[256,256]{0,1:T(8,128)}) %all-reduce.8.cloned.1.call-update) | async-done | bytes 262160 | tf_op jit(solution)/shard_map/psum | solution.py:14
  1247.4 1.1 copy.32
  1248.5 1.0 fusion.13
  1249.5 11.7 cholesky.206
  1261.3 9.8 custom-call.17
  1271.6 11.7 cholesky.223
  1283.4 0.7 compare_reduce_fusion.2
  1286.1 4.3 while.7
  1286.9 1.4 bitcast_dynamic-update-slice_fusion.7
  1289.0 1.4 bitcast_dynamic-update-slice_fusion.7
  1290.4 19.7 custom-call.18
  1312.2 127.5 %all-gather.6.cloned.1.call-done = f32[8192,256]{0,1:T(8,128)} async-done(((f32[128,256]{0,1:T(8,128)}), f32[8192,256]{0,1:T(8,128)}) %all-gather.6.cloned.1.call-update) | async-done | bytes 8388624 | tf_op jit(solution)/shard_map/all_gather | solution.py:55
  1439.7 16.9 convolution_subtract_fusion.1
  1456.6 3.4 copy-done.1
  1460.0 7.0 all_gather.22
  1467.0 0.7 broadcast_select_fusion
  1468.2 498.9 %all-reduce.10.cloned.1.call-done = f32[256,256]{0,1:T(8,128)} async-done(((f32[256,256]{0,1:T(8,128)}), f32[256,256]{0,1:T(8,128)}) %all-reduce.10.cloned.1.call-update) | async-done | bytes 262160 | tf_op jit(solution)/shard_map/psum | solution.py:14
  1967.1 1.1 copy.34
  1968.2 1.0 fusion.12
  1969.2 11.7 cholesky.240
  1981.0 9.8 custom-call.19
  1991.3 11.7 cholesky.257
  2003.1 0.7 compare_reduce_fusion
  2005.8 4.3 while.8
  2006.6 1.4 bitcast_dynamic-update-slice_fusion.8
  2008.7 1.4 bitcast_dynamic-update-slice_fusion.8
  2010.1 19.7 custom-call.20
  2032.8 1.4 scatter_custom_fusion
  2034.2 0.7 all_to_all.9
  2034.9 6.9 all-to-all-start
  2041.8 1.4 scatter_custom_fusion.1
  2043.2 116.0 %all-gather.8.cloned.1.call-done = f32[8192,256]{0,1:T(8,128)} async-done(((f32[128,256]{0,1:T(8,128)}), f32[8192,256]{0,1:T(8,128)}) %all-gather.8.cloned.1.call-update) | async-done | bytes 8388624 | tf_op jit(solution)/shard_map/all_gather | solution.py:55
  2159.2 20.5 fusion
  2179.7 9.1 copy.53
  2188.8 7.7 concatenate.10.clone
  2196.5 13.4 gather_fusion
  2209.9 9.8 reshape.190
  2219.7 7.9 all-to-all-start.1
  2228.1 0.7 reduce.13
  2229.0 1.1 copy.39
  2230.2 99.2 %all-to-all-done.1 = f32[64,4,8192]{2,1,0:T(4,128)} async-done(((f32[64,4,8192]{2,1,0:T(4,128)}), f32[64,4,8192]{2,1,0:T(4,128)}, u32[]{:S(2)}, u32[]{:S(2)}) %all-to-all-start.1) | async-done | bytes 8388640 | tf_op jit(solution)/shard_map/all_to_all | solution.py:83
  2329.4 10.0 reshape.249
  2339.3 16.8 scatter_custom_fusion.2
  2356.1 7.7 slice.119
  (92 shorter events, 15.3 us)
Async XLA Ops:
  7.2 520.9 %all-reduce.6.cloned.1.call-start = ((), (), s32[]{:S(2)}) async-start(), calls=%async_computation.2 | async-start | bytes 524288 | tf_op jit(solution)/shard_map/psum | solution.py:14
  25.2 694.8 %all-gather.4.cloned.1.call-start = ((), (), s32[]{:S(2)}) async-start(), calls=%async_computation.3 | async-start | bytes 8519680 | tf_op jit(solution)/shard_map/all_gather | solution.py:55
  592.5 655.0 %all-reduce.8.cloned.1.call-start = ((), (), s32[]{:S(2)}) async-start(), calls=%async_computation.4 | async-start | bytes 524288 | tf_op jit(solution)/shard_map/psum | solution.py:14
  736.9 3.4 copy-start
  748.1 691.6 %all-gather.6.cloned.1.call-start = ((), (), s32[]{:S(2)}) async-start(), calls=%async_computation.5 | async-start | bytes 8519680 | tf_op jit(solution)/shard_map/all_gather | solution.py:55
  1312.1 655.0 %all-reduce.10.cloned.1.call-start = ((), (), s32[]{:S(2)}) async-start(), calls=%async_computation.6 | async-start | bytes 524288 | tf_op jit(solution)/shard_map/psum | solution.py:14
  1312.2 719.6 %copy-start.2 = (s32[1,256]{1,0:T(1,128)S(1)}, s32[1,256]{1,0:T(1,128)}, u32[]{:S(2)}) copy-start(s32[1,256]{1,0:T(1,128)} %param.6) | copy-start | bytes 3076
  1456.6 3.4 copy-start.1
  1467.7 691.5 %all-gather.8.cloned.1.call-start = ((), (), s32[]{:S(2)}) async-start(), calls=%async_computation.7 | async-start | bytes 8519680 | tf_op jit(solution)/shard_map/all_gather | solution.py:55
  2034.9 184.8 %all-to-all-start = ((s32[64,1,4]{2,1,0:T(1,128)}), s32[64,1,4]{2,1,0:T(1,128)S(1)}, u32[]{:S(2)}, u32[]{:S(2)}) async-start(s32[64,1,4]{2,1,0:T(1,128)} %bitcast.23), calls=%async_computation | async-start | bytes 65536 | tf_op jit(solution)/shard_map/all_to_all | solution.py:84
  2219.7 109.6 %all-to-all-start.1 = ((f32[64,4,8192]{2,1,0:T(4,128)}), f32[64,4,8192]{2,1,0:T(4,128)}, u32[]{:S(2)}, u32[]{:S(2)}) async-start(f32[64,4,8192]{2,1,0:T(4,128)} %reshape.190), calls=%async_computation.1 | async-start | bytes 16777216 | tf_op jit(solution)/shard_map/all_to_all | solution.py:83
Sparse Core Ops, SparseCore 0:
  25.3 502.7 all-reduce.5
  592.6 127.3 all-gather.3
  748.2 499.2 all-reduce.7
  1312.2 127.3 all-gather.5
  1467.9 499.2 all-reduce.9
  2031.9 127.2 all-gather.7
where the time goes:
time: 2380 us; the launch traced here: 2370 us
  waiting for transfers between devices  1970 us (83%)
  other arithmetic  186 us (8%)
  local copies, waits for them, and re-layouts  97.4 us (4%)
  matrix products  59.6 us (3%)
    psum x3, waiting for transfers between devices, from_root(): return lax.psum(block, axis)  1500 us
    all_gather x3, waiting for transfers between devices, local(): lax.all_gather(own_rows, 'row', axis=0, tiled=True)  371 us
    another operation x20, other arithmetic, panel_factor(): lower_factor = jnp.linalg.cholesky(diagonal)  103 us
    all_to_all x1, waiting for transfers between devices, local(): lax.all_to_all(outgoing, 'row', split_axis=0, concat_axis=0, tiled=True)  99.2 us
    another operation x7, other arithmetic, panel_factor(): lax.linalg.triangular_solve(lower_factor, identity, left_side=True, lower...  59.1 us
    dot_general x3, matrix products, times_rows(): lax.dot_general(left_factor, piece_rows, (((1,), (1,)), ((), ())), precis...  54.3 us
  transfers between devices with their start and end apart: 8, of which 7 were waited for; matrix products, arithmetic and copies ran while one was open for 3% of the time, Pallas kernels for 0%

commit v1 on v0

v1 whole, which is shorter than its diff:
```python
import jax
import jax.numpy as jnp
from jax import lax
from jax.experimental import pallas as pl
from jax.experimental.pallas import tpu as pltpu
from jax.sharding import PartitionSpec as P

NP = 3
N_ROW = 64
CAP = 4
PW = 256

full = lax.Precision.HIGHEST


def dot_t(a, b):
    return lax.dot_general(
        a, b, (((1,), (1,)), ((), ())), precision=full, preferred_element_type=jnp.float32
    )


def dot_n(a, b):
    return lax.dot_general(
        a, b, (((1,), (0,)), ((), ())), precision=full, preferred_element_type=jnp.float32
    )


def row_id(z, y, x, k):
    return ((z * 2 + y) * 4 + x) * 2 + k


def spread(block, root):
    row = lax.axis_index("row")
    sizes = (4, 2, 4, 2)
    strides = (16, 8, 2, 1)
    start = tuple((root // s) % n for s, n in zip(strides, sizes))
    have = [start]
    value = block
    for axis in (2, 0, 1, 3):
        got = value
        for step in range(1, sizes[axis]):
            pairs = []
            for h in have:
                to = list(h)
                to[axis] = (h[axis] + step) % sizes[axis]
                pairs.append((row_id(*h), row_id(*to)))
            arrived = lax.ppermute(value, "row", pairs)
            mine = (row // strides[axis]) % sizes[axis]
            got = jnp.where(mine == (start[axis] + step) % sizes[axis], arrived, got)
        value = got
        more = []
        for h in have:
            for step in range(sizes[axis]):
                to = list(h)
                to[axis] = (h[axis] + step) % sizes[axis]
                more.append(tuple(to))
        have = more
    return value


def pack_kernel(slot_ref, rows_ref, out_ref):
    for g in range(N_ROW):
        out_ref[slot_ref[g]] = rows_ref[g * CAP : (g + 1) * CAP, :]


def pack_runs(slots, rows, tile=512):
    height, width = rows.shape
    return pl.pallas_call(
        pack_kernel,
        out_shape=jax.ShapeDtypeStruct((N_ROW, CAP, width), rows.dtype),
        grid_spec=pltpu.PrefetchScalarGridSpec(
            num_scalar_prefetch=1,
            grid=(width // tile,),
            in_specs=[pl.BlockSpec((height, tile), lambda i, s: (0, i))],
            out_specs=pl.BlockSpec((N_ROW, CAP, tile), lambda i, s: (0, 0, i)),
        ),
        cost_estimate=pl.CostEstimate(
            flops=0, bytes_accessed=2 * 4 * height * width, transcendentals=0
        ),
        name="pack_runs",
    )(slots, rows)


def inverse_factor(block):
    lower = jnp.linalg.cholesky(block)
    eye = jnp.eye(PW, dtype=jnp.float32)
    return lax.linalg.triangular_solve(lower, eye, left_side=True, lower=True)


def panel_rows(rows, w0, w1, w2, l10, l20, l21):
    a0, a1, a2 = rows[:, :PW], rows[:, PW : 2 * PW], rows[:, 2 * PW :]
    l0 = dot_t(a0, w0)
    l1 = dot_t(a1 - dot_t(l0, l10), w1)
    l2 = dot_t(a2 - dot_t(l0, l20) - dot_t(l1, l21), w2)
    return l0, l1, l2


def weave(own, other, col):
    first = jnp.where(col == 0, own, other)
    second = jnp.where(col == 0, other, own)
    parts = []
    for k in range(NP):
        parts += [first[:, k * 128 : (k + 1) * 128], second[:, k * 128 : (k + 1) * 128]]
    return jnp.concatenate(parts, axis=1)


def local(front_matrix, row_map):
    width = front_matrix.shape[1]
    row = lax.axis_index("row")
    col = lax.axis_index("col")
    swap = [(0, 1), (1, 0)]
    head = NP * 128
    own = front_matrix[:, :head]
    panel = weave(own, lax.ppermute(own, "col", swap), col)

    targets = row_map[0].reshape(N_ROW, CAP)[:, 0] // PW
    within = (row_map[0] % PW).reshape(N_ROW, CAP)
    hits = targets[None, :] == jnp.arange(N_ROW, dtype=jnp.int32)[:, None]
    outgoing = pack_runs(targets, front_matrix)
    out_index = jnp.sum(jnp.where(hits[:, :, None], within[None, :, :], 0), axis=1)
    arrived_index = lax.all_to_all(out_index, "row", split_axis=0, concat_axis=0, tiled=True)
    arrived = lax.all_to_all(outgoing, "row", split_axis=0, concat_axis=0, tiled=True)

    mine = lax.dynamic_slice_in_dim(panel, col * 128, 128, 0)
    gathered = lax.all_gather(mine, "row", axis=0, tiled=True)

    s0 = spread(panel[:, :PW], 0)
    s1 = spread(panel[:, : 2 * PW], 1)
    s2 = spread(panel, 2)
    w0 = inverse_factor(s0)
    l10 = dot_t(s1[:, :PW], w0)
    w1 = inverse_factor(s1[:, PW:] - dot_t(l10, l10))
    l20 = dot_t(s2[:, :PW], w0)
    l21 = dot_t(s2[:, PW : 2 * PW] - dot_t(l20, l10), w1)
    w2 = inverse_factor(s2[:, 2 * PW :] - dot_t(l20, l20) - dot_t(l21, l21))

    factors = panel_rows(panel, w0, w1, w2, l10, l20, l21)
    factors = jnp.concatenate(
        [jnp.where(row >= k, f, 0.0) for k, f in enumerate(factors)], axis=1
    )

    arrived = arrived.reshape(PW, width)
    own_rows = arrived[:, :head]
    rows = weave(own_rows, lax.ppermute(own_rows, "col", swap), col)
    k0, k1, k2 = panel_rows(rows, w0, w1, w2, l10, l20, l21)
    x2 = dot_n(k2, w2)
    x1 = dot_n(k1 - dot_n(x2, l21), w1)
    x0 = dot_n(k0 - dot_n(x1, l10) - dot_n(x2, l20), w0)
    x = jnp.concatenate([x0, x1, x2], axis=1)
    slots = jnp.arange(PW, dtype=jnp.int32)
    place = (arrived_index.reshape(1, PW) == slots[:, None]) & (slots[None, :] >= NP * CAP)
    place = place.astype(jnp.float32)
    update = lax.dot_general(
        dot_n(place, x),
        gathered,
        (((1,), (1,)), ((), ())),
        precision=lax.Precision.HIGH,
        preferred_element_type=jnp.float32,
    )
    column_ids = lax.broadcasted_iota(jnp.int32, (1, width), 1)
    parent = jnp.where(column_ids >= head, dot_n(place, arrived) - update, 0.0)
    return factors, parent


def solution(mesh):
    placed = (P("row", "col"), P("row", None))
    return jax.shard_map(
        local,
        mesh=mesh,
        in_specs=placed,
        out_specs=(P("row", None), P("row", "col")),
        check_vma=False,
    )
```

time: 2380 us -> 507 us (0.21)
  waiting for transfers between devices: 1970 us -> 136 us
  local copies, waits for them, and re-layouts: 97.4 us -> 32.5 us
  starting transfers between devices: 15.6 us -> 74 us
    psum x3 -> x0, waiting for transfers between devices: 1500 us -> none  [from_root(): return lax.psum(block, axis)]
    all_gather x3 -> x1, waiting for transfers between devices: 371 us -> 0.02 us  [local(): gathered = lax.all_gather(mine, 'row', axis=0, tiled=True)]
    ppermute x0 -> x26, waiting for transfers between devices: none -> 136 us  [the longest x24 122 us: spread(): arrived = lax.ppermute(value, 'row', pairs)]
    all_to_all x1, waiting for transfers between devices: 99.2 us -> 0.01 us  [local(): lax.all_to_all(outgoing, 'row', split_axis=0, concat_axis=0, tiled=True)]
    ppermute x0 -> x26, starting transfers between devices: none -> 50.4 us  [the longest x24 41 us: spread(): arrived = lax.ppermute(value, 'row', pairs)]
    dot_general x6 -> x28, matrix products: 55.5 us -> 48.3 us  [the longest x8 18.7 us: dot_n(): lax.dot_general(a, b, (((1,), (0,)), ((), ())), precision=full, preferred...]
    another operation x29 -> x27, other arithmetic: 163 us -> 163 us  [the longest x20 103 us: inverse_factor(): lower = jnp.linalg.cholesky(block)]
  transfers between devices with their start and end apart: 8 -> 29, of which waited for: 7 -> 6; matrix products, arithmetic and copies ran while one was open for 3% -> 44% of each run, Pallas kernels for 0% -> 3%
where the time goes in v1:
time: 507 us; the launch traced here: 499 us
  other arithmetic  170 us (34%)
  waiting for transfers between devices  136 us (27%)
  starting transfers between devices  74 us (15%)
  matrix products  53.9 us (11%)
  local copies, waits for them, and re-layouts  32.5 us (6%)
  between operations  19.5 us (4%)
  Pallas kernels  12.8 us (3%)
    ppermute x24, waiting for transfers between devices, spread(): arrived = lax.ppermute(value, 'row', pairs)  122 us
    another operation x20, other arithmetic, inverse_factor(): lower = jnp.linalg.cholesky(block)  103 us
    another operation x7, other arithmetic, inverse_factor(): return lax.linalg.triangular_solve(lower, eye, left_side=True, lower=True)  59.6 us
    ppermute x24, starting transfers between devices, spread(): arrived = lax.ppermute(value, 'row', pairs)  41 us
    dot_general x8, matrix products, dot_n(): lax.dot_general(a, b, (((1,), (0,)), ((), ())), precision=full, preferred...  18.7 us
    dot_general x1, matrix products, local(): lax.dot_general(dot_n(place, x), gathered, (((1,), (1,)), ((), ())), prec...  18.4 us
    all_to_all x1, starting transfers between devices, local(): lax.all_to_all(outgoing, 'row', split_axis=0, concat_axis=0, tiled=True)  16.3 us
    another operation x22, local copies, waits for them, and re-layouts, inverse_factor(): return lax.linalg.triangular_solve(lower, eye, left_side=True, lower=True)  13.9 us
  transfers between devices with their start and end apart: 29, of which 6 were waited for; matrix products, arithmetic and copies ran while one was open for 44% of the time, Pallas kernels for 3%

profile of v1, /device:TPU:1, one launch (start us, length us, event | category | flops | bytes accessed | tf_op | source)
XLA Modules:
  0.0 499.1 jit_solution(3112297264267751203)
XLA Ops:
  7.2 1.0 slice.113
  8.4 3.8 collective-permute-start
  12.2 8.6 %collective-permute-done = f32[256,384]{0,1:T(8,128)S(1)} collective-permute-done((f32[256,384]{0,1:T(8,128)S(1)}, f32[256,384]{0,1:T(8,128)S(1)}, u32[]{:S(2)}, u32[]{:S(2)}) %collective-permute-start) | collective-permute-done | bytes 393248 | tf_op jit(solution)/shard_map/ppermute | solution.py:114
  22.3 0.8 constant_dynamic-slice_fusion.3
  23.7 1.4 reduce.16
  25.4 5.2 %collective-permute-start.9 = (f32[256,512]{0,1:T(8,128)S(1)}, f32[256,512]{0,1:T(8,128)}, u32[]{:S(2)}, u32[]{:S(2)}) collective-permute-start(f32[256,512]{0,1:T(8,128)S(1)} %pad_maximum_fusion.1), channel_id=1, source_target_pairs={{2,14},{3,15}} | collective-permute-start | bytes 1572872 | tf_op jit(solution)/shard_map/ppermute | solution.py:47
  30.6 2.1 collective-permute-start.10
  34.0 1.4 collective-permute-start.3
  36.4 7.2 %all-to-all-start = ((s32[64,1,4]{2,1,0:T(1,128)}), s32[64,1,4]{2,1,0:T(1,128)}, u32[]{:S(2)}, u32[]{:S(2)}) async-start(s32[64,1,4]{2,1,0:T(1,128)} %copy.67), calls=%async_computation | async-start | bytes 65536 | tf_op jit(solution)/shard_map/all_to_all | solution.py:121
  44.1 4.1 collective-permute-start.11
  49.0 1.6 collective-permute-start.18
  50.6 1.6 collective-permute-start.19
  53.0 12.8 %pack_runs.1 = f32[64,4,8192]{2,1,0:T(4,128)} custom-call(s32[64]{0:T(128)} %copy-done.6, f32[256,8192]{1,0:T(8,128)} %rows_ref.1), custom_call_target="tpu_custom_call" | custom-call | bytes 16777216 | tf_op jit(solution)/shard_map/pack_runs/pallas_call | solution.py:68
  65.8 16.3 %all-to-all-start.1 = ((f32[64,4,8192]{2,1,0:T(4,128)}), f32[64,4,8192]{2,1,0:T(4,128)}, u32[]{:S(2)}, u32[]{:S(2)}) async-start(f32[64,4,8192]{2,1,0:T(4,128)} %pack_runs.1), calls=%async_computation.1 | async-start | bytes 16777216 | tf_op jit(solution)/shard_map/all_to_all | solution.py:122
  82.2 1.5 reduce.17
  85.4 4.7 collective-permute-start.12
  90.1 1.3 collective-permute-start.13
  91.6 1.3 collective-permute-start.14
  93.6 1.3 select_select_fusion.1
  95.0 1.6 collective-permute-start.20
  96.5 1.6 collective-permute-start.21
  98.1 55.3 %collective-permute-done.12 = f32[256,512]{0,1:T(8,128)S(1)} collective-permute-done((f32[256,512]{0,1:T(8,128)S(1)}, f32[256,512]{0,1:T(8,128)S(1)}, u32[]{:S(2)}, u32[]{:S(2)}) %collective-permute-start.12) | collective-permute-done | bytes 524320 | tf_op jit(solution)/shard_map/ppermute | solution.py:47
  153.5 1.6 collective-permute-start.22
  155.0 48.2 %collective-permute-done.13 = f32[256,512]{0,1:T(8,128)S(1)} collective-permute-done((f32[256,512]{0,1:T(8,128)S(1)}, f32[256,512]{0,1:T(8,128)S(1)}, u32[]{:S(2)}, u32[]{:S(2)}) %collective-permute-start.13) | collective-permute-done | bytes 524320 | tf_op jit(solution)/shard_map/ppermute | solution.py:47
  203.2 1.3 collective-permute-start.8
  204.5 18.2 %collective-permute-done.14 = f32[256,512]{0,1:T(8,128)S(1)} collective-permute-done((f32[256,512]{0,1:T(8,128)S(1)}, f32[256,512]{0,1:T(8,128)S(1)}, u32[]{:S(2)}, u32[]{:S(2)}) %collective-permute-start.14) | collective-permute-done | bytes 524320 | tf_op jit(solution)/shard_map/ppermute | solution.py:47
  222.8 2.3 collective-permute-start.15
  225.3 11.7 %cholesky.172 = f32[128,128]{1,0:T(8,128)S(1)} custom-call(f32[128,128]{1,0:T(8,128)S(1)} %cholesky.270), custom_call_target="Cholesky" | custom-call | tf_op jit(solution)/shard_map/jit(cholesky)/cholesky | solution.py:85
  237.1 9.8 %custom-call.15 = f32[1,128,128]{1,2,0:T(8,128)S(1)} custom-call(f32[1,128,128]{2,1,0:T(8,128)S(1)} %get-tuple-element.96), custom_call_target="InvertDiagBlocksLowerTriangular" | custom-call | tf_op jit(solution)/shard_map/jit(cholesky)/cholesky | solution.py:85
  247.4 11.7 %cholesky.189 = f32[128,128]{1,0:T(8,128)S(1)} custom-call(f32[128,128]{1,0:T(8,128)S(1)} %slice_subtract_fusion.4), custom_call_target="Cholesky" | custom-call | tf_op jit(solution)/shard_map/jit(cholesky)/cholesky | solution.py:85
  261.8 3.9 while.6
  262.4 1.3 bitcast_dynamic-update-slice_fusion.6
  264.4 1.3 bitcast_dynamic-update-slice_fusion.6
  266.3 19.7 %custom-call.16 = f32[2,128,128]{1,2,0:T(8,128)S(1)} custom-call(f32[2,128,128]{2,1,0:T(8,128)S(1)} %get-tuple-element.24), custom_call_target="InvertDiagBlocksLowerTriangular" | custom-call | tf_op jit(solution)/shard_map/triangular_solve/custom-call.0 | solution.py:87
  286.6 1.3 collective-permute-start.16
  288.3 1.1 broadcast_select_fusion.9
  289.6 2.0 collective-permute-start.23
  293.0 11.7 %cholesky.206 = f32[128,128]{1,0:T(8,128)S(1)} custom-call(f32[128,128]{1,0:T(8,128)S(1)} %cholesky.273), custom_call_target="Cholesky" | custom-call | tf_op jit(solution)/shard_map/jit(cholesky)/cholesky | solution.py:85
  304.7 9.8 %custom-call.17 = f32[1,128,128]{1,2,0:T(8,128)S(1)} custom-call(f32[1,128,128]{2,1,0:T(8,128)S(1)} %get-tuple-element.92), custom_call_target="InvertDiagBlocksLowerTriangular" | custom-call | tf_op jit(solution)/shard_map/jit(cholesky)/cholesky | solution.py:85
  315.0 11.7 %cholesky.223 = f32[128,128]{1,0:T(8,128)S(1)} custom-call(f32[128,128]{1,0:T(8,128)S(1)} %convolution_subtract_fusion.8), custom_call_target="Cholesky" | custom-call | tf_op jit(solution)/shard_map/jit(cholesky)/cholesky | solution.py:85
  329.5 5.3 %while.7 = (s32[]{:T(128)}, f32[256,256]{1,0:T(8,128)S(1)}, s32[2,2]{1,0:T(2,128)}, f32[2,128,128]{2,1,0:T(8,128)S(1)}, s32[]{:T(128)}) while((s32[]{:T(128)}, f32[256,256]{1,0:T(8,128)S(1)}, s32[2,2]{1,0:T(2,128)}, f32[2,128,128]{2,1,0:T(8,128)S(1)}, s32[]{:T(128)}) %tuple.97), condition=%wide.while_cond.clone, body=%wide.while_body.clone.sunk | while | flops 2 | bytes 131189 | solution.py:87
  330.8 1.4 bitcast_dynamic-update-slice_fusion.7
  333.4 1.4 bitcast_dynamic-update-slice_fusion.7
  334.8 19.7 %custom-call.18 = f32[2,128,128]{1,2,0:T(8,128)S(1)} custom-call(f32[2,128,128]{2,1,0:T(8,128)S(1)} %get-tuple-element.25), custom_call_target="InvertDiagBlocksLowerTriangular" | custom-call | tf_op jit(solution)/shard_map/triangular_solve/custom-call.0 | solution.py:87
  354.9 1.5 collective-permute-start.24
  357.4 1.1 broadcast_select_fusion.8
  361.9 11.7 %cholesky.240 = f32[128,128]{1,0:T(8,128)S(1)} custom-call(f32[128,128]{1,0:T(8,128)S(1)} %cholesky.276), custom_call_target="Cholesky" | custom-call | tf_op jit(solution)/shard_map/jit(cholesky)/cholesky | solution.py:85
  373.6 9.8 %custom-call.19 = f32[1,128,128]{1,2,0:T(8,128)S(1)} custom-call(f32[1,128,128]{2,1,0:T(8,128)S(1)} %get-tuple-element.88), custom_call_target="InvertDiagBlocksLowerTriangular" | custom-call | tf_op jit(solution)/shard_map/jit(cholesky)/cholesky | solution.py:85
  383.9 11.9 %cholesky.257 = f32[128,128]{1,0:T(8,128)S(1)} custom-call(f32[128,128]{1,0:T(8,128)S(1)} %convolution_subtract_fusion.7), custom_call_target="Cholesky" | custom-call | tf_op jit(solution)/shard_map/jit(cholesky)/cholesky | solution.py:85
  398.5 4.1 while.8
  399.2 1.4 bitcast_dynamic-update-slice_fusion.8
  401.3 1.4 bitcast_dynamic-update-slice_fusion.8
  402.7 19.7 %custom-call.20 = f32[2,128,128]{1,2,0:T(8,128)S(1)} custom-call(f32[2,128,128]{2,1,0:T(8,128)S(1)} %get-tuple-element.26), custom_call_target="InvertDiagBlocksLowerTriangular" | custom-call | tf_op jit(solution)/shard_map/triangular_solve/custom-call.0 | solution.py:87
  422.7 0.9 convolution_subtract_fusion.4
  424.5 10.1 %reshape.107 = f32[256,8192]{1,0:T(8,128)} reshape(f32[64,4,8192]{2,1,0:T(4,128)} %all-to-all-done.1) | data formatting | bytes 16777216 | tf_op jit(solution)/shard_map/reshape | solution.py:142
  434.6 1.0 slice.196
  435.8 5.5 %collective-permute-start.25 = (f32[256,384]{0,1:T(8,128)S(1)}, f32[256,384]{0,1:T(8,128)}, u32[]{:S(2)}, u32[]{:S(2)}) collective-permute-start(f32[256,384]{0,1:T(8,128)S(1)} %copy.84), channel_id=1, source_target_pairs={{0,1},{1,0},{2,3},{3,2},{4,5},{5,4},{6,7},{7,6},{8,9},{9,8},{10,11... | collective-permute-start | bytes 1179656 | tf_op jit(solution)/shard_map/ppermute | solution.py:144
  441.3 1.2 fusion.54
  442.6 1.3 convolution_select_fusion
  444.0 1.1 copy.72
  445.1 5.2 %collective-permute-done.25 = f32[256,384]{0,1:T(8,128)} collective-permute-done((f32[256,384]{0,1:T(8,128)S(1)}, f32[256,384]{0,1:T(8,128)}, u32[]{:S(2)}, u32[]{:S(2)}) %collective-permute-start.25) | collective-permute-done | bytes 393248 | tf_op jit(solution)/shard_map/ppermute | solution.py:144
  450.4 1.0 broadcast_select_fusion.5
  458.8 18.4 %fusion.97 = f32[256,8192]{1,0:T(8,128)} fusion(f32[256,768]{1,0:T(8,128)S(1)} %fusion.1, f32[8192,768]{0,1:T(8,128)} %all-gather.2.cloned.1.call-done), kind=kOutput, calls=%fused_computation.199 | convolution fusion | flops 9663676416 | bytes 34340864 | tf_op jit(solution)/shard_map/dot_general | solution.py:153
  477.2 14.5 %fusion = f32[256,8192]{1,0:T(8,128)} fusion(f32[256,8192]{1,0:T(8,128)} %fusion.97, f32[256,8192]{1,0:T(8,128)} %reshape.107, pred[8192]{0:T(1024)(128)(4,1)S(1)} %iota_compare_fusion.6, s32[256]{0:T(256)S(1)} %eq.133, pred[256]{0:T(512)(128)(4,1)S(1)} %iota_compare_fusion.7), kind=kOutput, calls=%fused_computation.7 | convolution fusion | flops 6446776320 | bytes 25175296 | tf_op jit(solution)/shard_map/dot_general | solution.py:23
  (167 shorter events, 36.8 us)
Async XLA Ops:
  7.2 451.6 %all-gather.2.cloned.1.call-start = ((), (), s32[]{:S(2)}) async-start(), calls=%async_computation.2 | async-start | bytes 25559040 | tf_op jit(solution)/shard_map/all_gather | solution.py:125
  8.4 12.4 %collective-permute-start = (f32[256,384]{0,1:T(8,128)S(1)}, f32[256,384]{0,1:T(8,128)S(1)}, u32[]{:S(2)}, u32[]{:S(2)}) collective-permute-start(f32[256,384]{0,1:T(8,128)S(1)} %copy.83), channel_id=1, source_target_pairs={{0,1},{1,0},{2,3},{3,2},{4,5},{5,4},{6,7},{7,6},{8,9},{9,8},{10,11... | collective-permute-start | bytes 1179656 | tf_op jit(solution)/shard_map/ppermute | solution.py:114
  25.3 27.7 %copy-start.6 = (s32[64]{0:T(128)}, s32[64]{0:T(128)S(1)}, u32[]{:S(2)}) copy-start(s32[64]{0:T(128)S(1)} %and_select_fusion.slot_ref) | copy-start | bytes 772
  25.4 25.2 %collective-permute-start.9 = (f32[256,512]{0,1:T(8,128)S(1)}, f32[256,512]{0,1:T(8,128)}, u32[]{:S(2)}, u32[]{:S(2)}) collective-permute-start(f32[256,512]{0,1:T(8,128)S(1)} %pad_maximum_fusion.1), channel_id=1, source_target_pairs={{2,14},{3,15}} | collective-permute-start | bytes 1572872 | tf_op jit(solution)/shard_map/ppermute | solution.py:47
  30.6 21.6 %collective-permute-start.10 = (f32[256,512]{0,1:T(8,128)S(1)}, f32[256,512]{0,1:T(8,128)}, u32[]{:S(2)}, u32[]{:S(2)}) collective-permute-start(f32[256,512]{0,1:T(8,128)S(1)} %pad_maximum_fusion.1), channel_id=1, source_target_pairs={{2,10},{3,11}} | collective-permute-start | bytes 1572872 | tf_op jit(solution)/shard_map/ppermute | solution.py:47
  32.7 11.5 %collective-permute-start.1 = (f32[256,256]{0,1:T(8,128)S(1)}, f32[256,256]{0,1:T(8,128)S(1)}, u32[]{:S(2)}, u32[]{:S(2)}) collective-permute-start(f32[256,256]{0,1:T(8,128)S(1)} %pad_maximum_fusion.2), channel_id=1, source_target_pairs={{0,12},{1,13}} | collective-permute-start | bytes 786440 | tf_op jit(solution)/shard_map/ppermute | solution.py:47
  33.4 14.9 %collective-permute-start.2 = (f32[256,256]{0,1:T(8,128)S(1)}, f32[256,256]{0,1:T(8,128)S(1)}, u32[]{:S(2)}, u32[]{:S(2)}) collective-permute-start(f32[256,256]{0,1:T(8,128)S(1)} %pad_maximum_fusion.2), channel_id=1, source_target_pairs={{0,8},{1,9}} | collective-permute-start | bytes 786440 | tf_op jit(solution)/shard_map/ppermute | solution.py:47
  34.0 14.9 %collective-permute-start.3 = (f32[256,256]{0,1:T(8,128)S(1)}, f32[256,256]{0,1:T(8,128)}, u32[]{:S(2)}, u32[]{:S(2)}) collective-permute-start(f32[256,256]{0,1:T(8,128)S(1)} %pad_maximum_fusion.2), channel_id=1, source_target_pairs={{0,4},{1,5}} | collective-permute-start | bytes 786440 | tf_op jit(solution)/shard_map/ppermute | solution.py:47
  36.4 29.4 %all-to-all-start = ((s32[64,1,4]{2,1,0:T(1,128)}), s32[64,1,4]{2,1,0:T(1,128)}, u32[]{:S(2)}, u32[]{:S(2)}) async-start(s32[64,1,4]{2,1,0:T(1,128)} %copy.67), calls=%async_computation | async-start | bytes 65536 | tf_op jit(solution)/shard_map/all_to_all | solution.py:121
  44.1 39.6 %collective-permute-start.11 = (f32[256,512]{0,1:T(8,128)S(1)}, f32[256,512]{0,1:T(8,128)}, u32[]{:S(2)}, u32[]{:S(2)}) collective-permute-start(f32[256,512]{0,1:T(8,128)S(1)} %pad_maximum_fusion.1), channel_id=1, source_target_pairs={{2,6},{3,7}} | collective-permute-start | bytes 1572872 | tf_op jit(solution)/shard_map/ppermute | solution.py:47
  48.2 43.3 %collective-permute-start.17 = (f32[256,768]{0,1:T(8,128)S(1)}, f32[256,768]{0,1:T(8,128)S(1)}, u32[]{:S(2)}, u32[]{:S(2)}) collective-permute-start(f32[256,768]{0,1:T(8,128)S(1)} %constant_dynamic-update-slice_fusion), channel_id=1, source_target_pairs={{4,0},{5,1}} | collective-permute-start | bytes 2359304 | tf_op jit(solution)/shard_map/ppermute | solution.py:47
  49.0 43.9 %collective-permute-start.18 = (f32[256,768]{0,1:T(8,128)S(1)}, f32[256,768]{0,1:T(8,128)}, u32[]{:S(2)}, u32[]{:S(2)}) collective-permute-start(f32[256,768]{0,1:T(8,128)S(1)} %constant_dynamic-update-slice_fusion), channel_id=1, source_target_pairs={{4,12},{5,13}} | collective-permute-start | bytes 2359304 | tf_op jit(solution)/shard_map/ppermute | solution.py:47
  50.6 43.0 %collective-permute-start.19 = (f32[256,768]{0,1:T(8,128)S(1)}, f32[256,768]{0,1:T(8,128)}, u32[]{:S(2)}, u32[]{:S(2)}) collective-permute-start(f32[256,768]{0,1:T(8,128)S(1)} %constant_dynamic-update-slice_fusion), channel_id=1, source_target_pairs={{4,8},{5,9}} | collective-permute-start | bytes 2359304 | tf_op jit(solution)/shard_map/ppermute | solution.py:47
  52.2 32.3 %collective-permute-start.4 = (f32[256,256]{0,1:T(8,128)S(1)}, f32[256,256]{0,1:T(8,128)S(1)}, u32[]{:S(2)}, u32[]{:S(2)}) collective-permute-start(f32[256,256]{0,1:T(8,128)S(1)} %select_select_fusion.8), channel_id=1, source_target_pairs={{0,96},{4,100},{8,104},{12,108},{1,97},{5,101},{9,105},{13,109}} | collective-permute-start | bytes 786440 | tf_op jit(solution)/shard_map/ppermute | solution.py:47
  65.8 358.7 %all-to-all-start.1 = ((f32[64,4,8192]{2,1,0:T(4,128)}), f32[64,4,8192]{2,1,0:T(4,128)}, u32[]{:S(2)}, u32[]{:S(2)}) async-start(f32[64,4,8192]{2,1,0:T(4,128)} %pack_runs.1), calls=%async_computation.1 | async-start | bytes 16777216 | tf_op jit(solution)/shard_map/all_to_all | solution.py:122
  83.8 1.6 collective-permute-start.5
  84.5 5.6 %copy-start.4 = (f32[256,256]{0,1:T(8,128)}, f32[256,256]{0,1:T(8,128)S(1)}, u32[]{:S(2)}) copy-start(f32[256,256]{0,1:T(8,128)S(1)} %collective-permute-done.4) | copy-start | bytes 786436
  84.5 5.6 %collective-permute-start.6 = (f32[256,256]{0,1:T(8,128)S(1)}, f32[256,256]{0,1:T(8,128)S(1)}, u32[]{:S(2)}, u32[]{:S(2)}) collective-permute-start(f32[256,256]{0,1:T(8,128)S(1)} %select_select_fusion.8), channel_id=1, source_target_pairs={{0,32},{4,36},{8,40},{12,44},{1,33},{5,37},{9,41},{13,45}} | collective-permute-start | bytes 786440 | tf_op jit(solution)/shard_map/ppermute | solution.py:47
  85.4 68.1 %collective-permute-start.12 = (f32[256,512]{0,1:T(8,128)S(1)}, f32[256,512]{0,1:T(8,128)S(1)}, u32[]{:S(2)}, u32[]{:S(2)}) collective-permute-start(f32[256,512]{0,1:T(8,128)S(1)} %select_select_fusion.3), channel_id=1, source_target_pairs={{2,98},{6,102},{10,106},{14,110},{3,99},{7,103},{11,107},{15,111}} | collective-permute-start | bytes 1572872 | tf_op jit(solution)/shard_map/ppermute | solution.py:47
  90.1 113.1 %collective-permute-start.13 = (f32[256,512]{0,1:T(8,128)S(1)}, f32[256,512]{0,1:T(8,128)S(1)}, u32[]{:S(2)}, u32[]{:S(2)}) collective-permute-start(f32[256,512]{0,1:T(8,128)S(1)} %select_select_fusion.3), channel_id=1, source_target_pairs={{2,66},{6,70},{10,74},{14,78},{3,67},{7,71},{11,75},{15,79}} | collective-permute-start | bytes 1572872 | tf_op jit(solution)/shard_map/ppermute | solution.py:47
  91.6 2.0 copy-start.2
  91.6 131.1 %collective-permute-start.14 = (f32[256,512]{0,1:T(8,128)S(1)}, f32[256,512]{0,1:T(8,128)S(1)}, u32[]{:S(2)}, u32[]{:S(2)}) collective-permute-start(f32[256,512]{0,1:T(8,128)S(1)} %select_select_fusion.3), channel_id=1, source_target_pairs={{2,34},{6,38},{10,42},{14,46},{3,35},{7,39},{11,43},{15,47}} | collective-permute-start | bytes 1572872 | tf_op jit(solution)/shard_map/ppermute | solution.py:47
  92.9 3.6 collective-permute-start.7
  95.0 194.4 %collective-permute-start.20 = (f32[256,768]{0,1:T(8,128)S(1)}, f32[256,768]{0,1:T(8,128)}, u32[]{:S(2)}, u32[]{:S(2)}) collective-permute-start(f32[256,768]{0,1:T(8,128)S(1)} %select_select_fusion.1), channel_id=1, source_target_pairs={{4,100},{8,104},{12,108},{0,96},{5,101},{9,105},{13,109},{1,97}} | collective-permute-start | bytes 2359304 | tf_op jit(solution)/shard_map/ppermute | solution.py:47
  96.5 192.9 %collective-permute-start.21 = (f32[256,768]{0,1:T(8,128)S(1)}, f32[256,768]{0,1:T(8,128)}, u32[]{:S(2)}, u32[]{:S(2)}) collective-permute-start(f32[256,768]{0,1:T(8,128)S(1)} %select_select_fusion.1), channel_id=1, source_target_pairs={{4,68},{8,72},{12,76},{0,64},{5,69},{9,73},{13,77},{1,65}} | collective-permute-start | bytes 2359304 | tf_op jit(solution)/shard_map/ppermute | solution.py:47
  153.5 135.9 %collective-permute-start.22 = (f32[256,768]{0,1:T(8,128)S(1)}, f32[256,768]{0,1:T(8,128)}, u32[]{:S(2)}, u32[]{:S(2)}) collective-permute-start(f32[256,768]{0,1:T(8,128)S(1)} %select_select_fusion.1), channel_id=1, source_target_pairs={{4,36},{8,40},{12,44},{0,32},{5,37},{9,41},{13,45},{1,33}} | collective-permute-start | bytes 2359304 | tf_op jit(solution)/shard_map/ppermute | solution.py:47
  203.2 21.9 %collective-permute-start.8 = (f32[256,256]{0,1:T(8,128)S(1)}, f32[256,256]{0,1:T(8,128)S(1)}, u32[]{:S(2)}, u32[]{:S(2)}) collective-permute-start(f32[256,256]{0,1:T(8,128)S(1)} %broadcast_select_fusion.10), channel_id=1, source_target_pairs={{0,2},{16,18},{32,34},{48,50},{64,66},{80,82},{96,98},{112,114},{4... | collective-permute-start | bytes 786440 | tf_op jit(solution)/shard_map/ppermute | solution.py:47
  222.8 63.8 %collective-permute-start.15 = (f32[256,512]{0,1:T(8,128)S(1)}, f32[256,512]{0,1:T(8,128)}, u32[]{:S(2)}, u32[]{:S(2)}) collective-permute-start(f32[256,512]{0,1:T(8,128)S(1)} %select_select_fusion.2), channel_id=1, source_target_pairs={{2,18},{34,50},{66,82},{98,114},{6,22},{38,54},{70,86},{102,118},{... | collective-permute-start | bytes 1572872 | tf_op jit(solution)/shard_map/ppermute | solution.py:47
  265.8 0.5 copy-start.7
  286.6 5.0 %collective-permute-start.16 = (f32[256,512]{0,1:T(8,128)S(1)}, f32[256,512]{0,1:T(8,128)S(1)}, u32[]{:S(2)}, u32[]{:S(2)}) collective-permute-start(f32[256,512]{0,1:T(8,128)S(1)} %broadcast_select_fusion.2), channel_id=1, source_target_pairs={{2,0},{18,16},{34,32},{50,48},{66,64},{82,80},{98,96},{114,112},{6... | collective-permute-start | bytes 1572872 | tf_op jit(solution)/shard_map/ppermute | solution.py:47
  289.6 65.1 %collective-permute-start.23 = (f32[256,768]{0,1:T(8,128)S(1)}, f32[256,768]{0,1:T(8,128)}, u32[]{:S(2)}, u32[]{:S(2)}) collective-permute-start(f32[256,768]{0,1:T(8,128)S(1)} %select_select_fusion), channel_id=1, source_target_pairs={{4,20},{36,52},{68,84},{100,116},{8,24},{40,56},{72,88},{104,120},... | collective-permute-start | bytes 2359304 | tf_op jit(solution)/shard_map/ppermute | solution.py:47
  354.9 4.2 collective-permute-start.24
  358.5 40.0 %copy-start.8 = (s32[2,2]{1,0:T(2,128)S(1)}, s32[2,2]{1,0:T(2,128)}, u32[]{:S(2)}) copy-start(s32[2,2]{1,0:T(2,128)} %get-tuple-element.294) | copy-start | bytes 52
  422.4 1.6 copy-start.5
  424.4 18.1 %copy-start.3 = (f32[256,128]{0,1:T(8,128)S(1)}, f32[256,128]{0,1:T(8,128)}, u32[]{:S(2)}) copy-start(f32[256,128]{0,1:T(8,128)} %get-tuple-element.77) | copy-start | bytes 393220
  424.4 19.5 %copy-start = (f32[256,256]{0,1:T(8,128)S(1)}, f32[256,256]{0,1:T(8,128)}, u32[]{:S(2)}) copy-start(f32[256,256]{0,1:T(8,128)} %get-tuple-element.103) | copy-start | bytes 786436
  424.4 19.5 %copy-start.1 = (f32[256,256]{0,1:T(8,128)S(1)}, f32[256,256]{0,1:T(8,128)}, u32[]{:S(2)}) copy-start(f32[256,256]{0,1:T(8,128)} %get-tuple-element.105) | copy-start | bytes 786436
  435.8 14.6 %collective-permute-start.25 = (f32[256,384]{0,1:T(8,128)S(1)}, f32[256,384]{0,1:T(8,128)}, u32[]{:S(2)}, u32[]{:S(2)}) collective-permute-start(f32[256,384]{0,1:T(8,128)S(1)} %copy.84), channel_id=1, source_target_pairs={{0,1},{1,0},{2,3},{3,2},{4,5},{5,4},{6,7},{7,6},{8,9},{9,8},{10,11... | collective-permute-start | bytes 1179656 | tf_op jit(solution)/shard_map/ppermute | solution.py:144
Sparse Core Ops, SparseCore 0:
  23.2 308.6 all-gather.1

commit v2 on v1

v2 whole, which is shorter than its diff:
```python
import functools

import jax
import jax.numpy as jnp
from jax import lax
from jax.experimental import pallas as pl
from jax.experimental.pallas import tpu as pltpu
from jax.sharding import PartitionSpec as P

NP = 3
N_ROW = 64
CAP = 4
PW = 256
BW = 128
PANEL = NP * PW
HEAD = NP * BW
GRID = (4, 2, 4, 2)
PIECE_BLOCKS = (8, 8, 8, 4, 4)
PIECE_START = (0, 8, 16, 24, 28)

full = lax.Precision.HIGHEST


def dot_t(a, b):
    return lax.dot_general(
        a, b, (((1,), (1,)), ((), ())), precision=full, preferred_element_type=jnp.float32
    )


def dot_n(a, b):
    return lax.dot_general(
        a, b, (((1,), (0,)), ((), ())), precision=full, preferred_element_type=jnp.float32
    )


def row_id(z, y, x, k):
    return ((z * 2 + y) * 4 + x) * 2 + k


def pairs_of(kind, step):
    pairs = []
    for z in range(4):
        for y in range(2):
            for x in range(4):
                for k in range(2):
                    if kind == "y":
                        to = (z, 1 - y, x, k)
                    elif kind == "core":
                        to = (z, y, x, 1 - k)
                    elif (kind == "first") == (k == 0):
                        to = (z, y, (x + step) % 4, k)
                    else:
                        to = ((z + step) % 4, y, x, k)
                    pairs.append((row_id(z, y, x, k), row_id(*to)))
    return pairs


def move(value, kind, step=0):
    return lax.ppermute(value, "row", pairs_of(kind, step))


def ring(value, kind, beside=None):
    half = value.shape[0] // 2
    before = move(value, kind, 1)
    after = move(value, kind, -1)
    if beside is not None:
        before, after, beside = lax.optimization_barrier((before, after, beside))
    far_first = move(before[:half], kind, 1)
    far_second = move(after[half:], kind, -1)
    return [value, before, after, far_first, far_second], beside


def gather_rows(mine, beside):
    value = jnp.concatenate([mine, move(mine, "y")], axis=0)
    value = jnp.concatenate(ring(value, "first")[0], axis=0)
    pieces, beside = ring(value, "second", beside)
    return pieces + [move(p, "core") for p in pieces], beside


def block_order(row):
    z, y, x, k = row // 16, (row // 8) % 2, (row // 2) % 4, row % 2
    first = ((0, 0), (0, 1), (-1, 0), (-1, 1), (1, 0), (1, 1), (2, 0), (2, 1))
    order = []
    for swapped in (0, 1):
        core = k ^ swapped
        for second, part in ((0, first), (-1, first), (1, first), (2, first[:4]), (2, first[4:])):
            for along, flip in part:
                xs = jnp.where(core == 0, x + along, x + second) % 4
                zs = jnp.where(core == 0, z + second, z + along) % 4
                order.append(row_id(zs, y ^ flip, xs, core))
    return jnp.stack(order).astype(jnp.int32)


def pack_kernel(slot_ref, rows_ref, out_ref):
    for g in range(N_ROW):
        out_ref[slot_ref[g]] = rows_ref[g * CAP : (g + 1) * CAP, :]


def pack_runs(slots, rows, tile):
    height, width = rows.shape
    return pl.pallas_call(
        pack_kernel,
        out_shape=jax.ShapeDtypeStruct((N_ROW, CAP, width), rows.dtype),
        grid_spec=pltpu.PrefetchScalarGridSpec(
            num_scalar_prefetch=1,
            grid=(width // tile,),
            in_specs=[pl.BlockSpec((height, tile), lambda i, s: (0, i))],
            out_specs=pl.BlockSpec((N_ROW, CAP, tile), lambda i, s: (0, 0, i)),
        ),
        cost_estimate=pl.CostEstimate(
            flops=0, bytes_accessed=2 * 4 * height * width, transcendentals=0
        ),
        name="pack_runs",
    )(slots, rows)


def head_kernel(place_ref, col_ref, *refs):
    pieces, (rows_ref, square_ref), (sem,) = refs[:10], refs[10:12], refs[12:]
    for q in range(NP):
        at = place_ref[q]
        for p in range(10):
            low = 32 * (p // 5) + PIECE_START[p % 5]
            high = low + PIECE_BLOCKS[p % 5]

            @pl.when((at >= low) & (at < high))
            def _():
                start = pl.multiple_of((at - low) * BW, BW)
                copy = pltpu.make_async_copy(
                    pieces[p].at[pl.ds(start, BW)], rows_ref.at[pl.ds(q * BW, BW)], sem
                )
                copy.start()
                copy.wait()

    for c in range(2):

        @pl.when(col_ref[0] == c)
        def _():
            for q in range(NP):
                square_ref[:, q * BW : (q + 1) * BW] = rows_ref[
                    :, (2 * q + c) * BW : (2 * q + c + 1) * BW
                ]


def head_rows(place, col, pieces):
    return pl.pallas_call(
        head_kernel,
        out_shape=(
            jax.ShapeDtypeStruct((HEAD, PANEL), jnp.float32),
            jax.ShapeDtypeStruct((HEAD, HEAD), jnp.float32),
        ),
        in_specs=[pl.BlockSpec(memory_space=pltpu.SMEM)] * 2
        + [pl.BlockSpec(memory_space=pl.ANY)] * 10,
        out_specs=(pl.BlockSpec(memory_space=pltpu.VMEM),) * 2,
        scratch_shapes=[pltpu.SemaphoreType.DMA],
        cost_estimate=pl.CostEstimate(flops=0, bytes_accessed=4 * 10**6, transcendentals=0),
        name="head_rows",
    )(place, col, *pieces)


def inverse_lower(block, m):
    n = BW
    lane = lax.broadcasted_iota(jnp.int32, (8, n), 1)
    sub = lax.broadcasted_iota(jnp.int32, (8, n), 0)
    tiles = [block[8 * t : 8 * t + 8, :] for t in range(n // 8)]
    pivots = [None] * (n // 8)
    for k0 in range(0, n, m):
        tk, s0 = k0 // 8, k0 % 8
        group = (lane >= k0) & (lane < k0 + m)
        cols = [
            {
                t: jnp.broadcast_to(tiles[t][:, k0 + j : k0 + j + 1], (8, n))
                for t in range(tk, n // 8)
            }
            for j in range(m)
        ]
        rows, factors = [], []
        for j in range(m):
            unit = jnp.where(lane[:1] == k0 + j, 1.0, 0.0)
            r = jnp.where(group[:1], unit, tiles[tk][s0 + j : s0 + j + 1, :])
            for i in range(j):
                r = r - factors[i][tk][s0 + j : s0 + j + 1, :] * rows[i]
            rows.append(r)
            pivot = jnp.broadcast_to(cols[j][tk][s0 + j : s0 + j + 1, :], (8, n))
            kept = pivots[tk]
            pivots[tk] = pivot if kept is None else jnp.where(sub == s0 + j, pivot, kept)
            inverse = 1.0 / pivot
            f = {t: cols[j][t] * inverse for t in cols[j]}
            f[tk] = jnp.where(sub > s0 + j, f[tk], 0.0)
            factors.append(f)
            for l in range(j + 1, m):
                a = jnp.broadcast_to(cols[l][tk][s0 + j : s0 + j + 1, :], (8, n))
                for t in cols[l]:
                    cols[l][t] = cols[l][t] - f[t] * a
        rows = [jnp.broadcast_to(r, (8, n)) for r in rows]
        for t in range(tk, n // 8):
            if t == tk:
                unit = jnp.where(lane - k0 == sub - s0, 1.0, 0.0)
                v = jnp.where(group & (sub >= s0), unit, tiles[t])
            else:
                v = jnp.where(group, 0.0, tiles[t])
            for j in range(m):
                v = v - factors[j][t] * rows[j]
            tiles[t] = v
    out = [
        jnp.where(lane <= sub + 8 * t, tiles[t] * lax.rsqrt(pivots[t]), 0.0)
        for t in range(n // 8)
    ]
    return jnp.concatenate(out, axis=0)


def factor_kernel(col_ref, rows_ref, square_ref, w_ref):
    def span(i):
        return slice(i * BW, (i + 1) * BW)

    for c in range(2):

        @pl.when(col_ref[0] == c)
        def _():
            d = 1 - c
            for q in range(NP):
                for p in range(NP):
                    w_ref[span(2 * q + c), span(2 * p + c)] = rows_ref[span(q), span(2 * p + c)]
                    other = rows_ref[span(q), span(2 * p + d)]
                    w_ref[span(2 * q + c), span(2 * p + d)] = other
                    w_ref[span(2 * p + d), span(2 * q + c)] = other.T
                    w_ref[span(2 * q + d), span(2 * p + d)] = square_ref[span(q), span(p)]

    n = PANEL
    row_ids = lax.broadcasted_iota(jnp.int32, (n, BW), 0)
    eye = jnp.where(
        lax.broadcasted_iota(jnp.int32, (BW, BW), 0)
        == lax.broadcasted_iota(jnp.int32, (BW, BW), 1),
        1.0,
        0.0,
    )

    @pl.loop(0, n // BW)
    def _(b):
        at = pl.ds(pl.multiple_of(b * BW, BW), BW)
        inverse = inverse_lower(w_ref[at, at], 8)
        below = row_ids >= (b + 1) * BW
        column = jnp.where(below, w_ref[:, at], 0.0)
        lower = dot_t(column, inverse)
        w_ref[at, at] = eye
        r = dot_n(inverse, w_ref[at, :])
        w_ref[:, at] = jnp.where(below, 0.0, w_ref[:, at])
        w_ref[...] = w_ref[...] - dot_n(lower, r)
        w_ref[at, :] = r

    rows_of = lax.broadcasted_iota(jnp.int32, (n, n), 0)
    cols_of = lax.broadcasted_iota(jnp.int32, (n, n), 1)
    w_ref[...] = jnp.where(cols_of <= rows_of, w_ref[...], 0.0)


def inverse_factor(col, rows, square):
    return pl.pallas_call(
        factor_kernel,
        out_shape=jax.ShapeDtypeStruct((PANEL, PANEL), jnp.float32),
        in_specs=[pl.BlockSpec(memory_space=pltpu.SMEM)]
        + [pl.BlockSpec(memory_space=pltpu.VMEM)] * 2,
        out_specs=pl.BlockSpec(memory_space=pltpu.VMEM),
        compiler_params=pltpu.CompilerParams(vmem_limit_bytes=40 * 2**20),
        cost_estimate=pl.CostEstimate(
            flops=4 * 10**9, bytes_accessed=5 * 10**6, transcendentals=0
        ),
        name="inverse_factor",
    )(col, rows, square)


def update_kernel(order_ref, x_ref, *refs):
    pieces, out_ref = refs[:10], refs[10]
    high, low, held, made, in_sem, out_sem = refs[11:]
    steps = N_ROW // 2
    slots = held.shape[0]

    def fetch(step):
        for p in range(10):
            first = 16 * (p // 5) + PIECE_START[p % 5] // 2
            last = first + PIECE_BLOCKS[p % 5] // 2

            @pl.when((step >= first) & (step < last))
            def _():
                start = pl.multiple_of((step - first) * 2 * BW, 2 * BW)
                slot = lax.rem(step, slots)
                pltpu.make_async_copy(
                    pieces[p].at[pl.ds(start, 2 * BW)], held.at[slot], in_sem.at[slot]
                ).start()

    def store(step, half):
        slot = lax.rem(step, 2)
        to = pl.multiple_of(order_ref[2 * step + half] * BW, BW)
        return pltpu.make_async_copy(
            made.at[slot, half], out_ref.at[:, pl.ds(to, BW)], out_sem.at[slot, half]
        )

    for step in range(slots - 1):
        fetch(jnp.int32(step))
    x = x_ref[...]
    high[...] = x.astype(jnp.bfloat16)
    low[...] = (x - high[...].astype(jnp.float32)).astype(jnp.bfloat16)

    def times(a, b):
        return lax.dot_general(
            a, b, (((1,), (1,)), ((), ())), preferred_element_type=jnp.float32
        )

    @pl.loop(0, steps)
    def _(step):
        @pl.when(step + slots - 1 < steps)
        def _():
            fetch(step + slots - 1)

        slot = lax.rem(step, slots)
        pltpu.make_async_copy(
            pieces[0].at[pl.ds(0, 2 * BW)], held.at[slot], in_sem.at[slot]
        ).wait()
        rows = held[slot]
        rows_high = rows.astype(jnp.bfloat16)
        rows_low = (rows - rows_high.astype(jnp.float32)).astype(jnp.bfloat16)
        result = (
            times(high[...], rows_low) + times(low[...], rows_high)
        ) + times(high[...], rows_high)

        @pl.when(step >= 2)
        def _():
            for half in range(2):
                store(step - 2, half).wait()

        for half in range(2):
            made[lax.rem(step, 2), half] = result[:, half * BW : (half + 1) * BW]
            store(step, half).start()

    for step in range(steps - 2, steps):
        for half in range(2):
            store(jnp.int32(step), half).wait()


def update_of(order, x, pieces, width):
    return pl.pallas_call(
        update_kernel,
        out_shape=jax.ShapeDtypeStruct((PW, width), jnp.float32),
        in_specs=[pl.BlockSpec(memory_space=pltpu.SMEM), pl.BlockSpec(memory_space=pltpu.VMEM)]
        + [pl.BlockSpec(memory_space=pl.ANY)] * 10,
        out_specs=pl.BlockSpec(memory_space=pl.ANY),
        scratch_shapes=[
            pltpu.VMEM((PW, PANEL), jnp.bfloat16),
            pltpu.VMEM((PW, PANEL), jnp.bfloat16),
            pltpu.VMEM((4, 2 * BW, PANEL), jnp.float32),
            pltpu.VMEM((2, 2, PW, BW), jnp.float32),
            pltpu.SemaphoreType.DMA((4,)),
            pltpu.SemaphoreType.DMA((2, 2)),
        ],
        compiler_params=pltpu.CompilerParams(vmem_limit_bytes=40 * 2**20),
        cost_estimate=pl.CostEstimate(
            flops=6 * PW * width * PANEL, bytes_accessed=34 * 10**6, transcendentals=0
        ),
        name="update_of",
    )(order, x, *pieces)


def place_kernel(tile, place_ref, arrived_ref, update_ref, out_ref, rows):
    for b in range(N_ROW):
        rows[b * CAP : (b + 1) * CAP, :] = arrived_ref[b]
    place = place_ref[...]
    value = rows[...]
    total = None
    for part in range(3):
        piece = value.astype(jnp.bfloat16)
        term = jnp.dot(place, piece, preferred_element_type=jnp.float32)
        total = term if total is None else total + term
        if part < 2:
            value = value - piece.astype(jnp.float32)
    column = pl.program_id(0) * tile + lax.broadcasted_iota(jnp.int32, (1, tile), 1)
    out_ref[...] = jnp.where(column >= HEAD, total - update_ref[...], 0.0)


def place_rows(place, arrived, update, tile=512):
    width = arrived.shape[2]
    return pl.pallas_call(
        functools.partial(place_kernel, tile),
        out_shape=jax.ShapeDtypeStruct((PW, width), jnp.float32),
        grid=(width // tile,),
        in_specs=[
            pl.BlockSpec((PW, PW), lambda i: (0, 0)),
            pl.BlockSpec((N_ROW, CAP, tile), lambda i: (0, 0, i)),
            pl.BlockSpec((PW, tile), lambda i: (0, i)),
        ],
        out_specs=pl.BlockSpec((PW, tile), lambda i: (0, i)),
        scratch_shapes=[pltpu.VMEM((PW, tile), jnp.float32)],
        cost_estimate=pl.CostEstimate(
            flops=6 * PW * PW * width, bytes_accessed=12 * PW * width, transcendentals=0
        ),
        name="place_rows",
    )(place, arrived, update)


def weave(own, other, col):
    first = jnp.where(col == 0, own, other)
    second = jnp.where(col == 0, other, own)
    parts = []
    for k in range(NP):
        parts += [first[:, k * BW : (k + 1) * BW], second[:, k * BW : (k + 1) * BW]]
    return jnp.concatenate(parts, axis=1)


def local(front_matrix, row_map):
    width = front_matrix.shape[1]
    row = lax.axis_index("row")
    col = lax.axis_index("col")
    swap = [(0, 1), (1, 0)]
    own = front_matrix[:, :HEAD]
    panel = weave(own, lax.ppermute(own, "col", swap), col)

    targets = row_map[0].reshape(N_ROW, CAP)[:, 0] // PW
    within = (row_map[0] % PW).astype(jnp.float32)
    small = jnp.concatenate([panel, jnp.broadcast_to(within[:, None], (PW, BW))], axis=1)
    small = pack_runs(targets, small, small.shape[1])
    small = lax.all_to_all(small, "row", split_axis=0, concat_axis=0, tiled=True)
    outgoing = pack_runs(targets, front_matrix, 512)

    mine = lax.dynamic_slice_in_dim(panel, col * BW, BW, 0)
    pieces, small = gather_rows(mine, small)
    order = block_order(row)
    places = jnp.sum(
        jnp.where(
            order[None, :] == jnp.arange(NP, dtype=jnp.int32)[:, None],
            jnp.arange(N_ROW, dtype=jnp.int32)[None, :],
            0,
        ),
        axis=1,
    )
    cols = col.reshape(1).astype(jnp.int32)
    rows, square = head_rows(places, cols, pieces)
    other_square = lax.ppermute(square, "col", swap)
    outgoing, other_square = lax.optimization_barrier((outgoing, other_square))
    arrived = lax.all_to_all(outgoing, "row", split_axis=0, concat_axis=0, tiled=True)

    w = inverse_factor(cols, rows, other_square)
    small = small.reshape(PW, PANEL + BW)
    both = dot_t(jnp.concatenate([panel, small[:, :PANEL]], axis=0), w)
    panel_ids = lax.broadcasted_iota(jnp.int32, (1, PANEL), 1) // PW
    factors = jnp.where(row >= panel_ids, both[:PW], 0.0)

    slots = jnp.arange(PW, dtype=jnp.int32)
    goes = small[:, PANEL].astype(jnp.int32)
    place = (goes[None, :] == slots[:, None]) & (slots[None, :] >= NP * CAP)
    place = place.astype(jnp.float32)
    x = dot_n(dot_n(place, both[PW:]), w)
    update = update_of(order, x, pieces, width)
    parent = place_rows(place.astype(jnp.bfloat16), arrived, update)
    return factors, parent


def solution(mesh):
    placed = (P("row", "col"), P("row", None))
    return jax.shard_map(
        local,
        mesh=mesh,
        in_specs=placed,
        out_specs=(P("row", None), P("row", "col")),
        check_vma=False,
    )
```

time: 507 us -> 287 us (0.57)
  other arithmetic: 170 us -> 4.62 us
  Pallas kernels: 12.8 us -> 100 us
  matrix products: 53.9 us -> 6.73 us
  starting transfers between devices: 74 us -> 45.7 us
  waiting for transfers between devices: 136 us -> 109 us
  between operations: 19.5 us -> 0.86 us
  local copies, waits for them, and re-layouts: 32.5 us -> 16.1 us
    another operation x27 -> x0, other arithmetic: 163 us -> none  [the longest x20 103 us: inverse_factor(): lower = jnp.linalg.cholesky(block)]
    ppermute x25 -> x15, waiting for transfers between devices: 128 us -> 38.7 us  [the longest x14 38 us: move(): return lax.ppermute(value, 'row', pairs_of(kind, step))]
    pallas_call x0 -> x4, Pallas kernels: none -> 84.8 us  [the longest x1 41.9 us: inverse_factor(): pl.pallas_call(factor_kernel, out_shape=jax.ShapeDtypeStruct((PANEL, PANE...]
    all_to_all x1, waiting for transfers between devices: 0.01 us -> 32.6 us  [local(): lax.all_to_all(small, 'row', split_axis=0, concat_axis=0, tiled=True)]
    all_to_all x1, waiting for transfers between devices: 0.01 us -> 29 us  [local(): lax.all_to_all(outgoing, 'row', split_axis=0, concat_axis=0, tiled=True)]
    ppermute x25 -> x15, starting transfers between devices: 46.6 us -> 21.6 us  [the longest x14 18.6 us: move(): return lax.ppermute(value, 'row', pairs_of(kind, step))]
    dot_general x1 -> x0, matrix products: 18.4 us -> none  [local(): lax.dot_general(dot_n(place, x), gathered, (((1,), (1,)), ((), ())), prec...]
    dot_general x8 -> x2, matrix products: 18.7 us -> 2.74 us  [dot_n(): lax.dot_general(a, b, (((1,), (0,)), ((), ())), precision=full, preferred...]
  transfers between devices with their start and end apart: 29 -> 18, of which waited for: 6 -> 10; matrix products, arithmetic and copies ran while one was open for 44% -> 7% of each run, Pallas kernels for 3% -> 28%
where the time goes in v2:
time: 287 us; the launch traced here: 283 us
  waiting for transfers between devices  109 us (38%)
  Pallas kernels  100 us (35%)
  starting transfers between devices  45.7 us (16%)
  local copies, waits for them, and re-layouts  16.1 us (6%)
  matrix products  6.73 us (2%)
  other arithmetic  4.62 us (2%)
    pallas_call x1, Pallas kernels, inverse_factor(): pl.pallas_call(factor_kernel, out_shape=jax.ShapeDtypeStruct((PANEL, PANE...  41.9 us
    ppermute x14, waiting for transfers between devices, move(): return lax.ppermute(value, 'row', pairs_of(kind, step))  38 us
    all_to_all x1, waiting for transfers between devices, local(): lax.all_to_all(small, 'row', split_axis=0, concat_axis=0, tiled=True)  32.6 us
    all_to_all x1, waiting for transfers between devices, local(): lax.all_to_all(outgoing, 'row', split_axis=0, concat_axis=0, tiled=True)  29 us
    pallas_call x1, Pallas kernels, update_of(): pl.pallas_call(update_kernel, out_shape=jax.ShapeDtypeStruct((PW, width),...  20.9 us
    ppermute x14, starting transfers between devices, move(): return lax.ppermute(value, 'row', pairs_of(kind, step))  18.6 us
    pallas_call x1, Pallas kernels, place_rows(): pl.pallas_call(functools.partial(place_kernel, tile), out_shape=jax.Shape...  17 us
    pallas_call x2, Pallas kernels, pack_runs(): pl.pallas_call(pack_kernel, out_shape=jax.ShapeDtypeStruct((N_ROW, CAP, w...  15.5 us
  transfers between devices with their start and end apart: 18, of which 10 were waited for; matrix products, arithmetic and copies ran while one was open for 7% of the time, Pallas kernels for 28%

profile of v2, /device:TPU:1, one launch (start us, length us, event | category | flops | bytes accessed | tf_op | source)
XLA Modules:
  0.0 283.2 jit_solution(3520314782909631468)
XLA Ops:
  0.6 1.0 slice.48
  1.7 3.8 %collective-permute-start = (f32[256,384]{1,0:T(8,128)S(1)}, f32[256,384]{1,0:T(8,128)S(1)}, u32[]{:S(2)}, u32[]{:S(2)}) collective-permute-start(f32[256,384]{1,0:T(8,128)S(1)} %slice.48), channel_id=1, source_target_pairs={{0,1},{1,0},{2,3},{3,2},{4,5},{5,4},{6,7},{7,6},{8,9},{9,8},{10,11... | collective-permute-start | bytes 1179656 | tf_op jit(solution)/shard_map/ppermute | solution.py:412
  5.5 8.6 %collective-permute-done = f32[256,384]{1,0:T(8,128)S(1)} collective-permute-done((f32[256,384]{1,0:T(8,128)S(1)}, f32[256,384]{1,0:T(8,128)S(1)}, u32[]{:S(2)}, u32[]{:S(2)}) %collective-permute-start) | collective-permute-done | bytes 393248 | tf_op jit(solution)/shard_map/ppermute | solution.py:412
  14.0 1.0 broadcast_select_fusion
  15.1 0.7 slice_dynamic-update-slice_fusion.10
  15.8 0.7 slice_dynamic-update-slice_fusion.8
  16.4 0.7 slice_dynamic-update-slice_fusion.6
  17.1 0.7 slice_dynamic-update-slice_fusion.4
  17.8 0.7 slice_dynamic-update-slice_fusion.2
  18.5 0.7 slice_dynamic-update-slice_fusion
  19.1 0.9 constant_dynamic-update-slice_fusion.5
  20.0 1.3 collective-permute-start.1
  21.3 7.8 %collective-permute-done.1 = f32[128,768]{1,0:T(8,128)S(1)} collective-permute-done((f32[128,768]{1,0:T(8,128)S(1)}, f32[128,768]{1,0:T(8,128)S(1)}, u32[]{:S(2)}, u32[]{:S(2)}) %collective-permute-start.1) | collective-permute-done | bytes 393248 | tf_op jit(solution)/shard_map/ppermute | solution.py:59
  29.2 1.7 collective-permute-start.2
  30.9 2.2 collective-permute-start.3
  33.1 9.6 %collective-permute-done.2 = f32[256,768]{1,0:T(8,128)S(1)} collective-permute-done((f32[256,768]{1,0:T(8,128)S(1)}, f32[256,768]{1,0:T(8,128)S(1)}, u32[]{:S(2)}, u32[]{:S(2)}) %collective-permute-start.2) | collective-permute-done | bytes 786464 | tf_op jit(solution)/shard_map/ppermute | solution.py:59
  42.7 0.1 collective-permute-start.4
  42.8 2.7 collective-permute-start.5
  45.5 0.8 constant_dynamic-update-slice_fusion.4
  46.3 0.9 constant_dynamic-update-slice_fusion.3
  47.3 0.9 constant_dynamic-update-slice_fusion.2
  48.2 2.7 collective-permute-done.4
  50.9 0.8 constant_dynamic-update-slice_fusion.1
  51.7 0.8 constant_dynamic-update-slice_fusion.refs_0_
  52.5 0.6 collective-permute-start.6
  53.1 2.1 collective-permute-start.7
  55.2 0.5 broadcast.158
  55.7 0.6 reduce.7
  56.2 0.1 reshape_squeeze.3
  56.4 0.1 slice_reduce_fusion
  56.5 0.5 and_select_fusion.1.slot_ref
  57.0 0.8 broadcast_dynamic-update-slice_fusion.rows_ref
  57.8 2.8 %pack_runs.2 = f32[64,4,896]{2,1,0:T(4,128)} custom-call(s32[64]{0:T(128)} %and_select_fusion.1.slot_ref, f32[256,896]{1,0:T(8,128)} %broadcast_dynamic-update-slice_fusion.rows_ref), custom_call_target="tpu_custom_call" | custom-call | bytes 1835008 | tf_op jit(solution)/shard_map/pack_runs/pallas_call | solution.py:101
  60.6 11.5 %all-to-all-start = ((f32[64,4,896]{2,1,0:T(4,128)}), f32[64,4,896]{2,1,0:T(4,128)}, u32[]{:S(2)}, u32[]{:S(2)}) async-start(f32[64,4,896]{2,1,0:T(4,128)} %pack_runs.2), calls=%async_computation | async-start | bytes 1835008 | tf_op jit(solution)/shard_map/all_to_all | solution.py:418
  72.1 0.6 collective-permute-start.10
  72.7 32.6 %all-to-all-done = f32[64,4,896]{2,1,0:T(4,128)} async-done(((f32[64,4,896]{2,1,0:T(4,128)}), f32[64,4,896]{2,1,0:T(4,128)}, u32[]{:S(2)}, u32[]{:S(2)}) %all-to-all-start) | async-done | bytes 917536 | tf_op jit(solution)/shard_map/all_to_all | solution.py:418
  105.3 0.1 slice.59
  105.4 0.1 collective-permute-start.8
  105.5 2.4 slice.60
  108.0 2.3 collective-permute-start.9
  110.3 1.2 collective-permute-start.11
  111.5 14.9 %collective-permute-done.8.refs_3_ = f32[512,768]{1,0:T(8,128)} collective-permute-done((f32[512,768]{1,0:T(8,128)S(1)}, f32[512,768]{1,0:T(8,128)}, u32[]{:S(2)}, u32[]{:S(2)}) %collective-permute-start.8) | collective-permute-done | bytes 1572896 | tf_op jit(solution)/shard_map/ppermute | solution.py:59
  126.4 2.0 collective-permute-start.13
  128.4 1.8 collective-permute-start.14
  130.2 0.1 stack.259.order_ref
  130.3 0.6 select_reduce_fusion.place_ref
  131.0 0.8 collective-permute-done.13.refs_8_
  131.8 2.2 collective-permute-done.14.refs_9_
  134.0 5.0 %head_rows.1 = (f32[384,768]{1,0:T(8,128)}, f32[384,384]{1,0:T(8,128)}) custom-call(s32[3]{0:T(128)} %select_reduce_fusion.place_ref, s32[1]{0:T(128)} %bitcast.1.col_ref, f32[1024,768]{1,0:T(8,128)} %constant_dynamic-update-slice_fusion.refs_0_, f32[1024,768]{1,0:T(8,128)} %copy-done, f32[1024,768]{1,0:T(8,128)} %collective-permute-done.7.refs_2_, ...), custom_call_target="tpu_custom_call" | custom-call | bytes 4000000 | tf_op jit(solution)/shard_map/head_rows/pallas_call | solution.py:145
  139.0 3.0 %collective-permute-start.15 = (f32[384,384]{1,0:T(8,128)}, f32[384,384]{1,0:T(8,128)S(1)}, u32[]{:S(2)}, u32[]{:S(2)}) collective-permute-start(f32[384,384]{1,0:T(8,128)} %get-tuple-element.13), channel_id=1, source_target_pairs={{0,1},{1,0},{2,3},{3,2},{4,5},{5,4},{6,7},{7,6},{8,9},{9,8},{10,11... | collective-permute-start | bytes 1769480 | tf_op jit(solution)/shard_map/ppermute | solution.py:434
  142.0 12.7 %pack_runs.3 = f32[64,4,8192]{2,1,0:T(4,128)} custom-call(s32[64]{0:T(128)} %and_select_fusion.1.slot_ref, f32[256,8192]{1,0:T(8,128)} %rows_ref.1), custom_call_target="tpu_custom_call" | custom-call | bytes 16777216 | tf_op jit(solution)/shard_map/pack_runs/pallas_call | solution.py:101
  154.7 0.7 collective-permute-done.15.square_ref
  155.4 8.8 %all-to-all-start.1 = ((f32[64,4,8192]{2,1,0:T(4,128)}), f32[64,4,8192]{2,1,0:T(4,128)}, u32[]{:S(2)}, u32[]{:S(2)}) async-start(f32[64,4,8192]{2,1,0:T(4,128)} %pack_runs.3), calls=%async_computation.1 | async-start | bytes 16777216 | tf_op jit(solution)/shard_map/all_to_all | solution.py:436
  164.2 1.6 reshape.83
  165.8 0.1 fusion.8
  165.9 0.7 convert_convert_fusion.place_ref
  166.7 41.9 %inverse_factor.1 = f32[768,768]{1,0:T(8,128)S(1)} custom-call(s32[1]{0:T(128)} %bitcast.1.col_ref, f32[384,768]{1,0:T(8,128)S(1)} %copy-done.2, f32[384,384]{1,0:T(8,128)S(1)} %collective-permute-done.15.square_ref), custom_call_target="tpu_custom_call" | custom-call | flops 4000000000 | bytes 5000000 | tf_op jit(solution)/shard_map/inverse_factor/pallas_call | solution.py:256
  208.6 4.0 %fusion = f32[512,768]{1,0:T(8,128)S(1)} fusion(f32[768,768]{1,0:T(8,128)S(1)} %inverse_factor.1, f32[256,768]{1,0:T(8,128)S(1)} %slice.73, f32[256,768]{1,0:T(8,128)S(1)} %copy-done.4), kind=kOutput, calls=%fused_computation | convolution fusion | flops 3624271872 | bytes 5505024 | tf_op jit(solution)/shard_map/dot_general | solution.py:25
  212.6 0.9 slice_select_fusion
  213.6 0.6 fusion.4
  214.1 2.1 fusion.18.x_ref
  216.3 20.9 %update_of.1.update_ref = f32[256,8192]{1,0:T(8,128)} custom-call(s32[64]{0:T(128)S(1)} %stack.259.order_ref, f32[256,768]{1,0:T(8,128)S(1)} %fusion.18.x_ref, f32[1024,768]{1,0:T(8,128)} %constant_dynamic-update-slice_fusion.refs_0_, f32[1024,768]{1,0:T(8,128)S(1)} %copy-done.1, f32[1024,768]{1,0:T(8,128)} %collective-permute-done.7.refs_2_, ...), custom_call_target="tpu_custom_call" | custom-call | flops 9663676416 | bytes 34000000 | tf_op jit(solution)/shard_map/update_of/pallas_call | solution.py:339
  237.2 29.0 %all-to-all-done.1.arrived_ref = f32[64,4,8192]{2,1,0:T(4,128)} async-done(((f32[64,4,8192]{2,1,0:T(4,128)}), f32[64,4,8192]{2,1,0:T(4,128)}, u32[]{:S(2)}, u32[]{:S(2)}) %all-to-all-start.1) | async-done | bytes 8388640 | tf_op jit(solution)/shard_map/all_to_all | solution.py:436
  266.2 17.0 %place_rows.1 = f32[256,8192]{1,0:T(8,128)} custom-call(bf16[256,256]{1,0:T(8,128)(2,1)} %convert_convert_fusion.place_ref, f32[64,4,8192]{2,1,0:T(4,128)} %all-to-all-done.1.arrived_ref, f32[256,8192]{1,0:T(8,128)} %update_of.1.update_ref), custom_call_target="tpu_custom_call" | custom-call | flops 3221225472 | bytes 25165824 | tf_op jit(solution)/shard_map/place_rows/pallas_call | solution.py:379
  (28 shorter events, 0.2 us)
Async XLA Ops:
  1.7 12.4 %collective-permute-start = (f32[256,384]{1,0:T(8,128)S(1)}, f32[256,384]{1,0:T(8,128)S(1)}, u32[]{:S(2)}, u32[]{:S(2)}) collective-permute-start(f32[256,384]{1,0:T(8,128)S(1)} %slice.48), channel_id=1, source_target_pairs={{0,1},{1,0},{2,3},{3,2},{4,5},{5,4},{6,7},{7,6},{8,9},{9,8},{10,11... | collective-permute-start | bytes 1179656 | tf_op jit(solution)/shard_map/ppermute | solution.py:412
  19.1 28.2 %copy-start.3 = (f32[256,768]{1,0:T(8,128)}, f32[256,768]{1,0:T(8,128)S(1)}, u32[]{:S(2)}) copy-start(f32[256,768]{1,0:T(8,128)S(1)} %get-tuple-element.21) | copy-start | bytes 2359300
  20.0 9.1 %collective-permute-start.1 = (f32[128,768]{1,0:T(8,128)S(1)}, f32[128,768]{1,0:T(8,128)S(1)}, u32[]{:S(2)}, u32[]{:S(2)}) collective-permute-start(f32[128,768]{1,0:T(8,128)S(1)} %get-tuple-element.17), channel_id=1, source_target_pairs={{0,16},{2,18},{4,20},{6,22},{8,24},{10,26},{12,28},{14,30},{16,0},... | collective-permute-start | bytes 1179656 | tf_op jit(solution)/shard_map/ppermute | solution.py:59
  29.2 13.5 %collective-permute-start.2 = (f32[256,768]{1,0:T(8,128)S(1)}, f32[256,768]{1,0:T(8,128)S(1)}, u32[]{:S(2)}, u32[]{:S(2)}) collective-permute-start(f32[256,768]{1,0:T(8,128)S(1)} %pad_maximum_fusion), channel_id=1, source_target_pairs={{0,4},{2,34},{4,8},{6,38},{8,12},{10,42},{12,0},{14,46},{16,20},{1... | collective-permute-start | bytes 2359304 | tf_op jit(solution)/shard_map/ppermute | solution.py:59
  30.9 11.9 %collective-permute-start.3 = (f32[256,768]{1,0:T(8,128)S(1)}, f32[256,768]{1,0:T(8,128)S(1)}, u32[]{:S(2)}, u32[]{:S(2)}) collective-permute-start(f32[256,768]{1,0:T(8,128)S(1)} %pad_maximum_fusion), channel_id=1, source_target_pairs={{0,12},{2,98},{4,0},{6,102},{8,4},{10,106},{12,8},{14,110},{16,28}... | collective-permute-start | bytes 2359304 | tf_op jit(solution)/shard_map/ppermute | solution.py:59
  42.7 13.0 %copy-start.5 = (s32[1,256]{1,0:T(1,128)S(1)}, s32[1,256]{1,0:T(1,128)}, u32[]{:S(2)}) copy-start(s32[1,256]{1,0:T(1,128)} %param.3) | copy-start | bytes 3076
  42.7 8.2 %collective-permute-start.4 = (f32[128,768]{1,0:T(8,128)S(1)}, f32[128,768]{1,0:T(8,128)S(1)}, u32[]{:S(2)}, u32[]{:S(2)}) collective-permute-start(f32[128,768]{1,0:T(8,128)S(1)} %slice.70), channel_id=1, source_target_pairs={{0,4},{2,34},{4,8},{6,38},{8,12},{10,42},{12,0},{14,46},{16,20},{1... | collective-permute-start | bytes 1179656 | tf_op jit(solution)/shard_map/ppermute | solution.py:59
  42.8 8.9 %collective-permute-start.5 = (f32[128,768]{1,0:T(8,128)S(1)}, f32[128,768]{1,0:T(8,128)S(1)}, u32[]{:S(2)}, u32[]{:S(2)}) collective-permute-start(f32[128,768]{1,0:T(8,128)S(1)} %slice.71), channel_id=1, source_target_pairs={{0,12},{2,98},{4,0},{6,102},{8,4},{10,106},{12,8},{14,110},{16,28}... | collective-permute-start | bytes 1179656 | tf_op jit(solution)/shard_map/ppermute | solution.py:59
  52.5 52.8 %collective-permute-start.6 = (f32[1024,768]{1,0:T(8,128)}, f32[1024,768]{1,0:T(8,128)S(1)}, u32[]{:S(2)}, u32[]{:S(2)}) collective-permute-start(f32[1024,768]{1,0:T(8,128)} %constant_dynamic-update-slice_fusion.refs_0_), channel_id=1, source_target_pairs={{0,32},{2,6},{4,36},{6,10},{8,40},{10,14},{12,44},{14,2},{16,48},{... | collective-permute-start | bytes 9437192 | tf_op jit(solution)/shard_map/ppermute | solution.py:59
  53.1 52.2 %collective-permute-start.7 = (f32[1024,768]{1,0:T(8,128)}, f32[1024,768]{1,0:T(8,128)}, u32[]{:S(2)}, u32[]{:S(2)}) collective-permute-start(f32[1024,768]{1,0:T(8,128)} %constant_dynamic-update-slice_fusion.refs_0_), channel_id=1, source_target_pairs={{0,96},{2,14},{4,100},{6,2},{8,104},{10,6},{12,108},{14,10},{16,11... | collective-permute-start | bytes 9437192 | tf_op jit(solution)/shard_map/ppermute | solution.py:59
  60.6 44.7 %all-to-all-start = ((f32[64,4,896]{2,1,0:T(4,128)}), f32[64,4,896]{2,1,0:T(4,128)}, u32[]{:S(2)}, u32[]{:S(2)}) async-start(f32[64,4,896]{2,1,0:T(4,128)} %pack_runs.2), calls=%async_computation | async-start | bytes 1835008 | tf_op jit(solution)/shard_map/all_to_all | solution.py:418
  72.1 58.9 %collective-permute-start.10 = (f32[1024,768]{1,0:T(8,128)}, f32[1024,768]{1,0:T(8,128)}, u32[]{:S(2)}, u32[]{:S(2)}) collective-permute-start(f32[1024,768]{1,0:T(8,128)} %constant_dynamic-update-slice_fusion.refs_0_), channel_id=1, source_target_pairs={{0,2},{2,0},{4,6},{6,4},{8,10},{10,8},{12,14},{14,12},{16,18},{18,... | collective-permute-start | bytes 9437192 | tf_op jit(solution)/shard_map/ppermute | solution.py:59
  105.3 5.0 %copy-start = (f32[1024,768]{1,0:T(8,128)}, f32[1024,768]{1,0:T(8,128)S(1)}, u32[]{:S(2)}) copy-start(f32[1024,768]{1,0:T(8,128)S(1)} %collective-permute-done.6.refs_1_) | copy-start | bytes 9437188
  105.4 20.9 %collective-permute-start.8 = (f32[512,768]{1,0:T(8,128)S(1)}, f32[512,768]{1,0:T(8,128)}, u32[]{:S(2)}, u32[]{:S(2)}) collective-permute-start(f32[512,768]{1,0:T(8,128)S(1)} %slice.59), channel_id=1, source_target_pairs={{0,32},{2,6},{4,36},{6,10},{8,40},{10,14},{12,44},{14,2},{16,48},{... | collective-permute-start | bytes 4718600 | tf_op jit(solution)/shard_map/ppermute | solution.py:59
  108.0 20.4 %collective-permute-start.9 = (f32[512,768]{1,0:T(8,128)S(1)}, f32[512,768]{1,0:T(8,128)}, u32[]{:S(2)}, u32[]{:S(2)}) collective-permute-start(f32[512,768]{1,0:T(8,128)S(1)} %slice.60), channel_id=1, source_target_pairs={{0,96},{2,14},{4,100},{6,2},{8,104},{10,6},{12,108},{14,10},{16,11... | collective-permute-start | bytes 4718600 | tf_op jit(solution)/shard_map/ppermute | solution.py:59
  110.3 23.7 %collective-permute-start.11 = (f32[1024,768]{1,0:T(8,128)S(1)}, f32[1024,768]{1,0:T(8,128)}, u32[]{:S(2)}, u32[]{:S(2)}) collective-permute-start(f32[1024,768]{1,0:T(8,128)S(1)} %collective-permute-done.6.refs_1_), channel_id=1, source_target_pairs={{0,2},{2,0},{4,6},{6,4},{8,10},{10,8},{12,14},{14,12},{16,18},{18,... | collective-permute-start | bytes 9437192 | tf_op jit(solution)/shard_map/ppermute | solution.py:59
  111.5 22.5 %collective-permute-start.12 = (f32[1024,768]{1,0:T(8,128)}, f32[1024,768]{1,0:T(8,128)}, u32[]{:S(2)}, u32[]{:S(2)}) collective-permute-start(f32[1024,768]{1,0:T(8,128)} %collective-permute-done.7.refs_2_), channel_id=1, source_target_pairs={{0,2},{2,0},{4,6},{6,4},{8,10},{10,8},{12,14},{14,12},{16,18},{18,... | collective-permute-start | bytes 9437192 | tf_op jit(solution)/shard_map/ppermute | solution.py:59
  126.4 5.4 %collective-permute-start.13 = (f32[512,768]{1,0:T(8,128)}, f32[512,768]{1,0:T(8,128)}, u32[]{:S(2)}, u32[]{:S(2)}) collective-permute-start(f32[512,768]{1,0:T(8,128)} %collective-permute-done.8.refs_3_), channel_id=1, source_target_pairs={{0,2},{2,0},{4,6},{6,4},{8,10},{10,8},{12,14},{14,12},{16,18},{18,... | collective-permute-start | bytes 4718600 | tf_op jit(solution)/shard_map/ppermute | solution.py:59
  128.4 5.6 %collective-permute-start.14 = (f32[512,768]{1,0:T(8,128)}, f32[512,768]{1,0:T(8,128)}, u32[]{:S(2)}, u32[]{:S(2)}) collective-permute-start(f32[512,768]{1,0:T(8,128)} %collective-permute-done.9.refs_4_), channel_id=1, source_target_pairs={{0,2},{2,0},{4,6},{6,4},{8,10},{10,8},{12,14},{14,12},{16,18},{18,... | collective-permute-start | bytes 4718600 | tf_op jit(solution)/shard_map/ppermute | solution.py:59
  139.0 16.4 %collective-permute-start.15 = (f32[384,384]{1,0:T(8,128)}, f32[384,384]{1,0:T(8,128)S(1)}, u32[]{:S(2)}, u32[]{:S(2)}) collective-permute-start(f32[384,384]{1,0:T(8,128)} %get-tuple-element.13), channel_id=1, source_target_pairs={{0,1},{1,0},{2,3},{3,2},{4,5},{5,4},{6,7},{7,6},{8,9},{9,8},{10,11... | collective-permute-start | bytes 1769480 | tf_op jit(solution)/shard_map/ppermute | solution.py:434
  155.4 110.9 %all-to-all-start.1 = ((f32[64,4,8192]{2,1,0:T(4,128)}), f32[64,4,8192]{2,1,0:T(4,128)}, u32[]{:S(2)}, u32[]{:S(2)}) async-start(f32[64,4,8192]{2,1,0:T(4,128)} %pack_runs.3), calls=%async_computation.1 | async-start | bytes 16777216 | tf_op jit(solution)/shard_map/all_to_all | solution.py:436
  164.1 2.5 copy-start.2
  166.7 42.0 %copy-start.4 = (f32[256,768]{1,0:T(8,128)S(1)}, f32[256,768]{1,0:T(8,128)}, u32[]{:S(2)}) copy-start(f32[256,768]{1,0:T(8,128)} %copy-done.3) | copy-start | bytes 2359300
  213.5 2.8 copy-start.1

commit v3 on v2

--- a/solution.py
+++ b/solution.py
@@ -2,6 +2,7 @@
 
 import jax
 import jax.numpy as jnp
+import numpy as np
 from jax import lax
 from jax.experimental import pallas as pl
 from jax.experimental.pallas import tpu as pltpu
@@ -59,36 +60,41 @@
     return lax.ppermute(value, "row", pairs_of(kind, step))
 
 
-def ring(value, kind, beside=None):
+def ring(value, kind, beside):
     half = value.shape[0] // 2
     before = move(value, kind, 1)
     after = move(value, kind, -1)
-    if beside is not None:
-        before, after, beside = lax.optimization_barrier((before, after, beside))
+    before, after, beside = lax.optimization_barrier((before, after, beside))
     far_first = move(before[:half], kind, 1)
     far_second = move(after[half:], kind, -1)
     return [value, before, after, far_first, far_second], beside
 
 
-def gather_rows(mine, beside):
+def gather_rows(mine, small, runs):
     value = jnp.concatenate([mine, move(mine, "y")], axis=0)
-    value = jnp.concatenate(ring(value, "first")[0], axis=0)
-    pieces, beside = ring(value, "second", beside)
-    return pieces + [move(p, "core") for p in pieces], beside
-
-
-def block_order(row):
-    z, y, x, k = row // 16, (row // 8) % 2, (row // 2) % 4, row % 2
+    parts, small = ring(value, "first", small)
+    value = jnp.concatenate(parts, axis=0)
+    pieces, runs = ring(value, "second", runs)
+    runs, *swapped = lax.optimization_barrier((runs, *(move(p, "core") for p in pieces)))
+    return pieces + swapped, small, runs
+
+
+def block_table():
     first = ((0, 0), (0, 1), (-1, 0), (-1, 1), (1, 0), (1, 1), (2, 0), (2, 1))
-    order = []
-    for swapped in (0, 1):
-        core = k ^ swapped
-        for second, part in ((0, first), (-1, first), (1, first), (2, first[:4]), (2, first[4:])):
-            for along, flip in part:
-                xs = jnp.where(core == 0, x + along, x + second) % 4
-                zs = jnp.where(core == 0, z + second, z + along) % 4
-                order.append(row_id(zs, y ^ flip, xs, core))
-    return jnp.stack(order).astype(jnp.int32)
+    table = np.zeros((N_ROW, BW), np.int32)
+    for row in range(N_ROW):
+        z, y, x, k = row // 16, (row // 8) % 2, (row // 2) % 4, row % 2
+        order = []
+        for core in (k, 1 - k):
+            for second, part in (
+                (0, first), (-1, first), (1, first), (2, first[:4]), (2, first[4:])
+            ):
+                for along, flip in part:
+                    xs, zs = (along, second) if core == 0 else (second, along)
+                    order.append(row_id((z + zs) % 4, y ^ flip, (x + xs) % 4, core))
+        table[row, :N_ROW] = order
+        table[row, N_ROW : N_ROW + NP] = [order.index(q) for q in range(NP)]
+    return table
 
 
 def pack_kernel(slot_ref, rows_ref, out_ref):
@@ -96,15 +102,15 @@
         out_ref[slot_ref[g]] = rows_ref[g * CAP : (g + 1) * CAP, :]
 
 
-def pack_runs(slots, rows, tile):
-    height, width = rows.shape
+def pack_runs(slots, rows, start, width, tile):
+    height = rows.shape[0]
     return pl.pallas_call(
         pack_kernel,
         out_shape=jax.ShapeDtypeStruct((N_ROW, CAP, width), rows.dtype),
         grid_spec=pltpu.PrefetchScalarGridSpec(
             num_scalar_prefetch=1,
             grid=(width // tile,),
-            in_specs=[pl.BlockSpec((height, tile), lambda i, s: (0, i))],
+            in_specs=[pl.BlockSpec((height, tile), lambda i, s: (0, i + start // tile))],
             out_specs=pl.BlockSpec((N_ROW, CAP, tile), lambda i, s: (0, 0, i)),
         ),
         cost_estimate=pl.CostEstimate(
@@ -208,7 +214,7 @@
     return jnp.concatenate(out, axis=0)
 
 
-def factor_kernel(col_ref, rows_ref, square_ref, w_ref):
+def factor_kernel(col_ref, rows_ref, squares_ref, w_ref):
     def span(i):
         return slice(i * BW, (i + 1) * BW)
 
@@ -223,7 +229,8 @@
                     other = rows_ref[span(q), span(2 * p + d)]
                     w_ref[span(2 * q + c), span(2 * p + d)] = other
                     w_ref[span(2 * p + d), span(2 * q + c)] = other.T
-                    w_ref[span(2 * q + d), span(2 * p + d)] = square_ref[span(q), span(p)]
+                    square = squares_ref[span(NP * d + q), span(p)]
+                    w_ref[span(2 * q + d), span(2 * p + d)] = square
 
     n = PANEL
     row_ids = lax.broadcasted_iota(jnp.int32, (n, BW), 0)
@@ -252,7 +259,7 @@
     w_ref[...] = jnp.where(cols_of <= rows_of, w_ref[...], 0.0)
 
 
-def inverse_factor(col, rows, square):
+def inverse_factor(col, rows, squares):
     return pl.pallas_call(
         factor_kernel,
         out_shape=jax.ShapeDtypeStruct((PANEL, PANEL), jnp.float32),
@@ -264,7 +271,7 @@
             flops=4 * 10**9, bytes_accessed=5 * 10**6, transcendentals=0
         ),
         name="inverse_factor",
-    )(col, rows, square)
+    )(col, rows, squares)
 
 
 def update_kernel(order_ref, x_ref, *refs):
@@ -358,40 +365,44 @@
     )(order, x, *pieces)
 
 
-def place_kernel(tile, place_ref, arrived_ref, update_ref, out_ref, rows):
+def place_kernel(start, tile, goes_ref, arrived_ref, update_ref, *refs):
+    out_ref = refs[-1]
+    masked = start < HEAD
+    if masked:
+        column = pl.program_id(0) * tile + lax.broadcasted_iota(jnp.int32, (1, tile), 1)
+        kept = column >= HEAD - start
     for b in range(N_ROW):
-        rows[b * CAP : (b + 1) * CAP, :] = arrived_ref[b]
-    place = place_ref[...]
-    value = rows[...]
-    total = None
-    for part in range(3):
-        piece = value.astype(jnp.bfloat16)
-        term = jnp.dot(place, piece, preferred_element_type=jnp.float32)
-        total = term if total is None else total + term
-        if part < 2:
-            value = value - piece.astype(jnp.float32)
-    column = pl.program_id(0) * tile + lax.broadcasted_iota(jnp.int32, (1, tile), 1)
-    out_ref[...] = jnp.where(column >= HEAD, total - update_ref[...], 0.0)
-
-
-def place_rows(place, arrived, update, tile=512):
+        for i in range(CAP):
+            at = b * CAP + i
+            if b < NP:
+                value = jnp.zeros((1, tile), jnp.float32)
+            else:
+                value = arrived_ref[b, i : i + 1, :] - update_ref[at : at + 1, :]
+                if masked:
+                    value = jnp.where(kept, value, 0.0)
+            out_ref[pl.ds(goes_ref[at], 1), :] = value
+
+
+def place_rows(goes, arrived, update, start, parent=None, tile=512):
     width = arrived.shape[2]
+    first = start // tile
     return pl.pallas_call(
-        functools.partial(place_kernel, tile),
-        out_shape=jax.ShapeDtypeStruct((PW, width), jnp.float32),
+        functools.partial(place_kernel, start, tile),
+        out_shape=jax.ShapeDtypeStruct(update.shape, jnp.float32),
         grid=(width // tile,),
         in_specs=[
-            pl.BlockSpec((PW, PW), lambda i: (0, 0)),
+            pl.BlockSpec(memory_space=pltpu.SMEM),
             pl.BlockSpec((N_ROW, CAP, tile), lambda i: (0, 0, i)),
-            pl.BlockSpec((PW, tile), lambda i: (0, i)),
-        ],
-        out_specs=pl.BlockSpec((PW, tile), lambda i: (0, i)),
-        scratch_shapes=[pltpu.VMEM((PW, tile), jnp.float32)],
+            pl.BlockSpec((PW, tile), lambda i: (0, i + first)),
+        ]
+        + ([] if parent is None else [pl.BlockSpec(memory_space=pl.ANY)]),
+        out_specs=pl.BlockSpec((PW, tile), lambda i: (0, i + first)),
+        input_output_aliases={} if parent is None else {3: 0},
         cost_estimate=pl.CostEstimate(
-            flops=6 * PW * PW * width, bytes_accessed=12 * PW * width, transcendentals=0
+            flops=PW * width, bytes_accessed=12 * PW * width, transcendentals=0
         ),
         name="place_rows",
-    )(place, arrived, update)
+    )(goes, arrived, update, *([] if parent is None else [parent]))
 
 
 def weave(own, other, col):
@@ -414,40 +425,37 @@
     targets = row_map[0].reshape(N_ROW, CAP)[:, 0] // PW
     within = (row_map[0] % PW).astype(jnp.float32)
     small = jnp.concatenate([panel, jnp.broadcast_to(within[:, None], (PW, BW))], axis=1)
-    small = pack_runs(targets, small, small.shape[1])
+    small = pack_runs(targets, small, 0, PANEL + BW, PANEL + BW)
+    mine = lax.dynamic_slice_in_dim(panel, col * BW, BW, 0)
+    mine, small = lax.optimization_barrier((mine, small))
     small = lax.all_to_all(small, "row", split_axis=0, concat_axis=0, tiled=True)
-    outgoing = pack_runs(targets, front_matrix, 512)
-
-    mine = lax.dynamic_slice_in_dim(panel, col * BW, BW, 0)
-    pieces, small = gather_rows(mine, small)
-    order = block_order(row)
-    places = jnp.sum(
-        jnp.where(
-            order[None, :] == jnp.arange(NP, dtype=jnp.int32)[:, None],
-            jnp.arange(N_ROW, dtype=jnp.int32)[None, :],
-            0,
-        ),
-        axis=1,
-    )
+
+    def packed(slots):
+        return pack_runs(slots, front_matrix, 0, width, 512)
+
+    def send(runs):
+        return lax.all_to_all(runs, "row", split_axis=0, concat_axis=0, tiled=True)
+
+    pieces, small, outgoing = gather_rows(mine, small, packed(targets))
+    cuts = (0,)
+    arrived = [send(outgoing)]
+
+    table = lax.dynamic_slice_in_dim(jnp.asarray(block_table()), row, 1, 0)[0]
+    order, places = table[:N_ROW], table[N_ROW : N_ROW + 8]
     cols = col.reshape(1).astype(jnp.int32)
     rows, square = head_rows(places, cols, pieces)
-    other_square = lax.ppermute(square, "col", swap)
-    outgoing, other_square = lax.optimization_barrier((outgoing, other_square))
-    arrived = lax.all_to_all(outgoing, "row", split_axis=0, concat_axis=0, tiled=True)
-
-    w = inverse_factor(cols, rows, other_square)
+    squares = lax.all_gather(square, "col", axis=0, tiled=True)
+
+    w = inverse_factor(cols, rows, squares)
     small = small.reshape(PW, PANEL + BW)
-    both = dot_t(jnp.concatenate([panel, small[:, :PANEL]], axis=0), w)
+    goes = small[:, PANEL].astype(jnp.int32)
+    lower = dot_t(small[:, :PANEL], w)
+    update = update_of(order, dot_n(lower, w), pieces, width)
     panel_ids = lax.broadcasted_iota(jnp.int32, (1, PANEL), 1) // PW
-    factors = jnp.where(row >= panel_ids, both[:PW], 0.0)
-
-    slots = jnp.arange(PW, dtype=jnp.int32)
-    goes = small[:, PANEL].astype(jnp.int32)
-    place = (goes[None, :] == slots[:, None]) & (slots[None, :] >= NP * CAP)
-    place = place.astype(jnp.float32)
-    x = dot_n(dot_n(place, both[PW:]), w)
-    update = update_of(order, x, pieces, width)
-    parent = place_rows(place.astype(jnp.bfloat16), arrived, update)
+    factors = jnp.where(row >= panel_ids, dot_t(panel, w), 0.0)
+    parent = None
+    for start, part in zip(cuts, arrived):
+        parent = place_rows(goes, part, update, start, parent)
     return factors, parent
 
 

time: 287 us -> 359 us (1.25)
  waiting for transfers between devices: 109 us -> 171 us
  between operations: 0.86 us -> 14.4 us
  starting transfers between devices: 45.7 us -> 40.5 us
    all_gather x0 -> x1, waiting for transfers between devices: none -> 102 us  [local(): squares = lax.all_gather(square, 'col', axis=0, tiled=True)]
    all_to_all x1, waiting for transfers between devices: 29 us -> 0.01 us  [send(): return lax.all_to_all(runs, 'row', split_axis=0, concat_axis=0, tiled=True)]
    all_to_all x1, waiting for transfers between devices: 32.6 us -> 12.3 us  [local(): lax.all_to_all(small, 'row', split_axis=0, concat_axis=0, tiled=True)]
    ppermute x14, waiting for transfers between devices: 38 us -> 51.7 us  [move(): return lax.ppermute(value, 'row', pairs_of(kind, step))]
    unnamed x24 -> x50, local copies, waits for them, and re-layouts: 8.93 us -> 11.2 us
  transfers between devices with their start and end apart: 18 -> 18, of which waited for: 10 -> 11; matrix products, arithmetic and copies ran while one was open for 7% -> 6% of each run, Pallas kernels for 28% -> 23%
where the time goes in v3:
time: 359 us; the launch traced here: 357 us
  waiting for transfers between devices  171 us (48%)
  Pallas kernels  102 us (28%)
  starting transfers between devices  40.5 us (11%)
  local copies, waits for them, and re-layouts  18.6 us (5%)
  between operations  14.4 us (4%)
  matrix products  7.34 us (2%)
  other arithmetic  3.71 us (1%)
    all_gather x1, waiting for transfers between devices, local(): squares = lax.all_gather(square, 'col', axis=0, tiled=True)  102 us
    ppermute x14, waiting for transfers between devices, move(): return lax.ppermute(value, 'row', pairs_of(kind, step))  51.7 us
    pallas_call x1, Pallas kernels, inverse_factor(): pl.pallas_call(factor_kernel, out_shape=jax.ShapeDtypeStruct((PANEL, PANE...  41.9 us
    pallas_call x1, Pallas kernels, update_of(): pl.pallas_call(update_kernel, out_shape=jax.ShapeDtypeStruct((PW, width),...  21.6 us
    ppermute x14, starting transfers between devices, move(): return lax.ppermute(value, 'row', pairs_of(kind, step))  19.8 us
    pallas_call x1, Pallas kernels, place_rows(): pl.pallas_call(functools.partial(place_kernel, start, tile), out_shape=ja...  17.7 us
    pallas_call x2, Pallas kernels, pack_runs(): pl.pallas_call(pack_kernel, out_shape=jax.ShapeDtypeStruct((N_ROW, CAP, w...  15.5 us
    all_to_all x1, waiting for transfers between devices, local(): lax.all_to_all(small, 'row', split_axis=0, concat_axis=0, tiled=True)  12.3 us
  transfers between devices with their start and end apart: 18, of which 11 were waited for; matrix products, arithmetic and copies ran while one was open for 6% of the time, Pallas kernels for 23%

profile of v3, /device:TPU:1, one launch (start us, length us, event | category | flops | bytes accessed | tf_op | source)
XLA Modules:
  0.0 357.4 jit_solution(9956561779013718504)
XLA Ops:
  7.2 1.0 slice.54
  8.2 3.8 %collective-permute-start = (f32[256,384]{1,0:T(8,128)S(1)}, f32[256,384]{1,0:T(8,128)S(1)}, u32[]{:S(2)}, u32[]{:S(2)}) collective-permute-start(f32[256,384]{1,0:T(8,128)S(1)} %slice.54), channel_id=1, source_target_pairs={{0,1},{1,0},{2,3},{3,2},{4,5},{5,4},{6,7},{7,6},{8,9},{9,8},{10,11... | collective-permute-start | bytes 1179656 | tf_op jit(solution)/shard_map/ppermute | solution.py:423
  12.0 0.5 broadcast.81
  12.5 1.3 reduce.5
  13.9 0.1 reshape_squeeze.3
  14.0 0.1 slice_reduce_fusion
  14.1 0.6 and_select_fusion.1.slot_ref
  14.7 0.7 fusion.6
  15.4 5.2 %collective-permute-done = f32[256,384]{1,0:T(8,128)S(1)} collective-permute-done((f32[256,384]{1,0:T(8,128)S(1)}, f32[256,384]{1,0:T(8,128)S(1)}, u32[]{:S(2)}, u32[]{:S(2)}) %collective-permute-start) | collective-permute-done | bytes 393248 | tf_op jit(solution)/shard_map/ppermute | solution.py:423
  20.6 1.0 broadcast_select_fusion
  21.8 0.0 copy-start.16
  21.8 0.1 broadcast_dynamic-update-slice_fusion.rows_ref
  21.9 0.0 copy-start.18
  21.9 1.0 copy-done.18
  22.9 2.9 pack_runs.2
  25.8 1.4 collective-permute-start.1
  27.2 10.2 %all-to-all-start = ((f32[64,4,896]{2,1,0:T(4,128)}), f32[64,4,896]{2,1,0:T(4,128)S(1)}, u32[]{:S(2)}, u32[]{:S(2)}) async-start(f32[64,4,896]{2,1,0:T(4,128)} %pack_runs.2), calls=%async_computation | async-start | bytes 1835008 | tf_op jit(solution)/shard_map/all_to_all | solution.py:431
  37.4 0.8 constant_dynamic-update-slice_fusion.1
  38.2 0.8 constant_dynamic-update-slice_fusion
  39.0 2.8 collective-permute-start.3
  41.8 12.3 %all-to-all-done = f32[64,4,896]{2,1,0:T(4,128)S(1)} async-done(((f32[64,4,896]{2,1,0:T(4,128)}), f32[64,4,896]{2,1,0:T(4,128)S(1)}, u32[]{:S(2)}, u32[]{:S(2)}) %all-to-all-start) | async-done | bytes 917536 | tf_op jit(solution)/shard_map/all_to_all | solution.py:431
  54.1 4.0 %collective-permute-done.3 = f32[256,768]{1,0:T(8,128)S(1)} collective-permute-done((f32[256,768]{1,0:T(8,128)S(1)}, f32[256,768]{1,0:T(8,128)S(1)}, u32[]{:S(2)}, u32[]{:S(2)}) %collective-permute-start.3) | collective-permute-done | bytes 786464 | tf_op jit(solution)/shard_map/ppermute | solution.py:60
  58.1 2.1 collective-permute-done.2
  60.3 0.1 collective-permute-start.4
  60.4 2.7 collective-permute-start.5
  63.1 0.9 constant_dynamic-update-slice_fusion.5
  64.0 0.9 constant_dynamic-update-slice_fusion.4
  65.0 3.4 collective-permute-done.4
  68.4 0.8 constant_dynamic-update-slice_fusion.3
  69.2 0.8 constant_dynamic-update-slice_fusion.2.refs_0_
  70.0 1.7 collective-permute-start.7
  71.7 12.7 %pack_runs.3 = f32[64,4,8192]{2,1,0:T(4,128)} custom-call(s32[64]{0:T(128)} %and_select_fusion.1.slot_ref, f32[256,8192]{1,0:T(8,128)} %rows_ref.1), custom_call_target="tpu_custom_call" | custom-call | bytes 16777216 | tf_op jit(solution)/shard_map/pack_runs/pallas_call | solution.py:107
  84.3 1.6 collective-permute-start.10
  86.0 20.7 %collective-permute-done.7.refs_2_ = f32[1024,768]{1,0:T(8,128)} collective-permute-done((f32[1024,768]{1,0:T(8,128)}, f32[1024,768]{1,0:T(8,128)}, u32[]{:S(2)}, u32[]{:S(2)}) %collective-permute-start.7) | collective-permute-done | bytes 3145760 | tf_op jit(solution)/shard_map/ppermute | solution.py:60
  106.7 2.8 collective-permute-done.6.refs_1_
  109.5 2.6 slice.67
  112.1 0.1 collective-permute-start.9
  112.2 0.1 slice.66
  112.3 1.5 collective-permute-start.8
  113.9 3.1 collective-permute-start.11
  116.9 14.9 %collective-permute-done.9.refs_4_ = f32[512,768]{1,0:T(8,128)S(1)} collective-permute-done((f32[512,768]{1,0:T(8,128)S(1)}, f32[512,768]{1,0:T(8,128)S(1)}, u32[]{:S(2)}, u32[]{:S(2)}) %collective-permute-start.9) | collective-permute-done | bytes 1572896 | tf_op jit(solution)/shard_map/ppermute | solution.py:60
  131.8 3.3 collective-permute-start.14
  135.1 1.5 collective-permute-start.13
  136.6 1.5 collective-permute-done.14.refs_9_
  138.2 2.2 collective-permute-done.13.refs_8_
  140.4 1.1 copy-done.8
  141.6 1.7 copy-done.15
  143.3 6.7 %all-to-all-start.1 = ((f32[64,4,8192]{2,1,0:T(4,128)}), f32[64,4,8192]{2,1,0:T(4,128)}, u32[]{:S(2)}, u32[]{:S(2)}) async-start(f32[64,4,8192]{2,1,0:T(4,128)} %pack_runs.3), calls=%async_computation.1 | async-start | bytes 16777216 | tf_op jit(solution)/shard_map/all_to_all | solution.py:437
  149.9 0.0 all-gather.2.cloned.1.call-start
  150.0 0.7 constant_dynamic-slice_fusion.1
  150.7 0.6 slice_bitcast_fusion.1.place_ref
  151.3 5.1 %head_rows.1 = (f32[384,768]{1,0:T(8,128)}, f32[384,384]{1,0:T(8,128)}) custom-call(s32[8]{0:T(128)} %slice_bitcast_fusion.1.place_ref, s32[1]{0:T(128)} %bitcast.col_ref, f32[1024,768]{1,0:T(8,128)} %constant_dynamic-update-slice_fusion.2.refs_0_, f32[1024,768]{1,0:T(8,128)} %copy-done, f32[1024,768]{1,0:T(8,128)} %collective-permute-done.7.refs_2_, ...), custom_call_target="tpu_custom_call" | custom-call | bytes 4000000 | tf_op jit(solution)/shard_map/head_rows/pallas_call | solution.py:151
  156.4 0.0 all-gather.2.cloned.1.call-update
  156.4 0.3 reshape.75
  156.8 0.7 copy.9
  157.5 101.9 %all-gather.2.cloned.1.call-done.squares_ref = f32[768,384]{1,0:T(8,128)} async-done(((f32[384,384]{1,0:T(8,128)}), f32[768,384]{1,0:T(8,128)}) %all-gather.2.cloned.1.call-update) | async-done | bytes 1179664 | tf_op jit(solution)/shard_map/all_gather | solution.py:447
  259.3 1.3 copy-done.10
  260.6 1.3 copy-done.11
  261.9 41.9 %inverse_factor.1 = f32[768,768]{1,0:T(8,128)S(1)} custom-call(s32[1]{0:T(128)} %bitcast.col_ref, f32[384,768]{1,0:T(8,128)S(1)} %copy-done.10, f32[768,384]{1,0:T(8,128)S(1)} %copy-done.11), custom_call_target="tpu_custom_call" | custom-call | flops 4000000000 | bytes 5000000 | tf_op jit(solution)/shard_map/inverse_factor/pallas_call | solution.py:263
  303.9 2.2 fusion
  306.1 2.1 fusion.8.x_ref
  308.2 3.0 convolution_select_fusion
  311.3 21.6 %update_of.1.update_ref = f32[256,8192]{1,0:T(8,128)} custom-call(s32[64]{0:T(128)S(1)} %slice_bitcast_fusion.order_ref, f32[256,768]{1,0:T(8,128)S(1)} %fusion.8.x_ref, f32[1024,768]{1,0:T(8,128)} %constant_dynamic-update-slice_fusion.2.refs_0_, f32[1024,768]{1,0:T(8,128)S(1)} %copy-done.1, f32[1024,768]{1,0:T(8,128)} %collective-permute-done.7.refs_2_, ...), custom_call_target="tpu_custom_call" | custom-call | flops 9663676416 | bytes 34000000 | tf_op jit(solution)/shard_map/update_of/pallas_call | solution.py:346
  332.9 17.7 %place_rows.1 = f32[256,8192]{1,0:T(8,128)} custom-call(s32[256]{0:T(256)} %bitcast.12, f32[64,4,8192]{2,1,0:T(4,128)} %all-to-all-done.1.arrived_ref, f32[256,8192]{1,0:T(8,128)} %update_of.1.update_ref), custom_call_target="tpu_custom_call" | custom-call | flops 2097152 | bytes 25165824 | tf_op jit(solution)/shard_map/place_rows/pallas_call | solution.py:389
  (53 shorter events, 0.3 us)
Async XLA Ops:
  8.2 12.4 %collective-permute-start = (f32[256,384]{1,0:T(8,128)S(1)}, f32[256,384]{1,0:T(8,128)S(1)}, u32[]{:S(2)}, u32[]{:S(2)}) collective-permute-start(f32[256,384]{1,0:T(8,128)S(1)} %slice.54), channel_id=1, source_target_pairs={{0,1},{1,0},{2,3},{3,2},{4,5},{5,4},{6,7},{7,6},{8,9},{9,8},{10,11... | collective-permute-start | bytes 1179656 | tf_op jit(solution)/shard_map/ppermute | solution.py:423
  21.8 5.4 %copy-start.16 = (f32[256,768]{1,0:T(8,128)}, f32[256,768]{1,0:T(8,128)S(1)}, u32[]{:S(2)}) copy-start(f32[256,768]{1,0:T(8,128)S(1)} %get-tuple-element.41) | copy-start | bytes 2359300
  21.9 1.0 copy-start.18
  25.8 12.4 %collective-permute-start.1 = (f32[128,768]{1,0:T(8,128)S(1)}, f32[128,768]{1,0:T(8,128)S(1)}, u32[]{:S(2)}, u32[]{:S(2)}) collective-permute-start(f32[128,768]{1,0:T(8,128)S(1)} %constant_dynamic-slice_fusion), channel_id=1, source_target_pairs={{0,16},{2,18},{4,20},{6,22},{8,24},{10,26},{12,28},{14,30},{16,0},... | collective-permute-start | bytes 1179656 | tf_op jit(solution)/shard_map/ppermute | solution.py:60
  27.2 26.9 %all-to-all-start = ((f32[64,4,896]{2,1,0:T(4,128)}), f32[64,4,896]{2,1,0:T(4,128)S(1)}, u32[]{:S(2)}, u32[]{:S(2)}) async-start(f32[64,4,896]{2,1,0:T(4,128)} %pack_runs.2), calls=%async_computation | async-start | bytes 1835008 | tf_op jit(solution)/shard_map/all_to_all | solution.py:431
  39.0 19.1 %collective-permute-start.3 = (f32[256,768]{1,0:T(8,128)S(1)}, f32[256,768]{1,0:T(8,128)S(1)}, u32[]{:S(2)}, u32[]{:S(2)}) collective-permute-start(f32[256,768]{1,0:T(8,128)S(1)} %get-tuple-element.36), channel_id=1, source_target_pairs={{0,12},{2,98},{4,0},{6,102},{8,4},{10,106},{12,8},{14,110},{16,28}... | collective-permute-start | bytes 2359304 | tf_op jit(solution)/shard_map/ppermute | solution.py:60
  41.8 18.4 %collective-permute-start.2 = (f32[256,768]{1,0:T(8,128)S(1)}, f32[256,768]{1,0:T(8,128)S(1)}, u32[]{:S(2)}, u32[]{:S(2)}) collective-permute-start(f32[256,768]{1,0:T(8,128)S(1)} %get-tuple-element.36), channel_id=1, source_target_pairs={{0,4},{2,34},{4,8},{6,38},{8,12},{10,42},{12,0},{14,46},{16,20},{1... | collective-permute-start | bytes 2359304 | tf_op jit(solution)/shard_map/ppermute | solution.py:60
  54.1 15.9 %copy-start.12 = (f32[64,4,896]{2,1,0:T(4,128)}, f32[64,4,896]{2,1,0:T(4,128)S(1)}, u32[]{:S(2)}) copy-start(f32[64,4,896]{2,1,0:T(4,128)S(1)} %all-to-all-done) | copy-start | bytes 2752516
  60.3 8.1 %collective-permute-start.4 = (f32[128,768]{1,0:T(8,128)S(1)}, f32[128,768]{1,0:T(8,128)S(1)}, u32[]{:S(2)}, u32[]{:S(2)}) collective-permute-start(f32[128,768]{1,0:T(8,128)S(1)} %slice.64), channel_id=1, source_target_pairs={{0,4},{2,34},{4,8},{6,38},{8,12},{10,42},{12,0},{14,46},{16,20},{1... | collective-permute-start | bytes 1179656 | tf_op jit(solution)/shard_map/ppermute | solution.py:60
  60.4 8.8 %collective-permute-start.5 = (f32[128,768]{1,0:T(8,128)S(1)}, f32[128,768]{1,0:T(8,128)S(1)}, u32[]{:S(2)}, u32[]{:S(2)}) collective-permute-start(f32[128,768]{1,0:T(8,128)S(1)} %slice.65), channel_id=1, source_target_pairs={{0,12},{2,98},{4,0},{6,102},{8,4},{10,106},{12,8},{14,110},{16,28}... | collective-permute-start | bytes 1179656 | tf_op jit(solution)/shard_map/ppermute | solution.py:60
  70.0 36.7 %collective-permute-start.7 = (f32[1024,768]{1,0:T(8,128)}, f32[1024,768]{1,0:T(8,128)}, u32[]{:S(2)}, u32[]{:S(2)}) collective-permute-start(f32[1024,768]{1,0:T(8,128)} %constant_dynamic-update-slice_fusion.2.refs_0_), channel_id=1, source_target_pairs={{0,96},{2,14},{4,100},{6,2},{8,104},{10,6},{12,108},{14,10},{16,11... | collective-permute-start | bytes 9437192 | tf_op jit(solution)/shard_map/ppermute | solution.py:60
  71.7 37.8 %collective-permute-start.6 = (f32[1024,768]{1,0:T(8,128)}, f32[1024,768]{1,0:T(8,128)S(1)}, u32[]{:S(2)}, u32[]{:S(2)}) collective-permute-start(f32[1024,768]{1,0:T(8,128)} %constant_dynamic-update-slice_fusion.2.refs_0_), channel_id=1, source_target_pairs={{0,32},{2,6},{4,36},{6,10},{8,40},{10,14},{12,44},{14,2},{16,48},{... | collective-permute-start | bytes 9437192 | tf_op jit(solution)/shard_map/ppermute | solution.py:60
  84.3 52.3 %collective-permute-start.10 = (f32[1024,768]{1,0:T(8,128)}, f32[1024,768]{1,0:T(8,128)S(1)}, u32[]{:S(2)}, u32[]{:S(2)}) collective-permute-start(f32[1024,768]{1,0:T(8,128)} %constant_dynamic-update-slice_fusion.2.refs_0_), channel_id=1, source_target_pairs={{0,2},{2,0},{4,6},{6,4},{8,10},{10,8},{12,14},{14,12},{16,18},{18,... | collective-permute-start | bytes 9437192 | tf_op jit(solution)/shard_map/ppermute | solution.py:60
  109.5 4.4 %copy-start = (f32[1024,768]{1,0:T(8,128)}, f32[1024,768]{1,0:T(8,128)S(1)}, u32[]{:S(2)}) copy-start(f32[1024,768]{1,0:T(8,128)S(1)} %collective-permute-done.6.refs_1_) | copy-start | bytes 9437188
  112.1 19.6 %collective-permute-start.9 = (f32[512,768]{1,0:T(8,128)S(1)}, f32[512,768]{1,0:T(8,128)S(1)}, u32[]{:S(2)}, u32[]{:S(2)}) collective-permute-start(f32[512,768]{1,0:T(8,128)S(1)} %slice.67), channel_id=1, source_target_pairs={{0,96},{2,14},{4,100},{6,2},{8,104},{10,6},{12,108},{14,10},{16,11... | collective-permute-start | bytes 4718600 | tf_op jit(solution)/shard_map/ppermute | solution.py:60
  112.3 22.8 %collective-permute-start.8 = (f32[512,768]{1,0:T(8,128)S(1)}, f32[512,768]{1,0:T(8,128)S(1)}, u32[]{:S(2)}, u32[]{:S(2)}) collective-permute-start(f32[512,768]{1,0:T(8,128)S(1)} %slice.66), channel_id=1, source_target_pairs={{0,32},{2,6},{4,36},{6,10},{8,40},{10,14},{12,44},{14,2},{16,48},{... | collective-permute-start | bytes 4718600 | tf_op jit(solution)/shard_map/ppermute | solution.py:60
  113.9 26.6 %collective-permute-start.11 = (f32[1024,768]{1,0:T(8,128)S(1)}, f32[1024,768]{1,0:T(8,128)S(1)}, u32[]{:S(2)}, u32[]{:S(2)}) collective-permute-start(f32[1024,768]{1,0:T(8,128)S(1)} %collective-permute-done.6.refs_1_), channel_id=1, source_target_pairs={{0,2},{2,0},{4,6},{6,4},{8,10},{10,8},{12,14},{14,12},{16,18},{18,... | collective-permute-start | bytes 9437192 | tf_op jit(solution)/shard_map/ppermute | solution.py:60
  116.9 26.4 %collective-permute-start.12 = (f32[1024,768]{1,0:T(8,128)}, f32[1024,768]{1,0:T(8,128)}, u32[]{:S(2)}, u32[]{:S(2)}) collective-permute-start(f32[1024,768]{1,0:T(8,128)} %collective-permute-done.7.refs_2_), channel_id=1, source_target_pairs={{0,2},{2,0},{4,6},{6,4},{8,10},{10,8},{12,14},{14,12},{16,18},{18,... | collective-permute-start | bytes 9437192 | tf_op jit(solution)/shard_map/ppermute | solution.py:60
  131.8 8.6 %copy-start.2 = (f32[512,768]{1,0:T(8,128)}, f32[512,768]{1,0:T(8,128)S(1)}, u32[]{:S(2)}) copy-start(f32[512,768]{1,0:T(8,128)S(1)} %collective-permute-done.9.refs_4_) | copy-start | bytes 4718596
  131.8 6.4 %collective-permute-start.14 = (f32[512,768]{1,0:T(8,128)S(1)}, f32[512,768]{1,0:T(8,128)S(1)}, u32[]{:S(2)}, u32[]{:S(2)}) collective-permute-start(f32[512,768]{1,0:T(8,128)S(1)} %collective-permute-done.9.refs_4_), channel_id=1, source_target_pairs={{0,2},{2,0},{4,6},{6,4},{8,10},{10,8},{12,14},{14,12},{16,18},{18,... | collective-permute-start | bytes 4718600 | tf_op jit(solution)/shard_map/ppermute | solution.py:60
  135.1 5.3 %copy-start.4 = (f32[512,768]{1,0:T(8,128)}, f32[512,768]{1,0:T(8,128)S(1)}, u32[]{:S(2)}) copy-start(f32[512,768]{1,0:T(8,128)S(1)} %collective-permute-done.8.refs_3_) | copy-start | bytes 4718596
  135.1 5.3 %collective-permute-start.13 = (f32[512,768]{1,0:T(8,128)S(1)}, f32[512,768]{1,0:T(8,128)S(1)}, u32[]{:S(2)}, u32[]{:S(2)}) collective-permute-start(f32[512,768]{1,0:T(8,128)S(1)} %collective-permute-done.8.refs_3_), channel_id=1, source_target_pairs={{0,2},{2,0},{4,6},{6,4},{8,10},{10,8},{12,14},{14,12},{16,18},{18,... | collective-permute-start | bytes 4718600 | tf_op jit(solution)/shard_map/ppermute | solution.py:60
  136.6 3.8 %copy-start.14 = (f32[1024,768]{1,0:T(8,128)}, f32[1024,768]{1,0:T(8,128)S(1)}, u32[]{:S(2)}) copy-start(f32[1024,768]{1,0:T(8,128)S(1)} %collective-permute-done.10.refs_5_) | copy-start | bytes 9437188
  138.2 2.3 copy-start.6
  140.4 1.1 copy-start.8
  141.6 1.7 copy-start.15
  143.3 189.6 %all-to-all-start.1 = ((f32[64,4,8192]{2,1,0:T(4,128)}), f32[64,4,8192]{2,1,0:T(4,128)}, u32[]{:S(2)}, u32[]{:S(2)}) async-start(f32[64,4,8192]{2,1,0:T(4,128)} %pack_runs.3), calls=%async_computation.1 | async-start | bytes 16777216 | tf_op jit(solution)/shard_map/all_to_all | solution.py:437
  149.9 109.4 %all-gather.2.cloned.1.call-start = ((), (), s32[]{:S(2)}) async-start(), calls=%async_computation.2 | async-start | bytes 1769472 | tf_op jit(solution)/shard_map/all_gather | solution.py:447
  151.3 5.1 %copy-start.13 = (f32[64,4,896]{2,1,0:T(4,128)S(1)}, f32[64,4,896]{2,1,0:T(4,128)}, u32[]{:S(2)}) copy-start(f32[64,4,896]{2,1,0:T(4,128)} %copy-done.12) | copy-start | bytes 2752516
  259.3 1.3 copy-start.10
  260.6 1.3 copy-start.11
  303.8 4.4 %copy-start.17 = (f32[256,768]{1,0:T(8,128)S(1)}, f32[256,768]{1,0:T(8,128)}, u32[]{:S(2)}) copy-start(f32[256,768]{1,0:T(8,128)} %copy-done.16) | copy-start | bytes 2359300
  303.8 7.4 %copy-start.9 = (f32[512,768]{1,0:T(8,128)S(1)}, f32[512,768]{1,0:T(8,128)}, u32[]{:S(2)}) copy-start(f32[512,768]{1,0:T(8,128)} %copy-done.8) | copy-start | bytes 4718596
  306.0 5.2 %copy-start.1 = (f32[1024,768]{1,0:T(8,128)S(1)}, f32[1024,768]{1,0:T(8,128)}, u32[]{:S(2)}) copy-start(f32[1024,768]{1,0:T(8,128)} %copy-done) | copy-start | bytes 9437188
  306.0 5.2 %copy-start.3 = (f32[512,768]{1,0:T(8,128)S(1)}, f32[512,768]{1,0:T(8,128)}, u32[]{:S(2)}) copy-start(f32[512,768]{1,0:T(8,128)} %copy-done.2) | copy-start | bytes 4718596
  306.0 5.2 %copy-start.5 = (f32[512,768]{1,0:T(8,128)S(1)}, f32[512,768]{1,0:T(8,128)}, u32[]{:S(2)}) copy-start(f32[512,768]{1,0:T(8,128)} %copy-done.4) | copy-start | bytes 4718596
  306.0 5.2 %copy-start.7 = (f32[512,768]{1,0:T(8,128)S(1)}, f32[512,768]{1,0:T(8,128)}, u32[]{:S(2)}) copy-start(f32[512,768]{1,0:T(8,128)} %copy-done.6) | copy-start | bytes 4718596
Sparse Core Ops, SparseCore 0:
  156.5 102.7 all-gather.1

commit v4 on v2

--- a/solution.py
+++ b/solution.py
@@ -2,6 +2,7 @@
 
 import jax
 import jax.numpy as jnp
+import numpy as np
 from jax import lax
 from jax.experimental import pallas as pl
 from jax.experimental.pallas import tpu as pltpu
@@ -70,25 +71,28 @@
     return [value, before, after, far_first, far_second], beside
 
 
-def gather_rows(mine, beside):
-    value = jnp.concatenate([mine, move(mine, "y")], axis=0)
+def gather_rows(value, runs):
     value = jnp.concatenate(ring(value, "first")[0], axis=0)
-    pieces, beside = ring(value, "second", beside)
-    return pieces + [move(p, "core") for p in pieces], beside
-
-
-def block_order(row):
-    z, y, x, k = row // 16, (row // 8) % 2, (row // 2) % 4, row % 2
+    pieces, runs = ring(value, "second", runs)
+    return pieces + [move(p, "core") for p in pieces], runs
+
+
+def block_table():
     first = ((0, 0), (0, 1), (-1, 0), (-1, 1), (1, 0), (1, 1), (2, 0), (2, 1))
-    order = []
-    for swapped in (0, 1):
-        core = k ^ swapped
-        for second, part in ((0, first), (-1, first), (1, first), (2, first[:4]), (2, first[4:])):
-            for along, flip in part:
-                xs = jnp.where(core == 0, x + along, x + second) % 4
-                zs = jnp.where(core == 0, z + second, z + along) % 4
-                order.append(row_id(zs, y ^ flip, xs, core))
-    return jnp.stack(order).astype(jnp.int32)
+    table = np.zeros((N_ROW, BW), np.int32)
+    for row in range(N_ROW):
+        z, y, x, k = row // 16, (row // 8) % 2, (row // 2) % 4, row % 2
+        order = []
+        for core in (k, 1 - k):
+            for second, part in (
+                (0, first), (-1, first), (1, first), (2, first[:4]), (2, first[4:])
+            ):
+                for along, flip in part:
+                    xs, zs = (along, second) if core == 0 else (second, along)
+                    order.append(row_id((z + zs) % 4, y ^ flip, (x + xs) % 4, core))
+        table[row, :N_ROW] = order
+        table[row, N_ROW : N_ROW + NP] = [order.index(q) for q in range(NP)]
+    return table
 
 
 def pack_kernel(slot_ref, rows_ref, out_ref):
@@ -96,15 +100,15 @@
         out_ref[slot_ref[g]] = rows_ref[g * CAP : (g + 1) * CAP, :]
 
 
-def pack_runs(slots, rows, tile):
-    height, width = rows.shape
+def pack_runs(slots, rows, start, width, tile):
+    height = rows.shape[0]
     return pl.pallas_call(
         pack_kernel,
         out_shape=jax.ShapeDtypeStruct((N_ROW, CAP, width), rows.dtype),
         grid_spec=pltpu.PrefetchScalarGridSpec(
             num_scalar_prefetch=1,
             grid=(width // tile,),
-            in_specs=[pl.BlockSpec((height, tile), lambda i, s: (0, i))],
+            in_specs=[pl.BlockSpec((height, tile), lambda i, s: (0, i + start // tile))],
             out_specs=pl.BlockSpec((N_ROW, CAP, tile), lambda i, s: (0, 0, i)),
         ),
         cost_estimate=pl.CostEstimate(
@@ -115,7 +119,7 @@
 
 
 def head_kernel(place_ref, col_ref, *refs):
-    pieces, (rows_ref, square_ref), (sem,) = refs[:10], refs[10:12], refs[12:]
+    pieces, (rows_ref, square_ref), (sems,) = refs[:10], refs[10:12], refs[12:]
     for q in range(NP):
         at = place_ref[q]
         for p in range(10):
@@ -125,11 +129,14 @@
             @pl.when((at >= low) & (at < high))
             def _():
                 start = pl.multiple_of((at - low) * BW, BW)
-                copy = pltpu.make_async_copy(
-                    pieces[p].at[pl.ds(start, BW)], rows_ref.at[pl.ds(q * BW, BW)], sem
-                )
-                copy.start()
-                copy.wait()
+                pltpu.make_async_copy(
+                    pieces[p].at[pl.ds(start, BW)], rows_ref.at[pl.ds(q * BW, BW)], sems.at[q]
+                ).start()
+
+    for q in range(NP):
+        pltpu.make_async_copy(
+            pieces[0].at[pl.ds(0, BW)], rows_ref.at[pl.ds(q * BW, BW)], sems.at[q]
+        ).wait()
 
     for c in range(2):
 
@@ -151,7 +158,7 @@
         in_specs=[pl.BlockSpec(memory_space=pltpu.SMEM)] * 2
         + [pl.BlockSpec(memory_space=pl.ANY)] * 10,
         out_specs=(pl.BlockSpec(memory_space=pltpu.VMEM),) * 2,
-        scratch_shapes=[pltpu.SemaphoreType.DMA],
+        scratch_shapes=[pltpu.SemaphoreType.DMA((NP,))],
         cost_estimate=pl.CostEstimate(flops=0, bytes_accessed=4 * 10**6, transcendentals=0),
         name="head_rows",
     )(place, col, *pieces)
@@ -359,19 +366,20 @@
 
 
 def place_kernel(tile, place_ref, arrived_ref, update_ref, out_ref, rows):
-    for b in range(N_ROW):
+    rows[: NP * CAP, :] = jnp.zeros((NP * CAP, tile), jnp.float32)
+    for b in range(NP, N_ROW):
         rows[b * CAP : (b + 1) * CAP, :] = arrived_ref[b]
+    value = rows[...] - update_ref[...]
+    high = value.astype(jnp.bfloat16)
+    low = (value - high.astype(jnp.float32)).astype(jnp.bfloat16)
     place = place_ref[...]
-    value = rows[...]
-    total = None
-    for part in range(3):
-        piece = value.astype(jnp.bfloat16)
-        term = jnp.dot(place, piece, preferred_element_type=jnp.float32)
-        total = term if total is None else total + term
-        if part < 2:
-            value = value - piece.astype(jnp.float32)
-    column = pl.program_id(0) * tile + lax.broadcasted_iota(jnp.int32, (1, tile), 1)
-    out_ref[...] = jnp.where(column >= HEAD, total - update_ref[...], 0.0)
+    out_ref[...] = jnp.dot(place, low, preferred_element_type=jnp.float32) + jnp.dot(
+        place, high, preferred_element_type=jnp.float32
+    )
+
+    @pl.when(pl.program_id(0) == 0)
+    def _():
+        out_ref[:, :HEAD] = jnp.zeros((PW, HEAD), jnp.float32)
 
 
 def place_rows(place, arrived, update, tile=512):
@@ -388,7 +396,7 @@
         out_specs=pl.BlockSpec((PW, tile), lambda i: (0, i)),
         scratch_shapes=[pltpu.VMEM((PW, tile), jnp.float32)],
         cost_estimate=pl.CostEstimate(
-            flops=6 * PW * PW * width, bytes_accessed=12 * PW * width, transcendentals=0
+            flops=4 * PW * PW * width, bytes_accessed=12 * PW * width, transcendentals=0
         ),
         name="place_rows",
     )(place, arrived, update)
@@ -408,47 +416,52 @@
     row = lax.axis_index("row")
     col = lax.axis_index("col")
     swap = [(0, 1), (1, 0)]
-    own = front_matrix[:, :HEAD]
-    panel = weave(own, lax.ppermute(own, "col", swap), col)
+
+    def send(runs):
+        return lax.all_to_all(runs, "row", split_axis=0, concat_axis=0, tiled=True)
+
+    def half_rows(half):
+        return lax.dynamic_slice(front_matrix, (half * BW, 0), (BW, HEAD))
+
+    own, others = half_rows(col), half_rows(1 - col)
+    own_beside = lax.ppermute(others, "col", swap)
+    own_across = move(own, "y")
+    mine = weave(own, own_beside, col)
+    across = weave(own_across, move(own_beside, "y"), col)
+    others_beside = lax.ppermute(own, "col", swap)
 
     targets = row_map[0].reshape(N_ROW, CAP)[:, 0] // PW
     within = (row_map[0] % PW).astype(jnp.float32)
+    outgoing = pack_runs(targets, front_matrix, 0, width, 512)
+    pieces, outgoing = gather_rows(jnp.concatenate([mine, across], axis=0), outgoing)
+
+    theirs = weave(others, others_beside, col)
+    panel = jnp.concatenate(
+        [jnp.where(col == 0, mine, theirs), jnp.where(col == 0, theirs, mine)], axis=0
+    )
     small = jnp.concatenate([panel, jnp.broadcast_to(within[:, None], (PW, BW))], axis=1)
-    small = pack_runs(targets, small, small.shape[1])
-    small = lax.all_to_all(small, "row", split_axis=0, concat_axis=0, tiled=True)
-    outgoing = pack_runs(targets, front_matrix, 512)
-
-    mine = lax.dynamic_slice_in_dim(panel, col * BW, BW, 0)
-    pieces, small = gather_rows(mine, small)
-    order = block_order(row)
-    places = jnp.sum(
-        jnp.where(
-            order[None, :] == jnp.arange(NP, dtype=jnp.int32)[:, None],
-            jnp.arange(N_ROW, dtype=jnp.int32)[None, :],
-            0,
-        ),
-        axis=1,
-    )
+    small = pack_runs(targets, small, 0, PANEL + BW, PANEL + BW)
+
+    table = lax.dynamic_slice_in_dim(jnp.asarray(block_table()), row, 1, 0)[0]
+    order, places = table[:N_ROW], table[N_ROW : N_ROW + 8]
     cols = col.reshape(1).astype(jnp.int32)
     rows, square = head_rows(places, cols, pieces)
-    other_square = lax.ppermute(square, "col", swap)
-    outgoing, other_square = lax.optimization_barrier((outgoing, other_square))
-    arrived = lax.all_to_all(outgoing, "row", split_axis=0, concat_axis=0, tiled=True)
-
-    w = inverse_factor(cols, rows, other_square)
+    square, small = lax.optimization_barrier((square, small))
+    square = lax.ppermute(square, "col", swap)
+    small = send(small)
+    outgoing, square, small = lax.optimization_barrier((outgoing, square, small))
+    arrived = send(outgoing)
+
+    w = inverse_factor(cols, rows, square)
     small = small.reshape(PW, PANEL + BW)
-    both = dot_t(jnp.concatenate([panel, small[:, :PANEL]], axis=0), w)
+    lower = dot_t(small[:, :PANEL], w)
+    update = update_of(order, dot_n(lower, w), pieces, width)
     panel_ids = lax.broadcasted_iota(jnp.int32, (1, PANEL), 1) // PW
-    factors = jnp.where(row >= panel_ids, both[:PW], 0.0)
-
+    factors = jnp.where(row >= panel_ids, dot_t(panel, w), 0.0)
     slots = jnp.arange(PW, dtype=jnp.int32)
     goes = small[:, PANEL].astype(jnp.int32)
     place = (goes[None, :] == slots[:, None]) & (slots[None, :] >= NP * CAP)
-    place = place.astype(jnp.float32)
-    x = dot_n(dot_n(place, both[PW:]), w)
-    update = update_of(order, x, pieces, width)
-    parent = place_rows(place.astype(jnp.bfloat16), arrived, update)
-    return factors, parent
+    return factors, place_rows(place.astype(jnp.bfloat16), arrived, update)
 
 
 def solution(mesh):

time: 287 us -> 303 us (1.056)
  starting transfers between devices: 45.7 us -> 63.5 us
  waiting for transfers between devices: 109 us -> 98.6 us
  local copies, waits for them, and re-layouts: 16.1 us -> 23 us
  other arithmetic: 4.62 us -> 7.84 us
    all_to_all x2, waiting for transfers between devices: 61.6 us -> 28.9 us  [send(): return lax.all_to_all(runs, 'row', split_axis=0, concat_axis=0, tiled=True)]
    ppermute x14 -> x15, starting transfers between devices: 18.6 us -> 40.3 us  [move(): return lax.ppermute(value, 'row', pairs_of(kind, step))]
    ppermute x2 -> x3, waiting for transfers between devices: 9.25 us -> 30.1 us  [the longest x1 22.7 us: local(): square = lax.ppermute(square, 'col', swap)]
    all_to_all x2, starting transfers between devices: 20.3 us -> 13.4 us  [send(): return lax.all_to_all(runs, 'row', split_axis=0, concat_axis=0, tiled=True)]
    ppermute x2 -> x3, starting transfers between devices: 6.81 us -> 9.82 us  [the longest x1 3.82 us: local(): others_beside = lax.ppermute(own, 'col', swap)]
    unnamed x24 -> x46, local copies, waits for them, and re-layouts: 8.93 us -> 10.6 us
    ppermute x14 -> x15, waiting for transfers between devices: 38 us -> 39.6 us  [move(): return lax.ppermute(value, 'row', pairs_of(kind, step))]
  transfers between devices with their start and end apart: 18 -> 20, of which waited for: 10 -> 11; matrix products, arithmetic and copies ran while one was open for 7% -> 10% of each run, Pallas kernels for 28% -> 26%
where the time goes in v4:
time: 303 us; the launch traced here: 299 us
  waiting for transfers between devices  98.6 us (33%)
  Pallas kernels  97.9 us (32%)
  starting transfers between devices  63.5 us (21%)
  local copies, waits for them, and re-layouts  23 us (8%)
  other arithmetic  7.84 us (3%)
  matrix products  7.34 us (2%)
    pallas_call x1, Pallas kernels, inverse_factor(): pl.pallas_call(factor_kernel, out_shape=jax.ShapeDtypeStruct((PANEL, PANE...  41.9 us
    ppermute x15, starting transfers between devices, move(): return lax.ppermute(value, 'row', pairs_of(kind, step))  40.3 us
    ppermute x15, waiting for transfers between devices, move(): return lax.ppermute(value, 'row', pairs_of(kind, step))  39.6 us
    all_to_all x2, waiting for transfers between devices, send(): return lax.all_to_all(runs, 'row', split_axis=0, concat_axis=0, tiled=True)  28.9 us
    ppermute x1, waiting for transfers between devices, local(): square = lax.ppermute(square, 'col', swap)  22.7 us
    pallas_call x1, Pallas kernels, update_of(): pl.pallas_call(update_kernel, out_shape=jax.ShapeDtypeStruct((PW, width),...  20.8 us
    pallas_call x1, Pallas kernels, place_rows(): pl.pallas_call(functools.partial(place_kernel, tile), out_shape=jax.Shape...  16.4 us
    pallas_call x2, Pallas kernels, pack_runs(): pl.pallas_call(pack_kernel, out_shape=jax.ShapeDtypeStruct((N_ROW, CAP, w...  15.5 us
  transfers between devices with their start and end apart: 20, of which 11 were waited for; matrix products, arithmetic and copies ran while one was open for 10% of the time, Pallas kernels for 26%

profile of v4, /device:TPU:1, one launch (start us, length us, event | category | flops | bytes accessed | tf_op | source)
XLA Modules:
  0.0 299.2 jit_solution(4552448676059435192)
XLA Ops:
  0.6 0.9 constant_dynamic-slice_fusion.2
  1.6 3.8 %collective-permute-start.1 = (f32[128,384]{1,0:T(8,128)S(1)}, f32[128,384]{1,0:T(8,128)S(1)}, u32[]{:S(2)}, u32[]{:S(2)}) collective-permute-start(f32[128,384]{1,0:T(8,128)S(1)} %constant_dynamic-slice_fusion.2), channel_id=1, source_target_pairs={{0,1},{1,0},{2,3},{3,2},{4,5},{5,4},{6,7},{7,6},{8,9},{9,8},{10,11... | collective-permute-start | bytes 589832 | tf_op jit(solution)/shard_map/ppermute | solution.py:431
  5.4 4.3 %collective-permute-done.1 = f32[128,384]{1,0:T(8,128)S(1)} collective-permute-done((f32[128,384]{1,0:T(8,128)S(1)}, f32[128,384]{1,0:T(8,128)S(1)}, u32[]{:S(2)}, u32[]{:S(2)}) %collective-permute-start.1) | collective-permute-done | bytes 196640 | tf_op jit(solution)/shard_map/ppermute | solution.py:431
  9.8 1.0 broadcast_select_fusion.4
  10.7 3.0 %collective-permute-start = (f32[128,384]{1,0:T(8,128)S(1)}, f32[128,384]{1,0:T(8,128)S(1)}, u32[]{:S(2)}, u32[]{:S(2)}) collective-permute-start(f32[128,384]{1,0:T(8,128)S(1)} %get-tuple-element.23), channel_id=1, source_target_pairs={{0,1},{1,0},{2,3},{3,2},{4,5},{5,4},{6,7},{7,6},{8,9},{9,8},{10,11... | collective-permute-start | bytes 589832 | tf_op jit(solution)/shard_map/ppermute | solution.py:427
  14.1 3.1 %collective-permute-done = f32[128,384]{1,0:T(8,128)S(1)} collective-permute-done((f32[128,384]{1,0:T(8,128)S(1)}, f32[128,384]{1,0:T(8,128)S(1)}, u32[]{:S(2)}, u32[]{:S(2)}) %collective-permute-start) | collective-permute-done | bytes 196640 | tf_op jit(solution)/shard_map/ppermute | solution.py:427
  17.2 1.0 broadcast_select_fusion.6
  18.2 0.6 slice_dynamic-update-slice_fusion.21
  18.9 0.7 slice_dynamic-update-slice_fusion.19
  19.5 0.7 slice_dynamic-update-slice_fusion.24
  20.2 0.6 slice_dynamic-update-slice_fusion.22
  20.9 0.7 slice_dynamic-update-slice_fusion.20
  21.5 1.3 collective-permute-start.3
  22.8 0.7 slice_dynamic-update-slice_fusion.18
  23.5 2.6 collective-permute-done.3
  26.1 0.6 slice_dynamic-update-slice_fusion.9
  26.8 0.7 slice_dynamic-update-slice_fusion.7
  27.5 3.8 %collective-permute-start.5 = (f32[256,768]{1,0:T(8,128)S(1)}, f32[256,768]{1,0:T(8,128)S(1)}, u32[]{:S(2)}, u32[]{:S(2)}) collective-permute-start(f32[256,768]{1,0:T(8,128)S(1)} %pad_maximum_fusion.1), channel_id=1, source_target_pairs={{0,12},{2,98},{4,0},{6,102},{8,4},{10,106},{12,8},{14,110},{16,28}... | collective-permute-start | bytes 2359304 | tf_op jit(solution)/shard_map/ppermute | solution.py:60
  31.3 0.7 slice_dynamic-update-slice_fusion.12
  32.0 0.7 slice_dynamic-update-slice_fusion.10
  32.6 0.7 slice_dynamic-update-slice_fusion.8
  33.3 7.0 %collective-permute-done.5 = f32[256,768]{1,0:T(8,128)S(1)} collective-permute-done((f32[256,768]{1,0:T(8,128)S(1)}, f32[256,768]{1,0:T(8,128)S(1)}, u32[]{:S(2)}, u32[]{:S(2)}) %collective-permute-start.5) | collective-permute-done | bytes 786464 | tf_op jit(solution)/shard_map/ppermute | solution.py:60
  40.3 3.2 %collective-permute-start.7 = (f32[128,768]{1,0:T(8,128)S(1)}, f32[128,768]{1,0:T(8,128)S(1)}, u32[]{:S(2)}, u32[]{:S(2)}) collective-permute-start(f32[128,768]{1,0:T(8,128)S(1)} %slice.135), channel_id=1, source_target_pairs={{0,12},{2,98},{4,0},{6,102},{8,4},{10,106},{12,8},{14,110},{16,28}... | collective-permute-start | bytes 1179656 | tf_op jit(solution)/shard_map/ppermute | solution.py:60
  43.8 0.6 slice_dynamic-update-slice_fusion.6
  44.4 0.9 constant_dynamic-update-slice_fusion.3
  45.3 0.9 constant_dynamic-update-slice_fusion.2
  46.3 5.3 %collective-permute-done.6 = f32[128,768]{1,0:T(8,128)S(1)} collective-permute-done((f32[128,768]{1,0:T(8,128)S(1)}, f32[128,768]{1,0:T(8,128)S(1)}, u32[]{:S(2)}, u32[]{:S(2)}) %collective-permute-start.6) | collective-permute-done | bytes 393248 | tf_op jit(solution)/shard_map/ppermute | solution.py:60
  51.6 0.8 constant_dynamic-update-slice_fusion.1
  52.4 0.8 constant_dynamic-update-slice_fusion.refs_0_
  53.1 2.9 collective-permute-start.9
  56.5 0.7 reduce.5
  57.2 0.7 reshape_squeeze.3
  57.9 0.9 slice_reduce_fusion
  59.3 12.7 %pack_runs.2 = f32[64,4,8192]{2,1,0:T(4,128)} custom-call(s32[64]{0:T(128)} %and_select_fusion.1.slot_ref, f32[256,8192]{1,0:T(8,128)} %rows_ref.1), custom_call_target="tpu_custom_call" | custom-call | bytes 16777216 | tf_op jit(solution)/shard_map/pack_runs/pallas_call | solution.py:105
  72.0 18.5 %collective-permute-done.9.refs_2_ = f32[1024,768]{1,0:T(8,128)} collective-permute-done((f32[1024,768]{1,0:T(8,128)}, f32[1024,768]{1,0:T(8,128)}, u32[]{:S(2)}, u32[]{:S(2)}) %collective-permute-start.9) | collective-permute-done | bytes 3145760 | tf_op jit(solution)/shard_map/ppermute | solution.py:60
  90.6 3.3 %collective-permute-done.8.refs_1_ = f32[1024,768]{1,0:T(8,128)S(1)} collective-permute-done((f32[1024,768]{1,0:T(8,128)}, f32[1024,768]{1,0:T(8,128)S(1)}, u32[]{:S(2)}, u32[]{:S(2)}) %collective-permute-start.8) | collective-permute-done | bytes 3145760 | tf_op jit(solution)/shard_map/ppermute | solution.py:60
  93.9 3.8 %slice.111 = f32[512,768]{1,0:T(8,128)} slice(f32[1024,768]{1,0:T(8,128)} %collective-permute-done.9.refs_2_), slice={[512:1024], [0:768]} | slice | bytes 3145728 | tf_op jit(solution)/shard_map/slice | solution.py:70
  97.7 1.3 slice.110
  99.0 1.5 collective-permute-start.10
  100.5 11.6 %collective-permute-start.12 = (f32[1024,768]{1,0:T(8,128)}, f32[1024,768]{1,0:T(8,128)}, u32[]{:S(2)}, u32[]{:S(2)}) collective-permute-start(f32[1024,768]{1,0:T(8,128)} %constant_dynamic-update-slice_fusion.refs_0_), channel_id=1, source_target_pairs={{0,2},{2,0},{4,6},{6,4},{8,10},{10,8},{12,14},{14,12},{16,18},{18,... | collective-permute-start | bytes 9437192 | tf_op jit(solution)/shard_map/ppermute | solution.py:60
  112.6 0.7 constant_dynamic-slice_fusion
  113.9 0.9 broadcast_select_fusion.5
  114.8 2.7 collective-permute-done.11.refs_4_
  117.5 11.9 %collective-permute-start.16 = (f32[512,768]{1,0:T(8,128)}, f32[512,768]{1,0:T(8,128)}, u32[]{:S(2)}, u32[]{:S(2)}) collective-permute-start(f32[512,768]{1,0:T(8,128)} %collective-permute-done.11.refs_4_), channel_id=1, source_target_pairs={{0,2},{2,0},{4,6},{6,4},{8,10},{10,8},{12,14},{14,12},{16,18},{18,... | collective-permute-start | bytes 4718600 | tf_op jit(solution)/shard_map/ppermute | solution.py:60
  129.5 3.2 %collective-permute-start.15 = (f32[512,768]{1,0:T(8,128)}, f32[512,768]{1,0:T(8,128)}, u32[]{:S(2)}, u32[]{:S(2)}) collective-permute-start(f32[512,768]{1,0:T(8,128)} %collective-permute-done.10.refs_3_), channel_id=1, source_target_pairs={{0,2},{2,0},{4,6},{6,4},{8,10},{10,8},{12,14},{14,12},{16,18},{18,... | collective-permute-start | bytes 4718600 | tf_op jit(solution)/shard_map/ppermute | solution.py:60
  132.7 1.1 broadcast_select_fusion.1
  133.9 0.6 copy-done.4
  134.5 1.0 pad_maximum_fusion.rows_ref
  135.5 2.9 pack_runs.3
  138.4 3.2 %head_rows.1 = (f32[384,768]{1,0:T(8,128)}, f32[384,384]{1,0:T(8,128)}) custom-call(s32[8]{0:T(128)} %slice_bitcast_fusion.1.place_ref, s32[1]{0:T(128)} %bitcast.col_ref, f32[1024,768]{1,0:T(8,128)} %constant_dynamic-update-slice_fusion.refs_0_, f32[1024,768]{1,0:T(8,128)} %copy-done, f32[1024,768]{1,0:T(8,128)} %collective-permute-done.9.refs_2_, ...), custom_call_target="tpu_custom_call" | custom-call | bytes 4000000 | tf_op jit(solution)/shard_map/head_rows/pallas_call | solution.py:152
  141.6 4.2 %all-to-all-start = ((f32[64,4,896]{2,1,0:T(4,128)}), f32[64,4,896]{2,1,0:T(4,128)S(1)}, u32[]{:S(2)}, u32[]{:S(2)}) async-start(f32[64,4,896]{2,1,0:T(4,128)} %pack_runs.3), calls=%async_computation | async-start | bytes 1835008 | tf_op jit(solution)/shard_map/all_to_all | solution.py:421
  145.9 3.0 collective-permute-start.17
  148.8 22.7 %collective-permute-done.17.square_ref = f32[384,384]{1,0:T(8,128)S(1)} collective-permute-done((f32[384,384]{1,0:T(8,128)}, f32[384,384]{1,0:T(8,128)S(1)}, u32[]{:S(2)}, u32[]{:S(2)}) %collective-permute-start.17) | collective-permute-done | bytes 589856 | tf_op jit(solution)/shard_map/ppermute | solution.py:450
  171.6 9.2 %all-to-all-start.1 = ((f32[64,4,8192]{2,1,0:T(4,128)}), f32[64,4,8192]{2,1,0:T(4,128)}, u32[]{:S(2)}, u32[]{:S(2)}) async-start(f32[64,4,8192]{2,1,0:T(4,128)} %pack_runs.2), calls=%async_computation.1 | async-start | bytes 16777216 | tf_op jit(solution)/shard_map/all_to_all | solution.py:421
  180.8 1.3 reshape.85
  182.1 0.9 slice_convert_fusion
  183.1 0.7 fusion.6.place_ref
  183.8 41.9 %inverse_factor.1 = f32[768,768]{1,0:T(8,128)S(1)} custom-call(s32[1]{0:T(128)} %bitcast.col_ref, f32[384,768]{1,0:T(8,128)S(1)} %copy-done.2, f32[384,384]{1,0:T(8,128)S(1)} %collective-permute-done.17.square_ref), custom_call_target="tpu_custom_call" | custom-call | flops 4000000000 | bytes 5000000 | tf_op jit(solution)/shard_map/inverse_factor/pallas_call | solution.py:263
  225.7 3.0 %convolution_select_fusion = f32[256,768]{1,0:T(8,128)} fusion(f32[768,768]{1,0:T(8,128)S(1)} %inverse_factor.1, f32[128,768]{1,0:T(8,128)S(1)} %copy-done.5, f32[128,768]{1,0:T(8,128)S(1)} %get-tuple-element.24, pred[768]{0:T(1024)(128)(4,1)S(1)} %fusion.7), kind=kOutput, calls=%fused_computation | convolution fusion | flops 1812332544 | bytes 3932928 | tf_op jit(solution)/shard_map/dot_general | solution.py:26
  228.8 2.2 fusion
  230.9 2.2 fusion.14.x_ref
  233.1 20.8 %update_of.1.update_ref = f32[256,8192]{1,0:T(8,128)} custom-call(s32[64]{0:T(128)S(1)} %slice_bitcast_fusion.order_ref, f32[256,768]{1,0:T(8,128)S(1)} %fusion.14.x_ref, f32[1024,768]{1,0:T(8,128)} %constant_dynamic-update-slice_fusion.refs_0_, f32[1024,768]{1,0:T(8,128)S(1)} %copy-done.1, f32[1024,768]{1,0:T(8,128)} %collective-permute-done.9.refs_2_, ...), custom_call_target="tpu_custom_call" | custom-call | flops 9663676416 | bytes 34000000 | tf_op jit(solution)/shard_map/update_of/pallas_call | solution.py:346
  254.0 28.9 %all-to-all-done.1.arrived_ref = f32[64,4,8192]{2,1,0:T(4,128)} async-done(((f32[64,4,8192]{2,1,0:T(4,128)}), f32[64,4,8192]{2,1,0:T(4,128)}, u32[]{:S(2)}, u32[]{:S(2)}) %all-to-all-start.1) | async-done | bytes 8388640 | tf_op jit(solution)/shard_map/all_to_all | solution.py:421
  282.8 16.4 %place_rows.1 = f32[256,8192]{1,0:T(8,128)} custom-call(bf16[256,256]{1,0:T(8,128)(2,1)} %fusion.6.place_ref, f32[64,4,8192]{2,1,0:T(4,128)} %all-to-all-done.1.arrived_ref, f32[256,8192]{1,0:T(8,128)} %update_of.1.update_ref), custom_call_target="tpu_custom_call" | custom-call | flops 2147483648 | bytes 25165824 | tf_op jit(solution)/shard_map/place_rows/pallas_call | solution.py:387
  (61 shorter events, 3.3 us)
Async XLA Ops:
  1.6 8.2 %collective-permute-start.1 = (f32[128,384]{1,0:T(8,128)S(1)}, f32[128,384]{1,0:T(8,128)S(1)}, u32[]{:S(2)}, u32[]{:S(2)}) collective-permute-start(f32[128,384]{1,0:T(8,128)S(1)} %constant_dynamic-slice_fusion.2), channel_id=1, source_target_pairs={{0,1},{1,0},{2,3},{3,2},{4,5},{5,4},{6,7},{7,6},{8,9},{9,8},{10,11... | collective-permute-start | bytes 589832 | tf_op jit(solution)/shard_map/ppermute | solution.py:431
  10.7 3.4 %copy-start.7 = (f32[128,384]{1,0:T(8,128)}, f32[128,384]{1,0:T(8,128)S(1)}, u32[]{:S(2)}) copy-start(f32[128,384]{1,0:T(8,128)S(1)} %get-tuple-element.23) | copy-start | bytes 589828
  10.7 6.5 %collective-permute-start = (f32[128,384]{1,0:T(8,128)S(1)}, f32[128,384]{1,0:T(8,128)S(1)}, u32[]{:S(2)}, u32[]{:S(2)}) collective-permute-start(f32[128,384]{1,0:T(8,128)S(1)} %get-tuple-element.23), channel_id=1, source_target_pairs={{0,1},{1,0},{2,3},{3,2},{4,5},{5,4},{6,7},{7,6},{8,9},{9,8},{10,11... | collective-permute-start | bytes 589832 | tf_op jit(solution)/shard_map/ppermute | solution.py:427
  13.7 9.7 %collective-permute-start.2 = (f32[128,384]{1,0:T(8,128)S(1)}, f32[128,384]{1,0:T(8,128)S(1)}, u32[]{:S(2)}, u32[]{:S(2)}) collective-permute-start(f32[128,384]{1,0:T(8,128)S(1)} %constant_dynamic-slice_fusion.2), channel_id=1, source_target_pairs={{0,16},{2,18},{4,20},{6,22},{8,24},{10,26},{12,28},{14,30},{16,0},... | collective-permute-start | bytes 589832 | tf_op jit(solution)/shard_map/ppermute | solution.py:60
  19.5 25.8 %copy-start.6 = (f32[128,768]{1,0:T(8,128)}, f32[128,768]{1,0:T(8,128)S(1)}, u32[]{:S(2)}) copy-start(f32[128,768]{1,0:T(8,128)S(1)} %get-tuple-element.30) | copy-start | bytes 1179652
  21.5 4.5 %collective-permute-start.3 = (f32[128,384]{1,0:T(8,128)S(1)}, f32[128,384]{1,0:T(8,128)S(1)}, u32[]{:S(2)}, u32[]{:S(2)}) collective-permute-start(f32[128,384]{1,0:T(8,128)S(1)} %collective-permute-done), channel_id=1, source_target_pairs={{0,16},{2,18},{4,20},{6,22},{8,24},{10,26},{12,28},{14,30},{16,0},... | collective-permute-start | bytes 589832 | tf_op jit(solution)/shard_map/ppermute | solution.py:60
  27.5 12.7 %collective-permute-start.5 = (f32[256,768]{1,0:T(8,128)S(1)}, f32[256,768]{1,0:T(8,128)S(1)}, u32[]{:S(2)}, u32[]{:S(2)}) collective-permute-start(f32[256,768]{1,0:T(8,128)S(1)} %pad_maximum_fusion.1), channel_id=1, source_target_pairs={{0,12},{2,98},{4,0},{6,102},{8,4},{10,106},{12,8},{14,110},{16,28}... | collective-permute-start | bytes 2359304 | tf_op jit(solution)/shard_map/ppermute | solution.py:60
  31.3 12.3 %collective-permute-start.4 = (f32[256,768]{1,0:T(8,128)S(1)}, f32[256,768]{1,0:T(8,128)S(1)}, u32[]{:S(2)}, u32[]{:S(2)}) collective-permute-start(f32[256,768]{1,0:T(8,128)S(1)} %pad_maximum_fusion.1), channel_id=1, source_target_pairs={{0,4},{2,34},{4,8},{6,38},{8,12},{10,42},{12,0},{14,46},{16,20},{1... | collective-permute-start | bytes 2359304 | tf_op jit(solution)/shard_map/ppermute | solution.py:60
  33.3 23.3 %copy-start.8 = (s32[1,256]{1,0:T(1,128)S(1)}, s32[1,256]{1,0:T(1,128)}, u32[]{:S(2)}) copy-start(s32[1,256]{1,0:T(1,128)} %param.4) | copy-start | bytes 3076
  40.3 12.1 %collective-permute-start.7 = (f32[128,768]{1,0:T(8,128)S(1)}, f32[128,768]{1,0:T(8,128)S(1)}, u32[]{:S(2)}, u32[]{:S(2)}) collective-permute-start(f32[128,768]{1,0:T(8,128)S(1)} %slice.135), channel_id=1, source_target_pairs={{0,12},{2,98},{4,0},{6,102},{8,4},{10,106},{12,8},{14,110},{16,28}... | collective-permute-start | bytes 1179656 | tf_op jit(solution)/shard_map/ppermute | solution.py:60
  43.7 7.9 %collective-permute-start.6 = (f32[128,768]{1,0:T(8,128)S(1)}, f32[128,768]{1,0:T(8,128)S(1)}, u32[]{:S(2)}, u32[]{:S(2)}) collective-permute-start(f32[128,768]{1,0:T(8,128)S(1)} %slice.134), channel_id=1, source_target_pairs={{0,4},{2,34},{4,8},{6,38},{8,12},{10,42},{12,0},{14,46},{16,20},{1... | collective-permute-start | bytes 1179656 | tf_op jit(solution)/shard_map/ppermute | solution.py:60
  53.1 37.4 %collective-permute-start.9 = (f32[1024,768]{1,0:T(8,128)}, f32[1024,768]{1,0:T(8,128)}, u32[]{:S(2)}, u32[]{:S(2)}) collective-permute-start(f32[1024,768]{1,0:T(8,128)} %constant_dynamic-update-slice_fusion.refs_0_), channel_id=1, source_target_pairs={{0,96},{2,14},{4,100},{6,2},{8,104},{10,6},{12,108},{14,10},{16,11... | collective-permute-start | bytes 9437192 | tf_op jit(solution)/shard_map/ppermute | solution.py:60
  56.0 37.8 %collective-permute-start.8 = (f32[1024,768]{1,0:T(8,128)}, f32[1024,768]{1,0:T(8,128)S(1)}, u32[]{:S(2)}, u32[]{:S(2)}) collective-permute-start(f32[1024,768]{1,0:T(8,128)} %constant_dynamic-update-slice_fusion.refs_0_), channel_id=1, source_target_pairs={{0,32},{2,6},{4,36},{6,10},{8,40},{10,14},{12,44},{14,2},{16,48},{... | collective-permute-start | bytes 9437192 | tf_op jit(solution)/shard_map/ppermute | solution.py:60
  93.9 18.2 %copy-start = (f32[1024,768]{1,0:T(8,128)}, f32[1024,768]{1,0:T(8,128)S(1)}, u32[]{:S(2)}) copy-start(f32[1024,768]{1,0:T(8,128)S(1)} %collective-permute-done.8.refs_1_) | copy-start | bytes 9437188
  97.7 19.9 %collective-permute-start.11 = (f32[512,768]{1,0:T(8,128)}, f32[512,768]{1,0:T(8,128)}, u32[]{:S(2)}, u32[]{:S(2)}) collective-permute-start(f32[512,768]{1,0:T(8,128)} %slice.111), channel_id=1, source_target_pairs={{0,96},{2,14},{4,100},{6,2},{8,104},{10,6},{12,108},{14,10},{16,11... | collective-permute-start | bytes 4718600 | tf_op jit(solution)/shard_map/ppermute | solution.py:60
  99.0 30.5 %collective-permute-start.10 = (f32[512,768]{1,0:T(8,128)}, f32[512,768]{1,0:T(8,128)}, u32[]{:S(2)}, u32[]{:S(2)}) collective-permute-start(f32[512,768]{1,0:T(8,128)} %slice.110), channel_id=1, source_target_pairs={{0,32},{2,6},{4,36},{6,10},{8,40},{10,14},{12,44},{14,2},{16,48},{... | collective-permute-start | bytes 4718600 | tf_op jit(solution)/shard_map/ppermute | solution.py:60
  100.5 37.9 %collective-permute-start.12 = (f32[1024,768]{1,0:T(8,128)}, f32[1024,768]{1,0:T(8,128)}, u32[]{:S(2)}, u32[]{:S(2)}) collective-permute-start(f32[1024,768]{1,0:T(8,128)} %constant_dynamic-update-slice_fusion.refs_0_), channel_id=1, source_target_pairs={{0,2},{2,0},{4,6},{6,4},{8,10},{10,8},{12,14},{14,12},{16,18},{18,... | collective-permute-start | bytes 9437192 | tf_op jit(solution)/shard_map/ppermute | solution.py:60
  112.1 26.3 %collective-permute-start.13 = (f32[1024,768]{1,0:T(8,128)S(1)}, f32[1024,768]{1,0:T(8,128)}, u32[]{:S(2)}, u32[]{:S(2)}) collective-permute-start(f32[1024,768]{1,0:T(8,128)S(1)} %collective-permute-done.8.refs_1_), channel_id=1, source_target_pairs={{0,2},{2,0},{4,6},{6,4},{8,10},{10,8},{12,14},{14,12},{16,18},{18,... | collective-permute-start | bytes 9437192 | tf_op jit(solution)/shard_map/ppermute | solution.py:60
  112.1 26.3 %collective-permute-start.14 = (f32[1024,768]{1,0:T(8,128)}, f32[1024,768]{1,0:T(8,128)}, u32[]{:S(2)}, u32[]{:S(2)}) collective-permute-start(f32[1024,768]{1,0:T(8,128)} %collective-permute-done.9.refs_2_), channel_id=1, source_target_pairs={{0,2},{2,0},{4,6},{6,4},{8,10},{10,8},{12,14},{14,12},{16,18},{18,... | collective-permute-start | bytes 9437192 | tf_op jit(solution)/shard_map/ppermute | solution.py:60
  117.5 20.8 %collective-permute-start.16 = (f32[512,768]{1,0:T(8,128)}, f32[512,768]{1,0:T(8,128)}, u32[]{:S(2)}, u32[]{:S(2)}) collective-permute-start(f32[512,768]{1,0:T(8,128)} %collective-permute-done.11.refs_4_), channel_id=1, source_target_pairs={{0,2},{2,0},{4,6},{6,4},{8,10},{10,8},{12,14},{14,12},{16,18},{18,... | collective-permute-start | bytes 4718600 | tf_op jit(solution)/shard_map/ppermute | solution.py:60
  129.5 8.9 %collective-permute-start.15 = (f32[512,768]{1,0:T(8,128)}, f32[512,768]{1,0:T(8,128)}, u32[]{:S(2)}, u32[]{:S(2)}) collective-permute-start(f32[512,768]{1,0:T(8,128)} %collective-permute-done.10.refs_3_), channel_id=1, source_target_pairs={{0,2},{2,0},{4,6},{6,4},{8,10},{10,8},{12,14},{14,12},{16,18},{18,... | collective-permute-start | bytes 4718600 | tf_op jit(solution)/shard_map/ppermute | solution.py:60
  133.8 0.7 copy-start.4
  141.6 30.0 %all-to-all-start = ((f32[64,4,896]{2,1,0:T(4,128)}), f32[64,4,896]{2,1,0:T(4,128)S(1)}, u32[]{:S(2)}, u32[]{:S(2)}) async-start(f32[64,4,896]{2,1,0:T(4,128)} %pack_runs.3), calls=%async_computation | async-start | bytes 1835008 | tf_op jit(solution)/shard_map/all_to_all | solution.py:421
  145.8 37.9 %copy-start.2 = (f32[384,768]{1,0:T(8,128)S(1)}, f32[384,768]{1,0:T(8,128)}, u32[]{:S(2)}) copy-start(f32[384,768]{1,0:T(8,128)} %get-tuple-element.14.rows_ref) | copy-start | bytes 3538948
  145.9 25.7 %collective-permute-start.17 = (f32[384,384]{1,0:T(8,128)}, f32[384,384]{1,0:T(8,128)S(1)}, u32[]{:S(2)}, u32[]{:S(2)}) collective-permute-start(f32[384,384]{1,0:T(8,128)} %get-tuple-element.17), channel_id=1, source_target_pairs={{0,1},{1,0},{2,3},{3,2},{4,5},{5,4},{6,7},{7,6},{8,9},{9,8},{10,11... | collective-permute-start | bytes 1769480 | tf_op jit(solution)/shard_map/ppermute | solution.py:450
  171.6 111.3 %all-to-all-start.1 = ((f32[64,4,8192]{2,1,0:T(4,128)}), f32[64,4,8192]{2,1,0:T(4,128)}, u32[]{:S(2)}, u32[]{:S(2)}) async-start(f32[64,4,8192]{2,1,0:T(4,128)} %pack_runs.2), calls=%async_computation.1 | async-start | bytes 16777216 | tf_op jit(solution)/shard_map/all_to_all | solution.py:421
  183.8 41.9 %copy-start.5 = (f32[128,768]{1,0:T(8,128)S(1)}, f32[128,768]{1,0:T(8,128)}, u32[]{:S(2)}) copy-start(f32[128,768]{1,0:T(8,128)} %copy-done.4) | copy-start | bytes 1179652
  225.7 3.0 %copy-start.3 = (f32[256,896]{1,0:T(8,128)S(1)}, f32[256,896]{1,0:T(8,128)}, u32[]{:S(2)}) copy-start(f32[256,896]{1,0:T(8,128)} %reshape.85) | copy-start | bytes 2752516
  228.8 4.3 %copy-start.1 = (f32[1024,768]{1,0:T(8,128)S(1)}, f32[1024,768]{1,0:T(8,128)}, u32[]{:S(2)}) copy-start(f32[1024,768]{1,0:T(8,128)} %copy-done) | copy-start | bytes 9437188

commit v5 on v4

--- a/solution.py
+++ b/solution.py
@@ -15,9 +15,10 @@
 BW = 128
 PANEL = NP * PW
 HEAD = NP * BW
-GRID = (4, 2, 4, 2)
-PIECE_BLOCKS = (8, 8, 8, 4, 4)
-PIECE_START = (0, 8, 16, 24, 28)
+PIECES = 16
+PIECE = 4
+
+LOWER = tuple((q, p) for q in range(NP) for p in range(q + 1))
 
 full = lax.Precision.HIGHEST
 
@@ -60,36 +61,44 @@
     return lax.ppermute(value, "row", pairs_of(kind, step))
 
 
-def ring(value, kind, beside=None):
-    half = value.shape[0] // 2
-    before = move(value, kind, 1)
-    after = move(value, kind, -1)
+def ring(near, across, kind, beside=None):
+    before_near = move(near, kind, 1)
+    after_across = move(across, kind, -1)
+    before_across = move(across, kind, 1)
+    after_near = move(near, kind, -1)
     if beside is not None:
-        before, after, beside = lax.optimization_barrier((before, after, beside))
-    far_first = move(before[:half], kind, 1)
-    far_second = move(after[half:], kind, -1)
-    return [value, before, after, far_first, far_second], beside
-
-
-def gather_rows(value, runs):
-    value = jnp.concatenate(ring(value, "first")[0], axis=0)
-    pieces, runs = ring(value, "second", runs)
-    return pieces + [move(p, "core") for p in pieces], runs
+        before_near, after_across, beside = lax.optimization_barrier(
+            (before_near, after_across, beside)
+        )
+    far_near = move(before_near, kind, 1)
+    far_across = move(after_across, kind, -1)
+    return (
+        [near, before_near, after_near, far_near],
+        [across, before_across, after_across, far_across],
+        beside,
+    )
+
+
+def gather_rows(mine, small, runs):
+    near, across, small = ring(mine, move(mine, "y"), "first", small)
+    near, across, runs = ring(
+        jnp.concatenate(near, axis=0), jnp.concatenate(across, axis=0), "second", runs
+    )
+    pieces = near + across
+    return pieces + [move(p, "core") for p in pieces], small, runs
 
 
 def block_table():
-    first = ((0, 0), (0, 1), (-1, 0), (-1, 1), (1, 0), (1, 1), (2, 0), (2, 1))
     table = np.zeros((N_ROW, BW), np.int32)
     for row in range(N_ROW):
         z, y, x, k = row // 16, (row // 8) % 2, (row // 2) % 4, row % 2
         order = []
         for core in (k, 1 - k):
-            for second, part in (
-                (0, first), (-1, first), (1, first), (2, first[:4]), (2, first[4:])
-            ):
-                for along, flip in part:
-                    xs, zs = (along, second) if core == 0 else (second, along)
-                    order.append(row_id((z + zs) % 4, y ^ flip, (x + xs) % 4, core))
+            for flip in (0, 1):
+                for second in (0, -1, 1, 2):
+                    for first in (0, -1, 1, 2):
+                        xs, zs = (first, second) if core == 0 else (second, first)
+                        order.append(row_id((z + zs) % 4, y ^ flip, (x + xs) % 4, core))
         table[row, :N_ROW] = order
         table[row, N_ROW : N_ROW + NP] = [order.index(q) for q in range(NP)]
     return table
@@ -119,16 +128,14 @@
 
 
 def head_kernel(place_ref, col_ref, *refs):
-    pieces, (rows_ref, square_ref), (sems,) = refs[:10], refs[10:12], refs[12:]
+    pieces, (rows_ref, lower_ref), (sems,) = refs[:PIECES], refs[PIECES : PIECES + 2], refs[PIECES + 2 :]
     for q in range(NP):
         at = place_ref[q]
-        for p in range(10):
-            low = 32 * (p // 5) + PIECE_START[p % 5]
-            high = low + PIECE_BLOCKS[p % 5]
-
-            @pl.when((at >= low) & (at < high))
+        for p in range(PIECES):
+
+            @pl.when((at >= p * PIECE) & (at < (p + 1) * PIECE))
             def _():
-                start = pl.multiple_of((at - low) * BW, BW)
+                start = pl.multiple_of((at - p * PIECE) * BW, BW)
                 pltpu.make_async_copy(
                     pieces[p].at[pl.ds(start, BW)], rows_ref.at[pl.ds(q * BW, BW)], sems.at[q]
                 ).start()
@@ -142,9 +149,9 @@
 
         @pl.when(col_ref[0] == c)
         def _():
-            for q in range(NP):
-                square_ref[:, q * BW : (q + 1) * BW] = rows_ref[
-                    :, (2 * q + c) * BW : (2 * q + c + 1) * BW
+            for i, (q, p) in enumerate(LOWER):
+                lower_ref[i * BW : (i + 1) * BW, :] = rows_ref[
+                    q * BW : (q + 1) * BW, (2 * p + c) * BW : (2 * p + c + 1) * BW
                 ]
 
 
@@ -153,10 +160,10 @@
         head_kernel,
         out_shape=(
             jax.ShapeDtypeStruct((HEAD, PANEL), jnp.float32),
-            jax.ShapeDtypeStruct((HEAD, HEAD), jnp.float32),
+            jax.ShapeDtypeStruct((len(LOWER) * BW, BW), jnp.float32),
         ),
         in_specs=[pl.BlockSpec(memory_space=pltpu.SMEM)] * 2
-        + [pl.BlockSpec(memory_space=pl.ANY)] * 10,
+        + [pl.BlockSpec(memory_space=pl.ANY)] * PIECES,
         out_specs=(pl.BlockSpec(memory_space=pltpu.VMEM),) * 2,
         scratch_shapes=[pltpu.SemaphoreType.DMA((NP,))],
         cost_estimate=pl.CostEstimate(flops=0, bytes_accessed=4 * 10**6, transcendentals=0),
@@ -215,7 +222,7 @@
     return jnp.concatenate(out, axis=0)
 
 
-def factor_kernel(col_ref, rows_ref, square_ref, w_ref):
+def factor_kernel(col_ref, rows_ref, lower_ref, w_ref):
     def span(i):
         return slice(i * BW, (i + 1) * BW)
 
@@ -230,7 +237,11 @@
                     other = rows_ref[span(q), span(2 * p + d)]
                     w_ref[span(2 * q + c), span(2 * p + d)] = other
                     w_ref[span(2 * p + d), span(2 * q + c)] = other.T
-                    w_ref[span(2 * q + d), span(2 * p + d)] = square_ref[span(q), span(p)]
+            for i, (q, p) in enumerate(LOWER):
+                block = lower_ref[span(i), :]
+                w_ref[span(2 * q + d), span(2 * p + d)] = block
+                if p < q:
+                    w_ref[span(2 * p + d), span(2 * q + d)] = block.T
 
     n = PANEL
     row_ids = lax.broadcasted_iota(jnp.int32, (n, BW), 0)
@@ -275,15 +286,14 @@
 
 
 def update_kernel(order_ref, x_ref, *refs):
-    pieces, out_ref = refs[:10], refs[10]
-    high, low, held, made, in_sem, out_sem = refs[11:]
+    pieces, out_ref = refs[:PIECES], refs[PIECES]
+    high, low, held, made, in_sem, out_sem = refs[PIECES + 1 :]
     steps = N_ROW // 2
     slots = held.shape[0]
 
     def fetch(step):
-        for p in range(10):
-            first = 16 * (p // 5) + PIECE_START[p % 5] // 2
-            last = first + PIECE_BLOCKS[p % 5] // 2
+        for p in range(PIECES):
+            first, last = p * PIECE // 2, (p + 1) * PIECE // 2
 
             @pl.when((step >= first) & (step < last))
             def _():
@@ -347,7 +357,7 @@
         update_kernel,
         out_shape=jax.ShapeDtypeStruct((PW, width), jnp.float32),
         in_specs=[pl.BlockSpec(memory_space=pltpu.SMEM), pl.BlockSpec(memory_space=pltpu.VMEM)]
-        + [pl.BlockSpec(memory_space=pl.ANY)] * 10,
+        + [pl.BlockSpec(memory_space=pl.ANY)] * PIECES,
         out_specs=pl.BlockSpec(memory_space=pl.ANY),
         scratch_shapes=[
             pltpu.VMEM((PW, PANEL), jnp.bfloat16),
@@ -382,7 +392,7 @@
         out_ref[:, :HEAD] = jnp.zeros((PW, HEAD), jnp.float32)
 
 
-def place_rows(place, arrived, update, tile=512):
+def place_rows(place, arrived, update, tile=2048):
     width = arrived.shape[2]
     return pl.pallas_call(
         functools.partial(place_kernel, tile),
@@ -395,6 +405,7 @@
         ],
         out_specs=pl.BlockSpec((PW, tile), lambda i: (0, i)),
         scratch_shapes=[pltpu.VMEM((PW, tile), jnp.float32)],
+        compiler_params=pltpu.CompilerParams(vmem_limit_bytes=40 * 2**20),
         cost_estimate=pl.CostEstimate(
             flops=4 * PW * PW * width, bytes_accessed=12 * PW * width, transcendentals=0
         ),
@@ -424,32 +435,25 @@
         return lax.dynamic_slice(front_matrix, (half * BW, 0), (BW, HEAD))
 
     own, others = half_rows(col), half_rows(1 - col)
-    own_beside = lax.ppermute(others, "col", swap)
-    own_across = move(own, "y")
-    mine = weave(own, own_beside, col)
-    across = weave(own_across, move(own_beside, "y"), col)
-    others_beside = lax.ppermute(own, "col", swap)
+    mine = weave(own, lax.ppermute(others, "col", swap), col)
+    theirs = weave(others, lax.ppermute(own, "col", swap), col)
+    panel = jnp.concatenate(
+        [jnp.where(col == 0, mine, theirs), jnp.where(col == 0, theirs, mine)], axis=0
+    )
 
     targets = row_map[0].reshape(N_ROW, CAP)[:, 0] // PW
     within = (row_map[0] % PW).astype(jnp.float32)
+    small = jnp.concatenate([panel, jnp.broadcast_to(within[:, None], (PW, BW))], axis=1)
+    small = send(pack_runs(targets, small, 0, PANEL + BW, PANEL + BW))
     outgoing = pack_runs(targets, front_matrix, 0, width, 512)
-    pieces, outgoing = gather_rows(jnp.concatenate([mine, across], axis=0), outgoing)
-
-    theirs = weave(others, others_beside, col)
-    panel = jnp.concatenate(
-        [jnp.where(col == 0, mine, theirs), jnp.where(col == 0, theirs, mine)], axis=0
-    )
-    small = jnp.concatenate([panel, jnp.broadcast_to(within[:, None], (PW, BW))], axis=1)
-    small = pack_runs(targets, small, 0, PANEL + BW, PANEL + BW)
+    pieces, small, outgoing = gather_rows(mine, small, outgoing)
 
     table = lax.dynamic_slice_in_dim(jnp.asarray(block_table()), row, 1, 0)[0]
     order, places = table[:N_ROW], table[N_ROW : N_ROW + 8]
     cols = col.reshape(1).astype(jnp.int32)
     rows, square = head_rows(places, cols, pieces)
-    square, small = lax.optimization_barrier((square, small))
     square = lax.ppermute(square, "col", swap)
-    small = send(small)
-    outgoing, square, small = lax.optimization_barrier((outgoing, square, small))
+    outgoing, square = lax.optimization_barrier((outgoing, square))
     arrived = send(outgoing)
 
     w = inverse_factor(cols, rows, square)

time: 303 us -> 286 us (0.944)
  local copies, waits for them, and re-layouts: 23 us -> 5.26 us
  waiting for transfers between devices: 98.6 us -> 105 us
  Pallas kernels: 97.9 us -> 92 us
    ppermute x15 -> x21, waiting for transfers between devices: 39.6 us -> 60.1 us  [move(): return lax.ppermute(value, 'row', pairs_of(kind, step))]
    ppermute x1, waiting for transfers between devices: 22.7 us -> 9.45 us  [local(): square = lax.ppermute(square, 'col', swap)]
    unnamed x46 -> x49, local copies, waits for them, and re-layouts: 10.6 us -> 2.31 us
    all_to_all x2, starting transfers between devices: 13.4 us -> 19.8 us  [send(): return lax.all_to_all(runs, 'row', split_axis=0, concat_axis=0, tiled=True)]
    pallas_call x1, Pallas kernels: 16.4 us -> 10.8 us  [place_rows(): pl.pallas_call(functools.partial(place_kernel, tile), out_shape=jax.Shape...]
    slice x4 -> x0, local copies, waits for them, and re-layouts: 5.18 us -> none  [the longest x2 3.82 us: ring(): far_second = move(after[half:], kind, -1)]
    ppermute x15 -> x21, starting transfers between devices: 40.3 us -> 36.7 us  [move(): return lax.ppermute(value, 'row', pairs_of(kind, step))]
    ppermute x2, waiting for transfers between devices: 7.41 us -> 4.32 us  [the longest x1 3.34 us: local(): mine = weave(own, lax.ppermute(others, 'col', swap), col)]
  transfers between devices with their start and end apart: 20 -> 26, of which waited for: 11 -> 12; matrix products, arithmetic and copies ran while one was open for 10% -> 5% of each run, Pallas kernels for 26% -> 27%
where the time goes in v5:
time: 286 us; the launch traced here: 283 us
  waiting for transfers between devices  105 us (37%)
  Pallas kernels  92 us (32%)
  starting transfers between devices  66 us (23%)
  matrix products  7.4 us (3%)
  other arithmetic  6.8 us (2%)
  local copies, waits for them, and re-layouts  5.26 us (2%)
    ppermute x21, waiting for transfers between devices, move(): return lax.ppermute(value, 'row', pairs_of(kind, step))  60.1 us
    pallas_call x1, Pallas kernels, inverse_factor(): pl.pallas_call(factor_kernel, out_shape=jax.ShapeDtypeStruct((PANEL, PANE...  41.8 us
    ppermute x21, starting transfers between devices, move(): return lax.ppermute(value, 'row', pairs_of(kind, step))  36.7 us
    all_to_all x2, waiting for transfers between devices, send(): return lax.all_to_all(runs, 'row', split_axis=0, concat_axis=0, tiled=True)  30.8 us
    pallas_call x1, Pallas kernels, update_of(): pl.pallas_call(update_kernel, out_shape=jax.ShapeDtypeStruct((PW, width),...  20.7 us
    all_to_all x2, starting transfers between devices, send(): return lax.all_to_all(runs, 'row', split_axis=0, concat_axis=0, tiled=True)  19.8 us
    pallas_call x2, Pallas kernels, pack_runs(): pl.pallas_call(pack_kernel, out_shape=jax.ShapeDtypeStruct((N_ROW, CAP, w...  15.5 us
    pallas_call x1, Pallas kernels, place_rows(): pl.pallas_call(functools.partial(place_kernel, tile), out_shape=jax.Shape...  10.8 us
  transfers between devices with their start and end apart: 26, of which 12 were waited for; matrix products, arithmetic and copies ran while one was open for 5% of the time, Pallas kernels for 27%

profile of v5, /device:TPU:1, one launch (start us, length us, event | category | flops | bytes accessed | tf_op | source)
XLA Modules:
  0.0 283.2 jit_solution(14181921228641251637)
XLA Ops:
  0.6 0.9 constant_dynamic-slice_fusion.2
  1.6 3.8 %collective-permute-start.1 = (f32[128,384]{1,0:T(8,128)S(1)}, f32[128,384]{1,0:T(8,128)S(1)}, u32[]{:S(2)}, u32[]{:S(2)}) collective-permute-start(f32[128,384]{1,0:T(8,128)S(1)} %constant_dynamic-slice_fusion.2), channel_id=1, source_target_pairs={{0,1},{1,0},{2,3},{3,2},{4,5},{5,4},{6,7},{7,6},{8,9},{9,8},{10,11... | collective-permute-start | bytes 589832 | tf_op jit(solution)/shard_map/ppermute | solution.py:439
  5.4 0.5 broadcast.94
  5.9 1.3 reduce.5
  7.3 0.7 fusion.11
  7.9 0.1 reshape_squeeze.3
  8.1 0.1 slice_reduce_fusion
  8.2 0.6 and_select_fusion.1.slot_ref
  8.8 1.0 collective-permute-done.1
  9.8 1.0 broadcast_select_fusion.2
  10.7 3.0 %collective-permute-start = (f32[128,384]{1,0:T(8,128)S(1)}, f32[128,384]{1,0:T(8,128)S(1)}, u32[]{:S(2)}, u32[]{:S(2)}) collective-permute-start(f32[128,384]{1,0:T(8,128)S(1)} %get-tuple-element.23), channel_id=1, source_target_pairs={{0,1},{1,0},{2,3},{3,2},{4,5},{5,4},{6,7},{7,6},{8,9},{9,8},{10,11... | collective-permute-start | bytes 589832 | tf_op jit(solution)/shard_map/ppermute | solution.py:438
  13.8 3.3 %collective-permute-done = f32[128,384]{1,0:T(8,128)S(1)} collective-permute-done((f32[128,384]{1,0:T(8,128)S(1)}, f32[128,384]{1,0:T(8,128)S(1)}, u32[]{:S(2)}, u32[]{:S(2)}) %collective-permute-start) | collective-permute-done | bytes 196640 | tf_op jit(solution)/shard_map/ppermute | solution.py:438
  17.2 1.0 broadcast_select_fusion.4
  18.2 0.1 broadcast_select_fusion.1
  18.3 0.1 broadcast_in_dim.22
  18.4 0.6 copy-done.9
  19.0 0.1 copy-done.11
  19.2 1.0 pad_maximum_fusion.1.rows_ref
  20.2 2.9 %pack_runs.2 = f32[64,4,896]{2,1,0:T(4,128)} custom-call(s32[64]{0:T(128)} %and_select_fusion.1.slot_ref, f32[256,896]{1,0:T(8,128)} %pad_maximum_fusion.1.rows_ref), custom_call_target="tpu_custom_call" | custom-call | bytes 1835008 | tf_op jit(solution)/shard_map/pack_runs/pallas_call | solution.py:114
  23.0 11.8 %all-to-all-start = ((f32[64,4,896]{2,1,0:T(4,128)}), f32[64,4,896]{2,1,0:T(4,128)S(1)}, u32[]{:S(2)}, u32[]{:S(2)}) async-start(f32[64,4,896]{2,1,0:T(4,128)} %pack_runs.2), calls=%async_computation | async-start | bytes 1835008 | tf_op jit(solution)/shard_map/all_to_all | solution.py:432
  34.8 1.5 collective-permute-start.3
  36.3 1.2 collective-permute-start.2
  37.5 17.6 %collective-permute-done.3 = f32[128,768]{1,0:T(8,128)S(1)} collective-permute-done((f32[128,768]{1,0:T(8,128)S(1)}, f32[128,768]{1,0:T(8,128)S(1)}, u32[]{:S(2)}, u32[]{:S(2)}) %collective-permute-start.3) | collective-permute-done | bytes 393248 | tf_op jit(solution)/shard_map/ppermute | solution.py:61
  55.1 2.7 collective-permute-start.4
  57.7 4.7 %collective-permute-done.4 = f32[128,768]{1,0:T(8,128)S(1)} collective-permute-done((f32[128,768]{1,0:T(8,128)S(1)}, f32[128,768]{1,0:T(8,128)S(1)}, u32[]{:S(2)}, u32[]{:S(2)}) %collective-permute-start.4) | collective-permute-done | bytes 393248 | tf_op jit(solution)/shard_map/ppermute | solution.py:61
  62.5 3.4 %collective-permute-start.9 = (f32[128,768]{1,0:T(8,128)S(1)}, f32[128,768]{1,0:T(8,128)S(1)}, u32[]{:S(2)}, u32[]{:S(2)}) collective-permute-start(f32[128,768]{1,0:T(8,128)S(1)} %collective-permute-done.4), channel_id=1, source_target_pairs={{0,12},{2,98},{4,0},{6,102},{8,4},{10,106},{12,8},{14,110},{16,28}... | collective-permute-start | bytes 1179656 | tf_op jit(solution)/shard_map/ppermute | solution.py:61
  65.9 0.1 collective-permute-start.5
  65.9 1.4 collective-permute-start.6
  67.4 3.1 %collective-permute-done.9 = f32[128,768]{1,0:T(8,128)S(1)} collective-permute-done((f32[128,768]{1,0:T(8,128)S(1)}, f32[128,768]{1,0:T(8,128)S(1)}, u32[]{:S(2)}, u32[]{:S(2)}) %collective-permute-start.9) | collective-permute-done | bytes 393248 | tf_op jit(solution)/shard_map/ppermute | solution.py:61
  70.6 2.8 collective-permute-start.10
  73.4 1.4 collective-permute-done.5
  74.8 1.1 pad_maximum_fusion.refs_0_
  75.9 1.1 collective-permute-start.7
  77.0 1.2 collective-permute-start.13
  78.3 6.8 %collective-permute-start.19 = (f32[512,768]{1,0:T(8,128)S(1)}, f32[512,768]{1,0:T(8,128)}, u32[]{:S(2)}, u32[]{:S(2)}) collective-permute-start(f32[512,768]{1,0:T(8,128)S(1)} %constant_dynamic-update-slice_fusion.refs_4_), channel_id=1, source_target_pairs={{0,2},{2,0},{4,6},{6,4},{8,10},{10,8},{12,14},{14,12},{16,18},{18,... | collective-permute-start | bytes 4718600 | tf_op jit(solution)/shard_map/ppermute | solution.py:61
  85.1 12.7 %pack_runs.3 = f32[64,4,8192]{2,1,0:T(4,128)} custom-call(s32[64]{0:T(128)} %and_select_fusion.1.slot_ref, f32[256,8192]{1,0:T(8,128)} %rows_ref.1), custom_call_target="tpu_custom_call" | custom-call | bytes 16777216 | tf_op jit(solution)/shard_map/pack_runs/pallas_call | solution.py:114
  97.8 3.5 %collective-permute-start.11 = (f32[512,768]{1,0:T(8,128)S(1)}, f32[512,768]{1,0:T(8,128)}, u32[]{:S(2)}, u32[]{:S(2)}) collective-permute-start(f32[512,768]{1,0:T(8,128)S(1)} %pad_maximum_fusion.refs_0_), channel_id=1, source_target_pairs={{0,96},{2,14},{4,100},{6,2},{8,104},{10,6},{12,108},{14,10},{16,11... | collective-permute-start | bytes 4718600 | tf_op jit(solution)/shard_map/ppermute | solution.py:61
  101.3 12.4 %collective-permute-done.13.refs_5_ = f32[512,768]{1,0:T(8,128)} collective-permute-done((f32[512,768]{1,0:T(8,128)S(1)}, f32[512,768]{1,0:T(8,128)}, u32[]{:S(2)}, u32[]{:S(2)}) %collective-permute-start.13) | collective-permute-done | bytes 1572896 | tf_op jit(solution)/shard_map/ppermute | solution.py:61
  113.8 5.9 %collective-permute-start.20 = (f32[512,768]{1,0:T(8,128)}, f32[512,768]{1,0:T(8,128)S(1)}, u32[]{:S(2)}, u32[]{:S(2)}) collective-permute-start(f32[512,768]{1,0:T(8,128)} %collective-permute-done.13.refs_5_), channel_id=1, source_target_pairs={{0,2},{2,0},{4,6},{6,4},{8,10},{10,8},{12,14},{14,12},{16,18},{18,... | collective-permute-start | bytes 4718600 | tf_op jit(solution)/shard_map/ppermute | solution.py:61
  119.7 3.4 %collective-permute-start.14 = (f32[512,768]{1,0:T(8,128)}, f32[512,768]{1,0:T(8,128)S(1)}, u32[]{:S(2)}, u32[]{:S(2)}) collective-permute-start(f32[512,768]{1,0:T(8,128)} %collective-permute-done.10.refs_6_), channel_id=1, source_target_pairs={{0,96},{2,14},{4,100},{6,2},{8,104},{10,6},{12,108},{14,10},{16,11... | collective-permute-start | bytes 4718600 | tf_op jit(solution)/shard_map/ppermute | solution.py:61
  123.1 0.5 collective-permute-start.21
  123.6 0.1 collective-permute-start.17
  123.7 17.5 %collective-permute-done.12.refs_3_ = f32[512,768]{1,0:T(8,128)} collective-permute-done((f32[512,768]{1,0:T(8,128)}, f32[512,768]{1,0:T(8,128)}, u32[]{:S(2)}, u32[]{:S(2)}) %collective-permute-start.12) | collective-permute-done | bytes 1572896 | tf_op jit(solution)/shard_map/ppermute | solution.py:61
  141.2 0.4 collective-permute-start.18
  141.6 0.7 collective-permute-start.22
  142.3 0.7 constant_dynamic-slice_fusion
  143.0 0.7 slice_bitcast_fusion.1.place_ref
  143.7 1.3 collective-permute-done.18.refs_11_
  145.0 2.0 collective-permute-done.22.refs_15_
  147.0 3.1 %head_rows.1 = (f32[384,768]{1,0:T(8,128)}, f32[768,128]{1,0:T(8,128)}) custom-call(s32[8]{0:T(128)} %slice_bitcast_fusion.1.place_ref, s32[1]{0:T(128)} %bitcast.col_ref, f32[512,768]{1,0:T(8,128)} %copy-done, f32[512,768]{1,0:T(8,128)} %collective-permute-done.7.refs_1_, f32[512,768]{1,0:T(8,128)} %collective-permute-done.11.refs_2_, ...), custom_call_target="tpu_custom_call" | custom-call | bytes 4000000 | tf_op jit(solution)/shard_map/head_rows/pallas_call | solution.py:159
  150.2 2.7 collective-permute-start.23
  152.9 9.4 %collective-permute-done.23.lower_ref = f32[768,128]{1,0:T(8,128)S(1)} collective-permute-done((f32[768,128]{1,0:T(8,128)}, f32[768,128]{1,0:T(8,128)S(1)}, u32[]{:S(2)}, u32[]{:S(2)}) %collective-permute-start.23) | collective-permute-done | bytes 393248 | tf_op jit(solution)/shard_map/ppermute | solution.py:455
  162.3 8.0 %all-to-all-start.1 = ((f32[64,4,8192]{2,1,0:T(4,128)}), f32[64,4,8192]{2,1,0:T(4,128)}, u32[]{:S(2)}, u32[]{:S(2)}) async-start(f32[64,4,8192]{2,1,0:T(4,128)} %pack_runs.3), calls=%async_computation.1 | async-start | bytes 16777216 | tf_op jit(solution)/shard_map/all_to_all | solution.py:432
  170.4 0.3 reshape.85
  170.8 0.1 copy.9
  170.8 0.1 fusion.6.place_ref
  170.9 0.7 copy-done.6
  171.6 41.8 %inverse_factor.1 = f32[768,768]{1,0:T(8,128)S(1)} custom-call(s32[1]{0:T(128)} %bitcast.col_ref, f32[384,768]{1,0:T(8,128)S(1)} %copy-done.6, f32[768,128]{1,0:T(8,128)S(1)} %collective-permute-done.23.lower_ref), custom_call_target="tpu_custom_call" | custom-call | flops 4000000000 | bytes 5000000 | tf_op jit(solution)/shard_map/inverse_factor/pallas_call | solution.py:274
  213.4 3.0 %convolution_select_fusion = f32[256,768]{1,0:T(8,128)} fusion(f32[768,768]{1,0:T(8,128)S(1)} %inverse_factor.1, f32[128,768]{1,0:T(8,128)S(1)} %copy-done.12, f32[128,768]{1,0:T(8,128)S(1)} %copy-done.10, pred[768]{0:T(1024)(128)(4,1)S(1)} %fusion.7), kind=kOutput, calls=%fused_computation.1 | convolution fusion | flops 1812332544 | bytes 3932928 | tf_op jit(solution)/shard_map/dot_general | solution.py:27
  216.5 2.2 fusion
  218.7 2.2 fusion.14.x_ref
  220.9 20.7 %update_of.1.update_ref = f32[256,8192]{1,0:T(8,128)} custom-call(s32[64]{0:T(128)S(1)} %slice_bitcast_fusion.order_ref, f32[256,768]{1,0:T(8,128)S(1)} %fusion.14.x_ref, f32[512,768]{1,0:T(8,128)S(1)} %copy-done.1, f32[512,768]{1,0:T(8,128)} %collective-permute-done.7.refs_1_, f32[512,768]{1,0:T(8,128)} %collective-permute-done.11.refs_2_, ...), custom_call_target="tpu_custom_call" | custom-call | flops 9663676416 | bytes 34000000 | tf_op jit(solution)/shard_map/update_of/pallas_call | solution.py:356
  241.6 30.8 %all-to-all-done.1.arrived_ref = f32[64,4,8192]{2,1,0:T(4,128)} async-done(((f32[64,4,8192]{2,1,0:T(4,128)}), f32[64,4,8192]{2,1,0:T(4,128)}, u32[]{:S(2)}, u32[]{:S(2)}) %all-to-all-start.1) | async-done | bytes 8388640 | tf_op jit(solution)/shard_map/all_to_all | solution.py:432
  272.4 10.8 %place_rows.1 = f32[256,8192]{1,0:T(8,128)} custom-call(bf16[256,256]{1,0:T(8,128)(2,1)S(1)} %fusion.6.place_ref, f32[64,4,8192]{2,1,0:T(4,128)} %all-to-all-done.1.arrived_ref, f32[256,8192]{1,0:T(8,128)} %update_of.1.update_ref), custom_call_target="tpu_custom_call" | custom-call | flops 2147483648 | bytes 25165824 | tf_op jit(solution)/shard_map/place_rows/pallas_call | solution.py:397
  (70 shorter events, 0.4 us)
Async XLA Ops:
  1.6 8.2 %collective-permute-start.1 = (f32[128,384]{1,0:T(8,128)S(1)}, f32[128,384]{1,0:T(8,128)S(1)}, u32[]{:S(2)}, u32[]{:S(2)}) collective-permute-start(f32[128,384]{1,0:T(8,128)S(1)} %constant_dynamic-slice_fusion.2), channel_id=1, source_target_pairs={{0,1},{1,0},{2,3},{3,2},{4,5},{5,4},{6,7},{7,6},{8,9},{9,8},{10,11... | collective-permute-start | bytes 589832 | tf_op jit(solution)/shard_map/ppermute | solution.py:439
  10.7 6.5 %collective-permute-start = (f32[128,384]{1,0:T(8,128)S(1)}, f32[128,384]{1,0:T(8,128)S(1)}, u32[]{:S(2)}, u32[]{:S(2)}) collective-permute-start(f32[128,384]{1,0:T(8,128)S(1)} %get-tuple-element.23), channel_id=1, source_target_pairs={{0,1},{1,0},{2,3},{3,2},{4,5},{5,4},{6,7},{7,6},{8,9},{9,8},{10,11... | collective-permute-start | bytes 589832 | tf_op jit(solution)/shard_map/ppermute | solution.py:438
  18.3 0.7 copy-start.9
  18.3 0.9 copy-start.11
  23.0 39.4 %all-to-all-start = ((f32[64,4,896]{2,1,0:T(4,128)}), f32[64,4,896]{2,1,0:T(4,128)S(1)}, u32[]{:S(2)}, u32[]{:S(2)}) async-start(f32[64,4,896]{2,1,0:T(4,128)} %pack_runs.2), calls=%async_computation | async-start | bytes 1835008 | tf_op jit(solution)/shard_map/all_to_all | solution.py:432
  34.8 20.2 %collective-permute-start.3 = (f32[128,768]{1,0:T(8,128)S(1)}, f32[128,768]{1,0:T(8,128)S(1)}, u32[]{:S(2)}, u32[]{:S(2)}) collective-permute-start(f32[128,768]{1,0:T(8,128)S(1)} %slice_dynamic-update-slice_fusion.6), channel_id=1, source_target_pairs={{0,16},{2,18},{4,20},{6,22},{8,24},{10,26},{12,28},{14,30},{16,0},... | collective-permute-start | bytes 1179656 | tf_op jit(solution)/shard_map/ppermute | solution.py:61
  36.3 21.4 %collective-permute-start.2 = (f32[128,768]{1,0:T(8,128)S(1)}, f32[128,768]{1,0:T(8,128)S(1)}, u32[]{:S(2)}, u32[]{:S(2)}) collective-permute-start(f32[128,768]{1,0:T(8,128)S(1)} %slice_dynamic-update-slice_fusion.6), channel_id=1, source_target_pairs={{0,4},{2,34},{4,8},{6,38},{8,12},{10,42},{12,0},{14,46},{16,20},{1... | collective-permute-start | bytes 1179656 | tf_op jit(solution)/shard_map/ppermute | solution.py:61
  55.1 7.4 %collective-permute-start.4 = (f32[128,768]{1,0:T(8,128)S(1)}, f32[128,768]{1,0:T(8,128)S(1)}, u32[]{:S(2)}, u32[]{:S(2)}) collective-permute-start(f32[128,768]{1,0:T(8,128)S(1)} %collective-permute-done.3), channel_id=1, source_target_pairs={{0,12},{2,98},{4,0},{6,102},{8,4},{10,106},{12,8},{14,110},{16,28}... | collective-permute-start | bytes 1179656 | tf_op jit(solution)/shard_map/ppermute | solution.py:61
  57.7 9.6 %collective-permute-start.8 = (f32[128,768]{1,0:T(8,128)S(1)}, f32[128,768]{1,0:T(8,128)S(1)}, u32[]{:S(2)}, u32[]{:S(2)}) collective-permute-start(f32[128,768]{1,0:T(8,128)S(1)} %collective-permute-done.3), channel_id=1, source_target_pairs={{0,4},{2,34},{4,8},{6,38},{8,12},{10,42},{12,0},{14,46},{16,20},{1... | collective-permute-start | bytes 1179656 | tf_op jit(solution)/shard_map/ppermute | solution.py:61
  57.7 17.1 %copy-start.16 = (f32[128,768]{1,0:T(8,128)}, f32[128,768]{1,0:T(8,128)S(1)}, u32[]{:S(2)}) copy-start(f32[128,768]{1,0:T(8,128)S(1)} %collective-permute-done.2) | copy-start | bytes 1179652
  62.5 3.5 %copy-start.7 = (f32[64,4,896]{2,1,0:T(4,128)}, f32[64,4,896]{2,1,0:T(4,128)S(1)}, u32[]{:S(2)}) copy-start(f32[64,4,896]{2,1,0:T(4,128)S(1)} %all-to-all-done) | copy-start | bytes 2752516
  62.5 8.1 %collective-permute-start.9 = (f32[128,768]{1,0:T(8,128)S(1)}, f32[128,768]{1,0:T(8,128)S(1)}, u32[]{:S(2)}, u32[]{:S(2)}) collective-permute-start(f32[128,768]{1,0:T(8,128)S(1)} %collective-permute-done.4), channel_id=1, source_target_pairs={{0,12},{2,98},{4,0},{6,102},{8,4},{10,106},{12,8},{14,110},{16,28}... | collective-permute-start | bytes 1179656 | tf_op jit(solution)/shard_map/ppermute | solution.py:61
  65.9 8.9 %collective-permute-start.5 = (f32[128,768]{1,0:T(8,128)S(1)}, f32[128,768]{1,0:T(8,128)S(1)}, u32[]{:S(2)}, u32[]{:S(2)}) collective-permute-start(f32[128,768]{1,0:T(8,128)S(1)} %slice_dynamic-update-slice_fusion.6), channel_id=1, source_target_pairs={{0,12},{2,98},{4,0},{6,102},{8,4},{10,106},{12,8},{14,110},{16,28}... | collective-permute-start | bytes 1179656 | tf_op jit(solution)/shard_map/ppermute | solution.py:61
  65.9 8.9 %collective-permute-start.6 = (f32[128,768]{1,0:T(8,128)S(1)}, f32[128,768]{1,0:T(8,128)S(1)}, u32[]{:S(2)}, u32[]{:S(2)}) collective-permute-start(f32[128,768]{1,0:T(8,128)S(1)} %collective-permute-done.2), channel_id=1, source_target_pairs={{0,4},{2,34},{4,8},{6,38},{8,12},{10,42},{12,0},{14,46},{16,20},{1... | collective-permute-start | bytes 1179656 | tf_op jit(solution)/shard_map/ppermute | solution.py:61
  70.6 27.2 %copy-start.2 = (f32[512,768]{1,0:T(8,128)}, f32[512,768]{1,0:T(8,128)S(1)}, u32[]{:S(2)}) copy-start(f32[512,768]{1,0:T(8,128)S(1)} %constant_dynamic-update-slice_fusion.refs_4_) | copy-start | bytes 4718596
  70.6 27.2 %collective-permute-start.10 = (f32[512,768]{1,0:T(8,128)S(1)}, f32[512,768]{1,0:T(8,128)}, u32[]{:S(2)}, u32[]{:S(2)}) collective-permute-start(f32[512,768]{1,0:T(8,128)S(1)} %constant_dynamic-update-slice_fusion.refs_4_), channel_id=1, source_target_pairs={{0,96},{2,14},{4,100},{6,2},{8,104},{10,6},{12,108},{14,10},{16,11... | collective-permute-start | bytes 4718600 | tf_op jit(solution)/shard_map/ppermute | solution.py:61
  75.9 21.9 %copy-start = (f32[512,768]{1,0:T(8,128)}, f32[512,768]{1,0:T(8,128)S(1)}, u32[]{:S(2)}) copy-start(f32[512,768]{1,0:T(8,128)S(1)} %pad_maximum_fusion.refs_0_) | copy-start | bytes 4718596
  75.9 25.4 %collective-permute-start.7 = (f32[512,768]{1,0:T(8,128)S(1)}, f32[512,768]{1,0:T(8,128)}, u32[]{:S(2)}, u32[]{:S(2)}) collective-permute-start(f32[512,768]{1,0:T(8,128)S(1)} %pad_maximum_fusion.refs_0_), channel_id=1, source_target_pairs={{0,32},{2,6},{4,36},{6,10},{8,40},{10,14},{12,44},{14,2},{16,48},{... | collective-permute-start | bytes 4718600 | tf_op jit(solution)/shard_map/ppermute | solution.py:61
  77.0 36.7 %collective-permute-start.13 = (f32[512,768]{1,0:T(8,128)S(1)}, f32[512,768]{1,0:T(8,128)}, u32[]{:S(2)}, u32[]{:S(2)}) collective-permute-start(f32[512,768]{1,0:T(8,128)S(1)} %constant_dynamic-update-slice_fusion.refs_4_), channel_id=1, source_target_pairs={{0,32},{2,6},{4,36},{6,10},{8,40},{10,14},{12,44},{14,2},{16,48},{... | collective-permute-start | bytes 4718600 | tf_op jit(solution)/shard_map/ppermute | solution.py:61
  78.3 41.4 %collective-permute-start.19 = (f32[512,768]{1,0:T(8,128)S(1)}, f32[512,768]{1,0:T(8,128)}, u32[]{:S(2)}, u32[]{:S(2)}) collective-permute-start(f32[512,768]{1,0:T(8,128)S(1)} %constant_dynamic-update-slice_fusion.refs_4_), channel_id=1, source_target_pairs={{0,2},{2,0},{4,6},{6,4},{8,10},{10,8},{12,14},{14,12},{16,18},{18,... | collective-permute-start | bytes 4718600 | tf_op jit(solution)/shard_map/ppermute | solution.py:61
  97.8 25.3 %collective-permute-start.15 = (f32[512,768]{1,0:T(8,128)S(1)}, f32[512,768]{1,0:T(8,128)S(1)}, u32[]{:S(2)}, u32[]{:S(2)}) collective-permute-start(f32[512,768]{1,0:T(8,128)S(1)} %pad_maximum_fusion.refs_0_), channel_id=1, source_target_pairs={{0,2},{2,0},{4,6},{6,4},{8,10},{10,8},{12,14},{14,12},{16,18},{18,... | collective-permute-start | bytes 4718600 | tf_op jit(solution)/shard_map/ppermute | solution.py:61
  97.8 25.3 %collective-permute-start.11 = (f32[512,768]{1,0:T(8,128)S(1)}, f32[512,768]{1,0:T(8,128)}, u32[]{:S(2)}, u32[]{:S(2)}) collective-permute-start(f32[512,768]{1,0:T(8,128)S(1)} %pad_maximum_fusion.refs_0_), channel_id=1, source_target_pairs={{0,96},{2,14},{4,100},{6,2},{8,104},{10,6},{12,108},{14,10},{16,11... | collective-permute-start | bytes 4718600 | tf_op jit(solution)/shard_map/ppermute | solution.py:61
  113.8 9.8 %collective-permute-start.20 = (f32[512,768]{1,0:T(8,128)}, f32[512,768]{1,0:T(8,128)S(1)}, u32[]{:S(2)}, u32[]{:S(2)}) collective-permute-start(f32[512,768]{1,0:T(8,128)} %collective-permute-done.13.refs_5_), channel_id=1, source_target_pairs={{0,2},{2,0},{4,6},{6,4},{8,10},{10,8},{12,14},{14,12},{16,18},{18,... | collective-permute-start | bytes 4718600 | tf_op jit(solution)/shard_map/ppermute | solution.py:61
  119.7 21.6 %collective-permute-start.12 = (f32[512,768]{1,0:T(8,128)}, f32[512,768]{1,0:T(8,128)}, u32[]{:S(2)}, u32[]{:S(2)}) collective-permute-start(f32[512,768]{1,0:T(8,128)} %collective-permute-done.7.refs_1_), channel_id=1, source_target_pairs={{0,32},{2,6},{4,36},{6,10},{8,40},{10,14},{12,44},{14,2},{16,48},{... | collective-permute-start | bytes 4718600 | tf_op jit(solution)/shard_map/ppermute | solution.py:61
  119.7 21.9 %collective-permute-start.14 = (f32[512,768]{1,0:T(8,128)}, f32[512,768]{1,0:T(8,128)S(1)}, u32[]{:S(2)}, u32[]{:S(2)}) collective-permute-start(f32[512,768]{1,0:T(8,128)} %collective-permute-done.10.refs_6_), channel_id=1, source_target_pairs={{0,96},{2,14},{4,100},{6,2},{8,104},{10,6},{12,108},{14,10},{16,11... | collective-permute-start | bytes 4718600 | tf_op jit(solution)/shard_map/ppermute | solution.py:61
  123.1 18.5 %copy-start.13 = (f32[512,768]{1,0:T(8,128)}, f32[512,768]{1,0:T(8,128)S(1)}, u32[]{:S(2)}) copy-start(f32[512,768]{1,0:T(8,128)S(1)} %collective-permute-done.15.refs_8_) | copy-start | bytes 4718596
  123.1 20.6 %collective-permute-start.16 = (f32[512,768]{1,0:T(8,128)}, f32[512,768]{1,0:T(8,128)}, u32[]{:S(2)}, u32[]{:S(2)}) collective-permute-start(f32[512,768]{1,0:T(8,128)} %collective-permute-done.7.refs_1_), channel_id=1, source_target_pairs={{0,2},{2,0},{4,6},{6,4},{8,10},{10,8},{12,14},{14,12},{16,18},{18,... | collective-permute-start | bytes 4718600 | tf_op jit(solution)/shard_map/ppermute | solution.py:61
  123.1 20.6 %collective-permute-start.21 = (f32[512,768]{1,0:T(8,128)}, f32[512,768]{1,0:T(8,128)S(1)}, u32[]{:S(2)}, u32[]{:S(2)}) collective-permute-start(f32[512,768]{1,0:T(8,128)} %collective-permute-done.10.refs_6_), channel_id=1, source_target_pairs={{0,2},{2,0},{4,6},{6,4},{8,10},{10,8},{12,14},{14,12},{16,18},{18,... | collective-permute-start | bytes 4718600 | tf_op jit(solution)/shard_map/ppermute | solution.py:61
  123.6 18.0 %copy-start.14 = (f32[512,768]{1,0:T(8,128)}, f32[512,768]{1,0:T(8,128)S(1)}, u32[]{:S(2)}) copy-start(f32[512,768]{1,0:T(8,128)S(1)} %collective-permute-done.20.refs_13_) | copy-start | bytes 4718596
  123.6 20.1 %collective-permute-start.17 = (f32[512,768]{1,0:T(8,128)}, f32[512,768]{1,0:T(8,128)}, u32[]{:S(2)}, u32[]{:S(2)}) collective-permute-start(f32[512,768]{1,0:T(8,128)} %collective-permute-done.11.refs_2_), channel_id=1, source_target_pairs={{0,2},{2,0},{4,6},{6,4},{8,10},{10,8},{12,14},{14,12},{16,18},{18,... | collective-permute-start | bytes 4718600 | tf_op jit(solution)/shard_map/ppermute | solution.py:61
  141.2 3.8 %collective-permute-start.18 = (f32[512,768]{1,0:T(8,128)}, f32[512,768]{1,0:T(8,128)}, u32[]{:S(2)}, u32[]{:S(2)}) collective-permute-start(f32[512,768]{1,0:T(8,128)} %collective-permute-done.12.refs_3_), channel_id=1, source_target_pairs={{0,2},{2,0},{4,6},{6,4},{8,10},{10,8},{12,14},{14,12},{16,18},{18,... | collective-permute-start | bytes 4718600 | tf_op jit(solution)/shard_map/ppermute | solution.py:61
  141.6 5.4 %copy-start.4 = (f32[512,768]{1,0:T(8,128)}, f32[512,768]{1,0:T(8,128)S(1)}, u32[]{:S(2)}) copy-start(f32[512,768]{1,0:T(8,128)S(1)} %collective-permute-done.14.refs_7_) | copy-start | bytes 4718596
  141.6 5.4 %collective-permute-start.22 = (f32[512,768]{1,0:T(8,128)S(1)}, f32[512,768]{1,0:T(8,128)}, u32[]{:S(2)}, u32[]{:S(2)}) collective-permute-start(f32[512,768]{1,0:T(8,128)S(1)} %collective-permute-done.14.refs_7_), channel_id=1, source_target_pairs={{0,2},{2,0},{4,6},{6,4},{8,10},{10,8},{12,14},{14,12},{16,18},{18,... | collective-permute-start | bytes 4718600 | tf_op jit(solution)/shard_map/ppermute | solution.py:61
  143.7 3.3 %copy-start.15 = (f32[512,768]{1,0:T(8,128)}, f32[512,768]{1,0:T(8,128)S(1)}, u32[]{:S(2)}) copy-start(f32[512,768]{1,0:T(8,128)S(1)} %collective-permute-done.21.refs_14_) | copy-start | bytes 4718596
  150.2 20.2 %copy-start.8 = (f32[64,4,896]{2,1,0:T(4,128)S(1)}, f32[64,4,896]{2,1,0:T(4,128)}, u32[]{:S(2)}) copy-start(f32[64,4,896]{2,1,0:T(4,128)} %copy-done.7) | copy-start | bytes 2752516
  150.2 12.1 %collective-permute-start.23 = (f32[768,128]{1,0:T(8,128)}, f32[768,128]{1,0:T(8,128)S(1)}, u32[]{:S(2)}, u32[]{:S(2)}) collective-permute-start(f32[768,128]{1,0:T(8,128)} %get-tuple-element.18), channel_id=1, source_target_pairs={{0,1},{1,0},{2,3},{3,2},{4,5},{5,4},{6,7},{7,6},{8,9},{9,8},{10,11... | collective-permute-start | bytes 1179656 | tf_op jit(solution)/shard_map/ppermute | solution.py:455
  162.3 110.1 %all-to-all-start.1 = ((f32[64,4,8192]{2,1,0:T(4,128)}), f32[64,4,8192]{2,1,0:T(4,128)}, u32[]{:S(2)}, u32[]{:S(2)}) async-start(f32[64,4,8192]{2,1,0:T(4,128)} %pack_runs.3), calls=%async_computation.1 | async-start | bytes 16777216 | tf_op jit(solution)/shard_map/all_to_all | solution.py:432
  170.4 1.3 copy-start.6
  171.6 41.8 %copy-start.10 = (f32[128,768]{1,0:T(8,128)S(1)}, f32[128,768]{1,0:T(8,128)}, u32[]{:S(2)}) copy-start(f32[128,768]{1,0:T(8,128)} %copy-done.9) | copy-start | bytes 1179652
  171.6 41.8 %copy-start.12 = (f32[128,768]{1,0:T(8,128)S(1)}, f32[128,768]{1,0:T(8,128)}, u32[]{:S(2)}) copy-start(f32[128,768]{1,0:T(8,128)} %copy-done.11) | copy-start | bytes 1179652
  216.5 4.4 %copy-start.5 = (f32[512,768]{1,0:T(8,128)S(1)}, f32[512,768]{1,0:T(8,128)}, u32[]{:S(2)}) copy-start(f32[512,768]{1,0:T(8,128)} %copy-done.4) | copy-start | bytes 4718596
  218.7 2.2 copy-start.1
  218.7 2.2 copy-start.3

commit v6 on v5

--- a/solution.py
+++ b/solution.py
@@ -72,6 +72,9 @@
         )
     far_near = move(before_near, kind, 1)
     far_across = move(after_across, kind, -1)
+    far_near, far_across, before_across, after_near = lax.optimization_barrier(
+        (far_near, far_across, before_across, after_near)
+    )
     return (
         [near, before_near, after_near, far_near],
         [across, before_across, after_across, far_across],
@@ -81,11 +84,13 @@
 
 def gather_rows(mine, small, runs):
     near, across, small = ring(mine, move(mine, "y"), "first", small)
-    near, across, runs = ring(
-        jnp.concatenate(near, axis=0), jnp.concatenate(across, axis=0), "second", runs
-    )
+    near, across, runs = lax.optimization_barrier(
+        (jnp.concatenate(near, axis=0), jnp.concatenate(across, axis=0), runs)
+    )
+    near, across, _ = ring(near, across, "second")
     pieces = near + across
-    return pieces + [move(p, "core") for p in pieces], small, runs
+    runs, *swapped = lax.optimization_barrier((runs, *(move(p, "core") for p in pieces)))
+    return pieces + swapped, small, runs
 
 
 def block_table():
@@ -123,6 +128,7 @@
         cost_estimate=pl.CostEstimate(
             flops=0, bytes_accessed=2 * 4 * height * width, transcendentals=0
         ),
+        compiler_params=pltpu.CompilerParams(vmem_limit_bytes=60 * 2**20),
         name="pack_runs",
     )(slots, rows)
 
@@ -277,9 +283,9 @@
         in_specs=[pl.BlockSpec(memory_space=pltpu.SMEM)]
         + [pl.BlockSpec(memory_space=pltpu.VMEM)] * 2,
         out_specs=pl.BlockSpec(memory_space=pltpu.VMEM),
-        compiler_params=pltpu.CompilerParams(vmem_limit_bytes=40 * 2**20),
+        compiler_params=pltpu.CompilerParams(vmem_limit_bytes=60 * 2**20),
         cost_estimate=pl.CostEstimate(
-            flops=4 * 10**9, bytes_accessed=5 * 10**6, transcendentals=0
+            flops=2 * 10**11, bytes_accessed=5 * 10**6, transcendentals=0
         ),
         name="inverse_factor",
     )(col, rows, square)
@@ -367,7 +373,7 @@
             pltpu.SemaphoreType.DMA((4,)),
             pltpu.SemaphoreType.DMA((2, 2)),
         ],
-        compiler_params=pltpu.CompilerParams(vmem_limit_bytes=40 * 2**20),
+        compiler_params=pltpu.CompilerParams(vmem_limit_bytes=60 * 2**20),
         cost_estimate=pl.CostEstimate(
             flops=6 * PW * width * PANEL, bytes_accessed=34 * 10**6, transcendentals=0
         ),
@@ -405,7 +411,7 @@
         ],
         out_specs=pl.BlockSpec((PW, tile), lambda i: (0, i)),
         scratch_shapes=[pltpu.VMEM((PW, tile), jnp.float32)],
-        compiler_params=pltpu.CompilerParams(vmem_limit_bytes=40 * 2**20),
+        compiler_params=pltpu.CompilerParams(vmem_limit_bytes=60 * 2**20),
         cost_estimate=pl.CostEstimate(
             flops=4 * PW * PW * width, bytes_accessed=12 * PW * width, transcendentals=0
         ),
@@ -443,27 +449,30 @@
 
     targets = row_map[0].reshape(N_ROW, CAP)[:, 0] // PW
     within = (row_map[0] % PW).astype(jnp.float32)
-    small = jnp.concatenate([panel, jnp.broadcast_to(within[:, None], (PW, BW))], axis=1)
-    small = send(pack_runs(targets, small, 0, PANEL + BW, PANEL + BW))
-    outgoing = pack_runs(targets, front_matrix, 0, width, 512)
+    small = jnp.concatenate(
+        [front_matrix[:, :HEAD], jnp.broadcast_to(within[:, None], (PW, BW))], axis=1
+    )
+    small = send(pack_runs(targets, small, 0, HEAD + BW, HEAD + BW)).reshape(PW, HEAD + BW)
+    outgoing = pack_runs(targets, front_matrix, 0, width, 2048)
     pieces, small, outgoing = gather_rows(mine, small, outgoing)
 
     table = lax.dynamic_slice_in_dim(jnp.asarray(block_table()), row, 1, 0)[0]
     order, places = table[:N_ROW], table[N_ROW : N_ROW + 8]
     cols = col.reshape(1).astype(jnp.int32)
     rows, square = head_rows(places, cols, pieces)
+    sent_rows = small[:, :HEAD]
+    panel_beside = lax.ppermute(sent_rows, "col", swap)
     square = lax.ppermute(square, "col", swap)
-    outgoing, square = lax.optimization_barrier((outgoing, square))
+    outgoing, panel_beside, square = lax.optimization_barrier((outgoing, panel_beside, square))
     arrived = send(outgoing)
 
     w = inverse_factor(cols, rows, square)
-    small = small.reshape(PW, PANEL + BW)
-    lower = dot_t(small[:, :PANEL], w)
+    lower = dot_t(weave(sent_rows, panel_beside, col), w)
     update = update_of(order, dot_n(lower, w), pieces, width)
     panel_ids = lax.broadcasted_iota(jnp.int32, (1, PANEL), 1) // PW
     factors = jnp.where(row >= panel_ids, dot_t(panel, w), 0.0)
     slots = jnp.arange(PW, dtype=jnp.int32)
-    goes = small[:, PANEL].astype(jnp.int32)
+    goes = small[:, HEAD].astype(jnp.int32)
     place = (goes[None, :] == slots[:, None]) & (slots[None, :] >= NP * CAP)
     return factors, place_rows(place.astype(jnp.bfloat16), arrived, update)
 

time: 286 us -> 270 us (0.944)
  starting transfers between devices: 66 us -> 54.4 us
  waiting for transfers between devices: 105 us -> 94.6 us
  local copies, waits for them, and re-layouts: 5.26 us -> 8.51 us
  other arithmetic: 6.8 us -> 9.93 us
    ppermute x21, waiting for transfers between devices: 60.1 us -> 47.3 us  [move(): return lax.ppermute(value, 'row', pairs_of(kind, step))]
    ppermute x21, starting transfers between devices: 36.7 us -> 24.3 us  [move(): return lax.ppermute(value, 'row', pairs_of(kind, step))]
    pallas_call x2, Pallas kernels: 15.5 us -> 10.3 us  [pack_runs(): pl.pallas_call(pack_kernel, out_shape=jax.ShapeDtypeStruct((N_ROW, CAP, w...]
    ppermute x1, waiting for transfers between devices: 0.98 us -> 4.35 us  [local(): theirs = weave(others, lax.ppermute(own, 'col', swap), col)]
    all_to_all x2, waiting for transfers between devices: 30.8 us -> 33.9 us  [send(): return lax.all_to_all(runs, 'row', split_axis=0, concat_axis=0, tiled=True)]
    pallas_call x1, Pallas kernels: 41.8 us -> 44.7 us  [inverse_factor(): pl.pallas_call(factor_kernel, out_shape=jax.ShapeDtypeStruct((PANEL, PANE...]
  transfers between devices with their start and end apart: 26 -> 27, of which waited for: 12 -> 14; matrix products, arithmetic and copies ran while one was open for 5% -> 6% of each run, Pallas kernels for 27% -> 30%
where the time goes in v6:
time: 270 us; the launch traced here: 267 us
  waiting for transfers between devices  94.6 us (35%)
  Pallas kernels  90.6 us (34%)
  starting transfers between devices  54.4 us (20%)
  other arithmetic  9.93 us (4%)
  local copies, waits for them, and re-layouts  8.51 us (3%)
  matrix products  8.31 us (3%)
    ppermute x21, waiting for transfers between devices, move(): return lax.ppermute(value, 'row', pairs_of(kind, step))  47.3 us
    pallas_call x1, Pallas kernels, inverse_factor(): pl.pallas_call(factor_kernel, out_shape=jax.ShapeDtypeStruct((PANEL, PANE...  44.7 us
    all_to_all x2, waiting for transfers between devices, send(): return lax.all_to_all(runs, 'row', split_axis=0, concat_axis=0, tiled=True)  33.9 us
    ppermute x21, starting transfers between devices, move(): return lax.ppermute(value, 'row', pairs_of(kind, step))  24.3 us
    pallas_call x1, Pallas kernels, update_of(): pl.pallas_call(update_kernel, out_shape=jax.ShapeDtypeStruct((PW, width),...  21.7 us
    all_to_all x2, starting transfers between devices, send(): return lax.all_to_all(runs, 'row', split_axis=0, concat_axis=0, tiled=True)  17.6 us
    pallas_call x1, Pallas kernels, place_rows(): pl.pallas_call(functools.partial(place_kernel, tile), out_shape=jax.Shape...  10.8 us
    pallas_call x2, Pallas kernels, pack_runs(): pl.pallas_call(pack_kernel, out_shape=jax.ShapeDtypeStruct((N_ROW, CAP, w...  10.3 us
  transfers between devices with their start and end apart: 27, of which 14 were waited for; matrix products, arithmetic and copies ran while one was open for 6% of the time, Pallas kernels for 30%

profile of v6, /device:TPU:1, one launch (start us, length us, event | category | flops | bytes accessed | tf_op | source)
XLA Modules:
  0.0 267.4 jit_solution(12735685446440013362)
XLA Ops:
  0.7 1.0 constant_dynamic-slice_fusion.2
  1.7 3.8 %collective-permute-start.1 = (f32[128,384]{1,0:T(8,128)S(1)}, f32[128,384]{1,0:T(8,128)S(1)}, u32[]{:S(2)}, u32[]{:S(2)}) collective-permute-start(f32[128,384]{1,0:T(8,128)S(1)} %constant_dynamic-slice_fusion.2), channel_id=1, source_target_pairs={{0,1},{1,0},{2,3},{3,2},{4,5},{5,4},{6,7},{7,6},{8,9},{9,8},{10,11... | collective-permute-start | bytes 589832 | tf_op jit(solution)/shard_map/ppermute | solution.py:445
  5.5 4.3 %collective-permute-done.1 = f32[128,384]{1,0:T(8,128)S(1)} collective-permute-done((f32[128,384]{1,0:T(8,128)S(1)}, f32[128,384]{1,0:T(8,128)S(1)}, u32[]{:S(2)}, u32[]{:S(2)}) %collective-permute-start.1) | collective-permute-done | bytes 196640 | tf_op jit(solution)/shard_map/ppermute | solution.py:445
  9.8 1.0 broadcast_select_fusion.4
  10.8 3.0 %collective-permute-start = (f32[128,384]{1,0:T(8,128)S(1)}, f32[128,384]{1,0:T(8,128)S(1)}, u32[]{:S(2)}, u32[]{:S(2)}) collective-permute-start(f32[128,384]{1,0:T(8,128)S(1)} %get-tuple-element.59), channel_id=1, source_target_pairs={{0,1},{1,0},{2,3},{3,2},{4,5},{5,4},{6,7},{7,6},{8,9},{9,8},{10,11... | collective-permute-start | bytes 589832 | tf_op jit(solution)/shard_map/ppermute | solution.py:444
  13.8 0.7 fusion.9
  14.5 0.5 broadcast.94
  15.0 0.7 reduce.5
  15.9 0.8 pad_maximum_fusion.2.rows_ref
  16.7 0.5 collective-permute-done
  17.3 1.0 broadcast_select_fusion.6
  18.3 1.3 collective-permute-start.3
  19.8 0.6 and_select_fusion.1.slot_ref
  20.3 2.5 pack_runs.2
  22.9 11.1 %all-to-all-start = ((f32[64,4,512]{2,1,0:T(4,128)}), f32[64,4,512]{2,1,0:T(4,128)S(1)}, u32[]{:S(2)}, u32[]{:S(2)}) async-start(f32[64,4,512]{2,1,0:T(4,128)} %pack_runs.2), calls=%async_computation | async-start | bytes 1048576 | tf_op jit(solution)/shard_map/all_to_all | solution.py:438
  33.9 1.5 collective-permute-start.2
  35.4 1.5 collective-permute-start.4
  36.9 1.4 collective-permute-start.8
  38.3 8.2 %all-to-all-done = f32[64,4,512]{2,1,0:T(4,128)S(1)} async-done(((f32[64,4,512]{2,1,0:T(4,128)}), f32[64,4,512]{2,1,0:T(4,128)S(1)}, u32[]{:S(2)}, u32[]{:S(2)}) %all-to-all-start) | async-done | bytes 524320 | tf_op jit(solution)/shard_map/all_to_all | solution.py:438
  46.7 0.5 collective-permute-start.7
  47.1 0.4 collective-permute-done.2
  47.6 0.7 collective-permute-start.5
  48.3 2.0 collective-permute-start.6
  50.3 7.8 %pack_runs.3 = f32[64,4,8192]{2,1,0:T(4,128)} custom-call(s32[64]{0:T(128)} %and_select_fusion.1.slot_ref, f32[256,8192]{1,0:T(8,128)} %rows_ref.1), custom_call_target="tpu_custom_call" | custom-call | bytes 16777216 | tf_op jit(solution)/shard_map/pack_runs/pallas_call | solution.py:119
  58.1 1.0 collective-permute-done.5
  59.1 0.7 copy-done.9
  59.8 2.9 %pad_maximum_fusion = (f32[512,768]{1,0:T(8,128)S(1)}, f32[512,768]{1,0:T(8,128)}) fusion(f32[128,768]{1,0:T(8,128)} %copy-done.9, f32[128,768]{1,0:T(8,128)} %collective-permute-done.8, f32[128,768]{1,0:T(8,128)} %copy-done.7, f32[128,768]{1,0:T(8,128)S(1)} %slice_dynamic-update-slice_fusion.12, f32[128,768]{1,0:T(8,128)} %collective-permute-done.6, ...), kind=kLoop, calls=%fused_computation | loop fusion | flops 2359296 | bytes 6291456 | tf_op jit(solution)/shard_map/concatenate | solution.py:88
  63.0 2.4 collective-permute-start.11
  65.4 0.6 collective-permute-start.14
  66.0 0.9 collective-permute-start.13
  66.9 16.7 %collective-permute-done.9.refs_1_ = f32[512,768]{1,0:T(8,128)} collective-permute-done((f32[512,768]{1,0:T(8,128)S(1)}, f32[512,768]{1,0:T(8,128)}, u32[]{:S(2)}, u32[]{:S(2)}) %collective-permute-start.9) | collective-permute-done | bytes 1572896 | tf_op jit(solution)/shard_map/ppermute | solution.py:61
  83.6 2.9 %collective-permute-start.12 = (f32[512,768]{1,0:T(8,128)}, f32[512,768]{1,0:T(8,128)}, u32[]{:S(2)}, u32[]{:S(2)}) collective-permute-start(f32[512,768]{1,0:T(8,128)} %collective-permute-done.11.refs_6_), channel_id=1, source_target_pairs={{0,96},{2,14},{4,100},{6,2},{8,104},{10,6},{12,108},{14,10},{16,11... | collective-permute-start | bytes 4718600 | tf_op jit(solution)/shard_map/ppermute | solution.py:61
  86.5 2.7 %collective-permute-start.15 = (f32[512,768]{1,0:T(8,128)S(1)}, f32[512,768]{1,0:T(8,128)}, u32[]{:S(2)}, u32[]{:S(2)}) collective-permute-start(f32[512,768]{1,0:T(8,128)S(1)} %get-tuple-element.36.refs_0_), channel_id=1, source_target_pairs={{0,2},{2,0},{4,6},{6,4},{8,10},{10,8},{12,14},{14,12},{16,18},{18,... | collective-permute-start | bytes 4718600 | tf_op jit(solution)/shard_map/ppermute | solution.py:61
  89.2 10.6 %collective-permute-done.14.refs_2_ = f32[512,768]{1,0:T(8,128)S(1)} collective-permute-done((f32[512,768]{1,0:T(8,128)S(1)}, f32[512,768]{1,0:T(8,128)S(1)}, u32[]{:S(2)}, u32[]{:S(2)}) %collective-permute-start.14) | collective-permute-done | bytes 1572896 | tf_op jit(solution)/shard_map/ppermute | solution.py:61
  99.8 1.2 copy-done.4
  101.0 2.5 collective-permute-start.19
  103.5 0.7 constant_dynamic-slice_fusion
  104.2 0.6 fusion.5
  104.8 0.5 slice_bitcast_fusion.order_ref
  105.3 0.6 slice_bitcast_fusion.1.place_ref
  105.9 11.4 %collective-permute-done.10.refs_3_ = f32[512,768]{1,0:T(8,128)} collective-permute-done((f32[512,768]{1,0:T(8,128)}, f32[512,768]{1,0:T(8,128)}, u32[]{:S(2)}, u32[]{:S(2)}) %collective-permute-start.10) | collective-permute-done | bytes 1572896 | tf_op jit(solution)/shard_map/ppermute | solution.py:61
  117.3 2.2 collective-permute-start.21
  119.5 0.5 collective-permute-start.18
  120.1 0.4 collective-permute-start.22
  120.6 1.0 broadcast_select_fusion.3
  121.9 1.0 collective-permute-done.21.refs_14_
  122.9 2.8 %collective-permute-start.23 = (f32[256,384]{1,0:T(8,128)S(1)}, f32[256,384]{1,0:T(8,128)S(1)}, u32[]{:S(2)}, u32[]{:S(2)}) collective-permute-start(f32[256,384]{1,0:T(8,128)S(1)} %slice.94), channel_id=1, source_target_pairs={{0,1},{1,0},{2,3},{3,2},{4,5},{5,4},{6,7},{7,6},{8,9},{9,8},{10,11... | collective-permute-start | bytes 1179656 | tf_op jit(solution)/shard_map/ppermute | solution.py:464
  125.7 1.7 collective-permute-done.18.refs_11_
  127.4 2.2 collective-permute-done.20.refs_13_
  129.6 2.2 collective-permute-done.22.refs_15_
  131.9 3.1 %head_rows.1 = (f32[384,768]{1,0:T(8,128)}, f32[768,128]{1,0:T(8,128)}) custom-call(s32[8]{0:T(128)} %slice_bitcast_fusion.1.place_ref, s32[1]{0:T(128)} %bitcast.col_ref, f32[512,768]{1,0:T(8,128)} %copy-done.3, f32[512,768]{1,0:T(8,128)} %collective-permute-done.9.refs_1_, f32[512,768]{1,0:T(8,128)} %copy-done.4, ...), custom_call_target="tpu_custom_call" | custom-call | bytes 4000000 | tf_op jit(solution)/shard_map/head_rows/pallas_call | solution.py:165
  135.0 2.9 %collective-permute-start.24 = (f32[768,128]{1,0:T(8,128)}, f32[768,128]{1,0:T(8,128)S(1)}, u32[]{:S(2)}, u32[]{:S(2)}) collective-permute-start(f32[768,128]{1,0:T(8,128)} %get-tuple-element.54), channel_id=1, source_target_pairs={{0,1},{1,0},{2,3},{3,2},{4,5},{5,4},{6,7},{7,6},{8,9},{9,8},{10,11... | collective-permute-start | bytes 1179656 | tf_op jit(solution)/shard_map/ppermute | solution.py:465
  137.9 0.7 fusion.4.place_ref
  138.6 8.5 %collective-permute-done.24.lower_ref = f32[768,128]{1,0:T(8,128)S(1)} collective-permute-done((f32[768,128]{1,0:T(8,128)}, f32[768,128]{1,0:T(8,128)S(1)}, u32[]{:S(2)}, u32[]{:S(2)}) %collective-permute-start.24) | collective-permute-done | bytes 393248 | tf_op jit(solution)/shard_map/ppermute | solution.py:465
  147.2 0.7 copy-done.14
  147.9 6.5 %all-to-all-start.1 = ((f32[64,4,8192]{2,1,0:T(4,128)}), f32[64,4,8192]{2,1,0:T(4,128)}, u32[]{:S(2)}, u32[]{:S(2)}) async-start(f32[64,4,8192]{2,1,0:T(4,128)} %pack_runs.3), calls=%async_computation.1 | async-start | bytes 16777216 | tf_op jit(solution)/shard_map/all_to_all | solution.py:438
  154.4 44.7 %inverse_factor.1 = f32[768,768]{1,0:T(8,128)} custom-call(s32[1]{0:T(128)} %bitcast.col_ref, f32[384,768]{1,0:T(8,128)} %get-tuple-element.51.rows_ref, f32[768,128]{1,0:T(8,128)} %copy-done.14), custom_call_target="tpu_custom_call" | custom-call | flops 199999995904 | bytes 5000000 | tf_op jit(solution)/shard_map/inverse_factor/pallas_call | solution.py:280
  199.3 1.5 copy-done
  200.9 3.1 %convolution_select_fusion = f32[256,768]{1,0:T(8,128)} fusion(f32[768,768]{1,0:T(8,128)S(1)} %copy-done, f32[128,768]{1,0:T(8,128)S(1)} %copy-done.6, f32[128,768]{1,0:T(8,128)S(1)} %copy-done.5, pred[768]{0:T(1024)(128)(4,1)S(1)} %copy-done.13), kind=kOutput, calls=%fused_computation.2 | convolution fusion | flops 1812332544 | bytes 3932928 | tf_op jit(solution)/shard_map/dot_general | solution.py:27
  204.0 2.2 fusion.12
  206.2 3.1 %fusion.13.x_ref = f32[256,768]{1,0:T(8,128)} fusion(f32[256,768]{1,0:T(8,128)S(1)} %fusion.12, f32[768,768]{1,0:T(8,128)S(1)} %copy-done), kind=kOutput, calls=%fused_computation.63 | convolution fusion | flops 1811939328 | bytes 3932160 | tf_op jit(solution)/shard_map/dot_general | solution.py:33
  209.2 21.7 %update_of.1.update_ref = f32[256,8192]{1,0:T(8,128)} custom-call(s32[64]{0:T(128)} %slice_bitcast_fusion.order_ref, f32[256,768]{1,0:T(8,128)} %fusion.13.x_ref, f32[512,768]{1,0:T(8,128)} %copy-done.3, f32[512,768]{1,0:T(8,128)} %collective-permute-done.9.refs_1_, f32[512,768]{1,0:T(8,128)} %copy-done.4, f32[512,768]{1,0:T(8,128)} %collective-permute-done.10.refs_3_, ...), custom_call_target="tpu_custom_call" | custom-call | flops 9663676416 | bytes 34000000 | tf_op jit(solution)/shard_map/update_of/pallas_call | solution.py:362
  230.9 25.7 %all-to-all-done.1.arrived_ref = f32[64,4,8192]{2,1,0:T(4,128)} async-done(((f32[64,4,8192]{2,1,0:T(4,128)}), f32[64,4,8192]{2,1,0:T(4,128)}, u32[]{:S(2)}, u32[]{:S(2)}) %all-to-all-start.1) | async-done | bytes 8388640 | tf_op jit(solution)/shard_map/all_to_all | solution.py:438
  256.6 10.8 %place_rows.1 = f32[256,8192]{1,0:T(8,128)} custom-call(bf16[256,256]{1,0:T(8,128)(2,1)} %fusion.4.place_ref, f32[64,4,8192]{2,1,0:T(4,128)} %all-to-all-done.1.arrived_ref, f32[256,8192]{1,0:T(8,128)} %update_of.1.update_ref), custom_call_target="tpu_custom_call" | custom-call | flops 2147483648 | bytes 25165824 | tf_op jit(solution)/shard_map/place_rows/pallas_call | solution.py:403
  (74 shorter events, 1.5 us)
Async XLA Ops:
  0.6 15.2 %slice-start = ((f32[256,8192]{1,0:T(8,128)}), f32[256,384]{1,0:T(8,128)S(1)}, s32[]{:S(2)}) async-start(f32[256,8192]{1,0:T(8,128)} %rows_ref.1), calls=%async_computation.2 | async-start | bytes 786432 | tf_op jit(solution)/shard_map/slice | solution.py:453
  0.6 14.3 %copy-start.12 = (s32[1,256]{1,0:T(1,128)S(1)}, s32[1,256]{1,0:T(1,128)}, u32[]{:S(2)}) copy-start(s32[1,256]{1,0:T(1,128)} %param.4) | copy-start | bytes 3076
  1.7 8.2 %collective-permute-start.1 = (f32[128,384]{1,0:T(8,128)S(1)}, f32[128,384]{1,0:T(8,128)S(1)}, u32[]{:S(2)}, u32[]{:S(2)}) collective-permute-start(f32[128,384]{1,0:T(8,128)S(1)} %constant_dynamic-slice_fusion.2), channel_id=1, source_target_pairs={{0,1},{1,0},{2,3},{3,2},{4,5},{5,4},{6,7},{7,6},{8,9},{9,8},{10,11... | collective-permute-start | bytes 589832 | tf_op jit(solution)/shard_map/ppermute | solution.py:445
  10.8 6.5 %collective-permute-start = (f32[128,384]{1,0:T(8,128)S(1)}, f32[128,384]{1,0:T(8,128)S(1)}, u32[]{:S(2)}, u32[]{:S(2)}) collective-permute-start(f32[128,384]{1,0:T(8,128)S(1)} %get-tuple-element.59), channel_id=1, source_target_pairs={{0,1},{1,0},{2,3},{3,2},{4,5},{5,4},{6,7},{7,6},{8,9},{9,8},{10,11... | collective-permute-start | bytes 589832 | tf_op jit(solution)/shard_map/ppermute | solution.py:444
  18.3 17.1 %collective-permute-start.3 = (f32[128,768]{1,0:T(8,128)S(1)}, f32[128,768]{1,0:T(8,128)S(1)}, u32[]{:S(2)}, u32[]{:S(2)}) collective-permute-start(f32[128,768]{1,0:T(8,128)S(1)} %slice_dynamic-update-slice_fusion.12), channel_id=1, source_target_pairs={{0,16},{2,18},{4,20},{6,22},{8,24},{10,26},{12,28},{14,30},{16,0},... | collective-permute-start | bytes 1179656 | tf_op jit(solution)/shard_map/ppermute | solution.py:61
  22.9 23.6 %all-to-all-start = ((f32[64,4,512]{2,1,0:T(4,128)}), f32[64,4,512]{2,1,0:T(4,128)S(1)}, u32[]{:S(2)}, u32[]{:S(2)}) async-start(f32[64,4,512]{2,1,0:T(4,128)} %pack_runs.2), calls=%async_computation | async-start | bytes 1048576 | tf_op jit(solution)/shard_map/all_to_all | solution.py:438
  33.9 13.6 %collective-permute-start.2 = (f32[128,768]{1,0:T(8,128)S(1)}, f32[128,768]{1,0:T(8,128)S(1)}, u32[]{:S(2)}, u32[]{:S(2)}) collective-permute-start(f32[128,768]{1,0:T(8,128)S(1)} %slice_dynamic-update-slice_fusion.12), channel_id=1, source_target_pairs={{0,4},{2,34},{4,8},{6,38},{8,12},{10,42},{12,0},{14,46},{16,20},{1... | collective-permute-start | bytes 1179656 | tf_op jit(solution)/shard_map/ppermute | solution.py:61
  35.4 12.2 %collective-permute-start.4 = (f32[128,768]{1,0:T(8,128)S(1)}, f32[128,768]{1,0:T(8,128)S(1)}, u32[]{:S(2)}, u32[]{:S(2)}) collective-permute-start(f32[128,768]{1,0:T(8,128)S(1)} %collective-permute-done.3), channel_id=1, source_target_pairs={{0,12},{2,98},{4,0},{6,102},{8,4},{10,106},{12,8},{14,110},{16,28}... | collective-permute-start | bytes 1179656 | tf_op jit(solution)/shard_map/ppermute | solution.py:61
  36.9 21.2 %collective-permute-start.8 = (f32[128,768]{1,0:T(8,128)S(1)}, f32[128,768]{1,0:T(8,128)}, u32[]{:S(2)}, u32[]{:S(2)}) collective-permute-start(f32[128,768]{1,0:T(8,128)S(1)} %slice_dynamic-update-slice_fusion.12), channel_id=1, source_target_pairs={{0,12},{2,98},{4,0},{6,102},{8,4},{10,106},{12,8},{14,110},{16,28}... | collective-permute-start | bytes 1179656 | tf_op jit(solution)/shard_map/ppermute | solution.py:61
  46.7 75.0 %copy-start.1 = (f32[256,512]{1,0:T(8,128)}, f32[256,512]{1,0:T(8,128)S(1)}, u32[]{:S(2)}) copy-start(f32[256,512]{1,0:T(8,128)S(1)} %reshape.85) | copy-start | bytes 1572868
  46.7 11.4 %collective-permute-start.7 = (f32[128,768]{1,0:T(8,128)S(1)}, f32[128,768]{1,0:T(8,128)S(1)}, u32[]{:S(2)}, u32[]{:S(2)}) collective-permute-start(f32[128,768]{1,0:T(8,128)S(1)} %collective-permute-done.3), channel_id=1, source_target_pairs={{0,4},{2,34},{4,8},{6,38},{8,12},{10,42},{12,0},{14,46},{16,20},{1... | collective-permute-start | bytes 1179656 | tf_op jit(solution)/shard_map/ppermute | solution.py:61
  47.6 10.5 %copy-start.7 = (f32[128,768]{1,0:T(8,128)}, f32[128,768]{1,0:T(8,128)S(1)}, u32[]{:S(2)}) copy-start(f32[128,768]{1,0:T(8,128)S(1)} %collective-permute-done.2) | copy-start | bytes 1179652
  47.6 10.5 %copy-start.8 = (f32[128,768]{1,0:T(8,128)}, f32[128,768]{1,0:T(8,128)S(1)}, u32[]{:S(2)}) copy-start(f32[128,768]{1,0:T(8,128)S(1)} %collective-permute-done.4) | copy-start | bytes 1179652
  47.6 11.5 %collective-permute-start.5 = (f32[128,768]{1,0:T(8,128)S(1)}, f32[128,768]{1,0:T(8,128)S(1)}, u32[]{:S(2)}, u32[]{:S(2)}) collective-permute-start(f32[128,768]{1,0:T(8,128)S(1)} %collective-permute-done.2), channel_id=1, source_target_pairs={{0,4},{2,34},{4,8},{6,38},{8,12},{10,42},{12,0},{14,46},{16,20},{1... | collective-permute-start | bytes 1179656 | tf_op jit(solution)/shard_map/ppermute | solution.py:61
  48.3 11.5 %collective-permute-start.6 = (f32[128,768]{1,0:T(8,128)S(1)}, f32[128,768]{1,0:T(8,128)}, u32[]{:S(2)}, u32[]{:S(2)}) collective-permute-start(f32[128,768]{1,0:T(8,128)S(1)} %collective-permute-done.4), channel_id=1, source_target_pairs={{0,12},{2,98},{4,0},{6,102},{8,4},{10,106},{12,8},{14,110},{16,28}... | collective-permute-start | bytes 1179656 | tf_op jit(solution)/shard_map/ppermute | solution.py:61
  59.1 0.7 copy-start.9
  62.7 58.9 %copy-start.3 = (f32[512,768]{1,0:T(8,128)}, f32[512,768]{1,0:T(8,128)S(1)}, u32[]{:S(2)}) copy-start(f32[512,768]{1,0:T(8,128)S(1)} %get-tuple-element.36.refs_0_) | copy-start | bytes 4718596
  62.7 20.9 %collective-permute-start.9 = (f32[512,768]{1,0:T(8,128)S(1)}, f32[512,768]{1,0:T(8,128)}, u32[]{:S(2)}, u32[]{:S(2)}) collective-permute-start(f32[512,768]{1,0:T(8,128)S(1)} %get-tuple-element.36.refs_0_), channel_id=1, source_target_pairs={{0,32},{2,6},{4,36},{6,10},{8,40},{10,14},{12,44},{14,2},{16,48},{... | collective-permute-start | bytes 4718600 | tf_op jit(solution)/shard_map/ppermute | solution.py:61
  63.0 20.6 %collective-permute-start.11 = (f32[512,768]{1,0:T(8,128)}, f32[512,768]{1,0:T(8,128)}, u32[]{:S(2)}, u32[]{:S(2)}) collective-permute-start(f32[512,768]{1,0:T(8,128)} %get-tuple-element.37.refs_4_), channel_id=1, source_target_pairs={{0,96},{2,14},{4,100},{6,2},{8,104},{10,6},{12,108},{14,10},{16,11... | collective-permute-start | bytes 4718600 | tf_op jit(solution)/shard_map/ppermute | solution.py:61
  65.4 34.4 %collective-permute-start.14 = (f32[512,768]{1,0:T(8,128)S(1)}, f32[512,768]{1,0:T(8,128)S(1)}, u32[]{:S(2)}, u32[]{:S(2)}) collective-permute-start(f32[512,768]{1,0:T(8,128)S(1)} %get-tuple-element.36.refs_0_), channel_id=1, source_target_pairs={{0,96},{2,14},{4,100},{6,2},{8,104},{10,6},{12,108},{14,10},{16,11... | collective-permute-start | bytes 4718600 | tf_op jit(solution)/shard_map/ppermute | solution.py:61
  66.0 37.5 %collective-permute-start.13 = (f32[512,768]{1,0:T(8,128)}, f32[512,768]{1,0:T(8,128)}, u32[]{:S(2)}, u32[]{:S(2)}) collective-permute-start(f32[512,768]{1,0:T(8,128)} %get-tuple-element.37.refs_4_), channel_id=1, source_target_pairs={{0,32},{2,6},{4,36},{6,10},{8,40},{10,14},{12,44},{14,2},{16,48},{... | collective-permute-start | bytes 4718600 | tf_op jit(solution)/shard_map/ppermute | solution.py:61
  83.6 33.7 %collective-permute-start.10 = (f32[512,768]{1,0:T(8,128)}, f32[512,768]{1,0:T(8,128)}, u32[]{:S(2)}, u32[]{:S(2)}) collective-permute-start(f32[512,768]{1,0:T(8,128)} %collective-permute-done.9.refs_1_), channel_id=1, source_target_pairs={{0,32},{2,6},{4,36},{6,10},{8,40},{10,14},{12,44},{14,2},{16,48},{... | collective-permute-start | bytes 4718600 | tf_op jit(solution)/shard_map/ppermute | solution.py:61
  83.6 35.9 %collective-permute-start.12 = (f32[512,768]{1,0:T(8,128)}, f32[512,768]{1,0:T(8,128)}, u32[]{:S(2)}, u32[]{:S(2)}) collective-permute-start(f32[512,768]{1,0:T(8,128)} %collective-permute-done.11.refs_6_), channel_id=1, source_target_pairs={{0,96},{2,14},{4,100},{6,2},{8,104},{10,6},{12,108},{14,10},{16,11... | collective-permute-start | bytes 4718600 | tf_op jit(solution)/shard_map/ppermute | solution.py:61
  86.5 33.0 %collective-permute-start.15 = (f32[512,768]{1,0:T(8,128)S(1)}, f32[512,768]{1,0:T(8,128)}, u32[]{:S(2)}, u32[]{:S(2)}) collective-permute-start(f32[512,768]{1,0:T(8,128)S(1)} %get-tuple-element.36.refs_0_), channel_id=1, source_target_pairs={{0,2},{2,0},{4,6},{6,4},{8,10},{10,8},{12,14},{14,12},{16,18},{18,... | collective-permute-start | bytes 4718600 | tf_op jit(solution)/shard_map/ppermute | solution.py:61
  99.8 1.2 copy-start.4
  101.0 19.0 %collective-permute-start.19 = (f32[512,768]{1,0:T(8,128)}, f32[512,768]{1,0:T(8,128)}, u32[]{:S(2)}, u32[]{:S(2)}) collective-permute-start(f32[512,768]{1,0:T(8,128)} %get-tuple-element.37.refs_4_), channel_id=1, source_target_pairs={{0,2},{2,0},{4,6},{6,4},{8,10},{10,8},{12,14},{14,12},{16,18},{18,... | collective-permute-start | bytes 4718600 | tf_op jit(solution)/shard_map/ppermute | solution.py:61
  103.5 16.6 %collective-permute-start.16 = (f32[512,768]{1,0:T(8,128)}, f32[512,768]{1,0:T(8,128)}, u32[]{:S(2)}, u32[]{:S(2)}) collective-permute-start(f32[512,768]{1,0:T(8,128)} %collective-permute-done.9.refs_1_), channel_id=1, source_target_pairs={{0,2},{2,0},{4,6},{6,4},{8,10},{10,8},{12,14},{14,12},{16,18},{18,... | collective-permute-start | bytes 4718600 | tf_op jit(solution)/shard_map/ppermute | solution.py:61
  117.3 5.6 %collective-permute-start.21 = (f32[512,768]{1,0:T(8,128)}, f32[512,768]{1,0:T(8,128)}, u32[]{:S(2)}, u32[]{:S(2)}) collective-permute-start(f32[512,768]{1,0:T(8,128)} %collective-permute-done.11.refs_6_), channel_id=1, source_target_pairs={{0,2},{2,0},{4,6},{6,4},{8,10},{10,8},{12,14},{14,12},{16,18},{18,... | collective-permute-start | bytes 4718600 | tf_op jit(solution)/shard_map/ppermute | solution.py:61
  119.5 6.2 %collective-permute-start.17 = (f32[512,768]{1,0:T(8,128)}, f32[512,768]{1,0:T(8,128)}, u32[]{:S(2)}, u32[]{:S(2)}) collective-permute-start(f32[512,768]{1,0:T(8,128)} %copy-done.4), channel_id=1, source_target_pairs={{0,2},{2,0},{4,6},{6,4},{8,10},{10,8},{12,14},{14,12},{16,18},{18,... | collective-permute-start | bytes 4718600 | tf_op jit(solution)/shard_map/ppermute | solution.py:61
  119.5 7.9 %collective-permute-start.18 = (f32[512,768]{1,0:T(8,128)}, f32[512,768]{1,0:T(8,128)}, u32[]{:S(2)}, u32[]{:S(2)}) collective-permute-start(f32[512,768]{1,0:T(8,128)} %collective-permute-done.10.refs_3_), channel_id=1, source_target_pairs={{0,2},{2,0},{4,6},{6,4},{8,10},{10,8},{12,14},{14,12},{16,18},{18,... | collective-permute-start | bytes 4718600 | tf_op jit(solution)/shard_map/ppermute | solution.py:61
  120.0 9.6 %collective-permute-start.20 = (f32[512,768]{1,0:T(8,128)}, f32[512,768]{1,0:T(8,128)}, u32[]{:S(2)}, u32[]{:S(2)}) collective-permute-start(f32[512,768]{1,0:T(8,128)} %collective-permute-done.13.refs_5_), channel_id=1, source_target_pairs={{0,2},{2,0},{4,6},{6,4},{8,10},{10,8},{12,14},{14,12},{16,18},{18,... | collective-permute-start | bytes 4718600 | tf_op jit(solution)/shard_map/ppermute | solution.py:61
  120.1 11.8 %collective-permute-start.22 = (f32[512,768]{1,0:T(8,128)}, f32[512,768]{1,0:T(8,128)}, u32[]{:S(2)}, u32[]{:S(2)}) collective-permute-start(f32[512,768]{1,0:T(8,128)} %collective-permute-done.12.refs_7_), channel_id=1, source_target_pairs={{0,2},{2,0},{4,6},{6,4},{8,10},{10,8},{12,14},{14,12},{16,18},{18,... | collective-permute-start | bytes 4718600 | tf_op jit(solution)/shard_map/ppermute | solution.py:61
  122.9 15.7 %collective-permute-start.23 = (f32[256,384]{1,0:T(8,128)S(1)}, f32[256,384]{1,0:T(8,128)S(1)}, u32[]{:S(2)}, u32[]{:S(2)}) collective-permute-start(f32[256,384]{1,0:T(8,128)S(1)} %slice.94), channel_id=1, source_target_pairs={{0,1},{1,0},{2,3},{3,2},{4,5},{5,4},{6,7},{7,6},{8,9},{9,8},{10,11... | collective-permute-start | bytes 1179656 | tf_op jit(solution)/shard_map/ppermute | solution.py:464
  135.0 12.1 %collective-permute-start.24 = (f32[768,128]{1,0:T(8,128)}, f32[768,128]{1,0:T(8,128)S(1)}, u32[]{:S(2)}, u32[]{:S(2)}) collective-permute-start(f32[768,128]{1,0:T(8,128)} %get-tuple-element.54), channel_id=1, source_target_pairs={{0,1},{1,0},{2,3},{3,2},{4,5},{5,4},{6,7},{7,6},{8,9},{9,8},{10,11... | collective-permute-start | bytes 1179656 | tf_op jit(solution)/shard_map/ppermute | solution.py:465
  138.6 8.6 %copy-start.10 = (f32[256,384]{1,0:T(8,128)}, f32[256,384]{1,0:T(8,128)S(1)}, u32[]{:S(2)}) copy-start(f32[256,384]{1,0:T(8,128)S(1)} %collective-permute-done.23) | copy-start | bytes 1179652
  147.2 0.8 copy-start.14
  147.9 108.7 %all-to-all-start.1 = ((f32[64,4,8192]{2,1,0:T(4,128)}), f32[64,4,8192]{2,1,0:T(4,128)}, u32[]{:S(2)}, u32[]{:S(2)}) async-start(f32[64,4,8192]{2,1,0:T(4,128)} %pack_runs.3), calls=%async_computation.1 | async-start | bytes 16777216 | tf_op jit(solution)/shard_map/all_to_all | solution.py:438
  154.4 44.7 %copy-start.2 = (f32[256,512]{1,0:T(8,128)S(1)}, f32[256,512]{1,0:T(8,128)}, u32[]{:S(2)}) copy-start(f32[256,512]{1,0:T(8,128)} %copy-done.1) | copy-start | bytes 1572868
  154.4 44.7 %copy-start.11 = (f32[256,384]{1,0:T(8,128)S(1)}, f32[256,384]{1,0:T(8,128)}, u32[]{:S(2)}) copy-start(f32[256,384]{1,0:T(8,128)} %copy-done.10) | copy-start | bytes 1179652
  199.1 1.7 copy-start
  199.1 1.7 copy-start.5
  199.1 1.8 copy-start.6
  199.1 1.8 copy-start.13

commit v7 on v6

--- a/solution.py
+++ b/solution.py
@@ -80,17 +80,6 @@
         [across, before_across, after_across, far_across],
         beside,
     )
-
-
-def gather_rows(mine, small, runs):
-    near, across, small = ring(mine, move(mine, "y"), "first", small)
-    near, across, runs = lax.optimization_barrier(
-        (jnp.concatenate(near, axis=0), jnp.concatenate(across, axis=0), runs)
-    )
-    near, across, _ = ring(near, across, "second")
-    pieces = near + across
-    runs, *swapped = lax.optimization_barrier((runs, *(move(p, "core") for p in pieces)))
-    return pieces + swapped, small, runs
 
 
 def block_table():
@@ -441,38 +430,47 @@
         return lax.dynamic_slice(front_matrix, (half * BW, 0), (BW, HEAD))
 
     own, others = half_rows(col), half_rows(1 - col)
-    mine = weave(own, lax.ppermute(others, "col", swap), col)
-    theirs = weave(others, lax.ppermute(own, "col", swap), col)
-    panel = jnp.concatenate(
-        [jnp.where(col == 0, mine, theirs), jnp.where(col == 0, theirs, mine)], axis=0
-    )
-
     targets = row_map[0].reshape(N_ROW, CAP)[:, 0] // PW
     within = (row_map[0] % PW).astype(jnp.float32)
     small = jnp.concatenate(
         [front_matrix[:, :HEAD], jnp.broadcast_to(within[:, None], (PW, BW))], axis=1
     )
-    small = send(pack_runs(targets, small, 0, HEAD + BW, HEAD + BW)).reshape(PW, HEAD + BW)
+    small = pack_runs(targets, small, 0, HEAD + BW, HEAD + BW)
+    own_beside, small = lax.optimization_barrier((lax.ppermute(others, "col", swap), small))
+    mine = weave(own, own_beside, col)
+    small = send(small)
+
+    near, across, small = ring(mine, move(mine, "y"), "first", small)
+    sent_rows, goes = small.reshape(PW, HEAD + BW)[:, :HEAD], small.reshape(PW, HEAD + BW)[:, HEAD]
     outgoing = pack_runs(targets, front_matrix, 0, width, 2048)
-    pieces, small, outgoing = gather_rows(mine, small, outgoing)
-
+    near, across, outgoing, own = lax.optimization_barrier(
+        (jnp.concatenate(near, axis=0), jnp.concatenate(across, axis=0), outgoing, own)
+    )
+    panel_beside = lax.ppermute(sent_rows, "col", swap)
+    theirs = weave(others, lax.ppermute(own, "col", swap), col)
+    near, across, _ = ring(near, across, "second")
+    pieces = near + across
+    pieces = pieces + [move(p, "core") for p in pieces]
     table = lax.dynamic_slice_in_dim(jnp.asarray(block_table()), row, 1, 0)[0]
     order, places = table[:N_ROW], table[N_ROW : N_ROW + 8]
     cols = col.reshape(1).astype(jnp.int32)
     rows, square = head_rows(places, cols, pieces)
-    sent_rows = small[:, :HEAD]
-    panel_beside = lax.ppermute(sent_rows, "col", swap)
     square = lax.ppermute(square, "col", swap)
-    outgoing, panel_beside, square = lax.optimization_barrier((outgoing, panel_beside, square))
+    outgoing, square, panel_beside, theirs = lax.optimization_barrier(
+        (outgoing, square, panel_beside, theirs)
+    )
     arrived = send(outgoing)
 
     w = inverse_factor(cols, rows, square)
+    panel = jnp.concatenate(
+        [jnp.where(col == 0, mine, theirs), jnp.where(col == 0, theirs, mine)], axis=0
+    )
     lower = dot_t(weave(sent_rows, panel_beside, col), w)
     update = update_of(order, dot_n(lower, w), pieces, width)
     panel_ids = lax.broadcasted_iota(jnp.int32, (1, PANEL), 1) // PW
     factors = jnp.where(row >= panel_ids, dot_t(panel, w), 0.0)
     slots = jnp.arange(PW, dtype=jnp.int32)
-    goes = small[:, HEAD].astype(jnp.int32)
+    goes = goes.astype(jnp.int32)
     place = (goes[None, :] == slots[:, None]) & (slots[None, :] >= NP * CAP)
     return factors, place_rows(place.astype(jnp.bfloat16), arrived, update)
 

time: 270 us -> 265 us (0.981)
  starting transfers between devices: 54.4 us -> 48.7 us
  local copies, waits for them, and re-layouts: 8.51 us -> 12.7 us
  waiting for transfers between devices: 94.6 us -> 90.7 us
    all_to_all x2, waiting for transfers between devices: 33.9 us -> 25.6 us  [send(): return lax.all_to_all(runs, 'row', split_axis=0, concat_axis=0, tiled=True)]
    ppermute x21, waiting for transfers between devices: 47.3 us -> 55 us  [move(): return lax.ppermute(value, 'row', pairs_of(kind, step))]
    ppermute x1, waiting for transfers between devices: 4.35 us -> 0.01 us  [local(): theirs = weave(others, lax.ppermute(own, 'col', swap), col)]
    ppermute x1, starting transfers between devices: 3.82 us -> 1.01 us  [local(): theirs = weave(others, lax.ppermute(own, 'col', swap), col)]
    unnamed x46 -> x61, local copies, waits for them, and re-layouts: 4.98 us -> 5.78 us
  transfers between devices with their start and end apart: 27 -> 27, of which waited for: 14 -> 9; matrix products, arithmetic and copies ran while one was open for 6% -> 8% of each run, Pallas kernels for 30% -> 30%
where the time goes in v7:
time: 265 us; the launch traced here: 262 us
  waiting for transfers between devices  90.7 us (34%)
  Pallas kernels  90.5 us (34%)
  starting transfers between devices  48.7 us (18%)
  local copies, waits for them, and re-layouts  12.7 us (5%)
  other arithmetic  9.62 us (4%)
  matrix products  8.31 us (3%)
    ppermute x21, waiting for transfers between devices, move(): return lax.ppermute(value, 'row', pairs_of(kind, step))  55 us
    pallas_call x1, Pallas kernels, inverse_factor(): pl.pallas_call(factor_kernel, out_shape=jax.ShapeDtypeStruct((PANEL, PANE...  44.6 us
    all_to_all x2, waiting for transfers between devices, send(): return lax.all_to_all(runs, 'row', split_axis=0, concat_axis=0, tiled=True)  25.6 us
    ppermute x21, starting transfers between devices, move(): return lax.ppermute(value, 'row', pairs_of(kind, step))  23.9 us
    pallas_call x1, Pallas kernels, update_of(): pl.pallas_call(update_kernel, out_shape=jax.ShapeDtypeStruct((PW, width),...  21.6 us
    all_to_all x2, starting transfers between devices, send(): return lax.all_to_all(runs, 'row', split_axis=0, concat_axis=0, tiled=True)  16.8 us
    pallas_call x1, Pallas kernels, place_rows(): pl.pallas_call(functools.partial(place_kernel, tile), out_shape=jax.Shape...  10.8 us
    pallas_call x2, Pallas kernels, pack_runs(): pl.pallas_call(pack_kernel, out_shape=jax.ShapeDtypeStruct((N_ROW, CAP, w...  10.3 us
  transfers between devices with their start and end apart: 27, of which 9 were waited for; matrix products, arithmetic and copies ran while one was open for 8% of the time, Pallas kernels for 30%

profile of v7, /device:TPU:1, one launch (start us, length us, event | category | flops | bytes accessed | tf_op | source)
XLA Modules:
  0.0 261.6 jit_solution(15551077987293171667)
XLA Ops:
  0.6 1.0 constant_dynamic-slice_fusion.1
  1.6 3.8 %collective-permute-start = (f32[128,384]{1,0:T(8,128)S(1)}, f32[128,384]{1,0:T(8,128)S(1)}, u32[]{:S(2)}, u32[]{:S(2)}) collective-permute-start(f32[128,384]{1,0:T(8,128)S(1)} %constant_dynamic-slice_fusion.1), channel_id=1, source_target_pairs={{0,1},{1,0},{2,3},{3,2},{4,5},{5,4},{6,7},{7,6},{8,9},{9,8},{10,11... | collective-permute-start | bytes 589832 | tf_op jit(solution)/shard_map/ppermute | solution.py:439
  5.5 0.5 broadcast.94
  6.0 1.3 reduce.5
  7.3 0.7 fusion.9
  8.3 0.9 pad_maximum_fusion.2.rows_ref
  9.2 0.6 and_select_fusion.1.slot_ref
  9.8 2.5 pack_runs.2
  12.3 1.0 broadcast_select_fusion.6
  13.4 0.5 copy-done.9
  14.0 0.4 collective-permute-start.2
  14.4 10.3 %all-to-all-start = ((f32[64,4,512]{2,1,0:T(4,128)}), f32[64,4,512]{2,1,0:T(4,128)S(1)}, u32[]{:S(2)}, u32[]{:S(2)}) async-start(f32[64,4,512]{2,1,0:T(4,128)} %pack_runs.2), calls=%async_computation | async-start | bytes 1048576 | tf_op jit(solution)/shard_map/all_to_all | solution.py:427
  24.7 1.5 collective-permute-start.1
  26.2 1.5 collective-permute-start.3
  27.7 1.4 collective-permute-start.7
  29.2 9.5 %collective-permute-done.1 = f32[128,768]{1,0:T(8,128)S(1)} collective-permute-done((f32[128,768]{1,0:T(8,128)S(1)}, f32[128,768]{1,0:T(8,128)S(1)}, u32[]{:S(2)}, u32[]{:S(2)}) %collective-permute-start.1) | collective-permute-done | bytes 393248 | tf_op jit(solution)/shard_map/ppermute | solution.py:61
  38.7 0.3 collective-permute-start.4
  39.0 2.4 collective-permute-start.5
  41.4 7.8 %pack_runs.3 = f32[64,4,8192]{2,1,0:T(4,128)} custom-call(s32[64]{0:T(128)} %and_select_fusion.1.slot_ref, f32[256,8192]{1,0:T(8,128)} %rows_ref.1), custom_call_target="tpu_custom_call" | custom-call | bytes 16777216 | tf_op jit(solution)/shard_map/pack_runs/pallas_call | solution.py:108
  49.3 0.7 copy-done.15
  50.1 1.8 pad_maximum_fusion
  51.9 1.0 collective-permute-start.8
  52.9 1.8 collective-permute-start.10
  54.7 1.2 collective-permute-start.13
  55.9 0.3 collective-permute-start.12
  56.1 16.7 %collective-permute-done.8.refs_1_ = f32[512,768]{1,0:T(8,128)} collective-permute-done((f32[512,768]{1,0:T(8,128)S(1)}, f32[512,768]{1,0:T(8,128)}, u32[]{:S(2)}, u32[]{:S(2)}) %collective-permute-start.8) | collective-permute-done | bytes 1572896 | tf_op jit(solution)/shard_map/ppermute | solution.py:61
  72.9 2.7 %collective-permute-start.11 = (f32[512,768]{1,0:T(8,128)}, f32[512,768]{1,0:T(8,128)}, u32[]{:S(2)}, u32[]{:S(2)}) collective-permute-start(f32[512,768]{1,0:T(8,128)} %collective-permute-done.10.refs_6_), channel_id=1, source_target_pairs={{0,96},{2,14},{4,100},{6,2},{8,104},{10,6},{12,108},{14,10},{16,11... | collective-permute-start | bytes 4718600 | tf_op jit(solution)/shard_map/ppermute | solution.py:61
  75.6 2.0 collective-permute-start.14
  77.5 11.8 %collective-permute-done.13.refs_2_ = f32[512,768]{1,0:T(8,128)S(1)} collective-permute-done((f32[512,768]{1,0:T(8,128)S(1)}, f32[512,768]{1,0:T(8,128)S(1)}, u32[]{:S(2)}, u32[]{:S(2)}) %collective-permute-start.13) | collective-permute-done | bytes 1572896 | tf_op jit(solution)/shard_map/ppermute | solution.py:61
  89.3 2.0 collective-permute-start.18
  91.3 1.2 copy-done.8
  92.5 1.1 collective-permute-start.15
  93.7 0.7 constant_dynamic-slice_fusion
  94.4 0.6 fusion.5
  95.0 0.5 slice_bitcast_fusion.order_ref
  95.5 11.1 %collective-permute-done.9.refs_3_ = f32[512,768]{1,0:T(8,128)} collective-permute-done((f32[512,768]{1,0:T(8,128)}, f32[512,768]{1,0:T(8,128)}, u32[]{:S(2)}, u32[]{:S(2)}) %collective-permute-start.9) | collective-permute-done | bytes 1572896 | tf_op jit(solution)/shard_map/ppermute | solution.py:61
  106.6 1.0 collective-permute-start.24
  107.6 0.6 slice_bitcast_fusion.1.place_ref
  108.2 2.0 reshape.86
  110.2 1.8 slice.111
  112.0 1.7 collective-permute-start.20
  113.7 1.9 collective-permute-start.16
  115.7 0.4 collective-permute-start.19
  116.3 0.9 slice_convert_fusion
  117.3 0.7 fusion.4.place_ref
  118.0 1.0 broadcast_select_fusion.4
  119.1 1.1 collective-permute-start.23
  120.2 1.4 collective-permute-done.17.refs_11_
  121.6 2.2 collective-permute-done.19.refs_13_
  123.8 2.2 collective-permute-done.21.refs_15_
  126.1 3.1 %head_rows.1 = (f32[384,768]{1,0:T(8,128)}, f32[768,128]{1,0:T(8,128)}) custom-call(s32[8]{0:T(128)} %slice_bitcast_fusion.1.place_ref, s32[1]{0:T(128)} %bitcast.2.col_ref, f32[512,768]{1,0:T(8,128)} %copy-done.1, f32[512,768]{1,0:T(8,128)} %collective-permute-done.8.refs_1_, f32[512,768]{1,0:T(8,128)} %copy-done.7, ...), custom_call_target="tpu_custom_call" | custom-call | bytes 4000000 | tf_op jit(solution)/shard_map/head_rows/pallas_call | solution.py:154
  129.2 2.0 collective-permute-start.22
  131.3 10.1 %collective-permute-done.22.lower_ref = f32[768,128]{1,0:T(8,128)S(1)} collective-permute-done((f32[768,128]{1,0:T(8,128)}, f32[768,128]{1,0:T(8,128)S(1)}, u32[]{:S(2)}, u32[]{:S(2)}) %collective-permute-start.22) | collective-permute-done | bytes 393248 | tf_op jit(solution)/shard_map/ppermute | solution.py:458
  141.4 0.7 copy-done.21
  142.1 6.5 %all-to-all-start.1 = ((f32[64,4,8192]{2,1,0:T(4,128)}), f32[64,4,8192]{2,1,0:T(4,128)}, u32[]{:S(2)}, u32[]{:S(2)}) async-start(f32[64,4,8192]{2,1,0:T(4,128)} %pack_runs.3), calls=%async_computation.1 | async-start | bytes 16777216 | tf_op jit(solution)/shard_map/all_to_all | solution.py:427
  148.6 44.6 %inverse_factor.1 = f32[768,768]{1,0:T(8,128)} custom-call(s32[1]{0:T(128)} %bitcast.2.col_ref, f32[384,768]{1,0:T(8,128)} %get-tuple-element.44.rows_ref, f32[768,128]{1,0:T(8,128)} %copy-done.21), custom_call_target="tpu_custom_call" | custom-call | flops 199999995904 | bytes 5000000 | tf_op jit(solution)/shard_map/inverse_factor/pallas_call | solution.py:269
  193.5 0.8 copy-done.6
  194.4 0.8 copy-done
  195.2 3.1 %convolution_select_fusion = f32[256,768]{1,0:T(8,128)} fusion(f32[768,768]{1,0:T(8,128)S(1)} %copy-done, f32[128,768]{1,0:T(8,128)S(1)} %get-tuple-element.53, f32[128,768]{1,0:T(8,128)S(1)} %get-tuple-element.52, pred[768]{0:T(1024)(128)(4,1)S(1)} %copy-done.20), kind=kOutput, calls=%fused_computation.2 | convolution fusion | flops 1812332544 | bytes 3932928 | tf_op jit(solution)/shard_map/dot_general | solution.py:27
  198.3 2.2 fusion.12
  200.5 3.1 %fusion.13.x_ref = f32[256,768]{1,0:T(8,128)} fusion(f32[256,768]{1,0:T(8,128)S(1)} %fusion.12, f32[768,768]{1,0:T(8,128)S(1)} %copy-done), kind=kOutput, calls=%fused_computation.63 | convolution fusion | flops 1811939328 | bytes 3932160 | tf_op jit(solution)/shard_map/dot_general | solution.py:33
  203.5 21.6 %update_of.1.update_ref = f32[256,8192]{1,0:T(8,128)} custom-call(s32[64]{0:T(128)} %slice_bitcast_fusion.order_ref, f32[256,768]{1,0:T(8,128)} %fusion.13.x_ref, f32[512,768]{1,0:T(8,128)} %copy-done.1, f32[512,768]{1,0:T(8,128)} %collective-permute-done.8.refs_1_, f32[512,768]{1,0:T(8,128)} %copy-done.7, f32[512,768]{1,0:T(8,128)} %collective-permute-done.9.refs_3_, ...), custom_call_target="tpu_custom_call" | custom-call | flops 9663676416 | bytes 34000000 | tf_op jit(solution)/shard_map/update_of/pallas_call | solution.py:351
  225.2 25.6 %all-to-all-done.1.arrived_ref = f32[64,4,8192]{2,1,0:T(4,128)} async-done(((f32[64,4,8192]{2,1,0:T(4,128)}), f32[64,4,8192]{2,1,0:T(4,128)}, u32[]{:S(2)}, u32[]{:S(2)}) %all-to-all-start.1) | async-done | bytes 8388640 | tf_op jit(solution)/shard_map/all_to_all | solution.py:427
  250.8 10.8 %place_rows.1 = f32[256,8192]{1,0:T(8,128)} custom-call(bf16[256,256]{1,0:T(8,128)(2,1)} %fusion.4.place_ref, f32[64,4,8192]{2,1,0:T(4,128)} %all-to-all-done.1.arrived_ref, f32[256,8192]{1,0:T(8,128)} %update_of.1.update_ref), custom_call_target="tpu_custom_call" | custom-call | flops 2147483648 | bytes 25165824 | tf_op jit(solution)/shard_map/place_rows/pallas_call | solution.py:392
  (88 shorter events, 1.4 us)
Async XLA Ops:
  0.6 7.7 %slice-start = ((f32[256,8192]{1,0:T(8,128)}), f32[256,384]{1,0:T(8,128)S(1)}, s32[]{:S(2)}) async-start(f32[256,8192]{1,0:T(8,128)} %rows_ref.1), calls=%async_computation.2 | async-start | bytes 786432 | tf_op jit(solution)/shard_map/slice | solution.py:436
  1.6 10.7 %collective-permute-start = (f32[128,384]{1,0:T(8,128)S(1)}, f32[128,384]{1,0:T(8,128)S(1)}, u32[]{:S(2)}, u32[]{:S(2)}) collective-permute-start(f32[128,384]{1,0:T(8,128)S(1)} %constant_dynamic-slice_fusion.1), channel_id=1, source_target_pairs={{0,1},{1,0},{2,3},{3,2},{4,5},{5,4},{6,7},{7,6},{8,9},{9,8},{10,11... | collective-permute-start | bytes 589832 | tf_op jit(solution)/shard_map/ppermute | solution.py:439
  13.3 0.7 copy-start.9
  14.0 36.1 %copy-start.5 = (f32[128,768]{1,0:T(8,128)}, f32[128,768]{1,0:T(8,128)S(1)}, u32[]{:S(2)}) copy-start(f32[128,768]{1,0:T(8,128)S(1)} %slice_dynamic-update-slice_fusion.12) | copy-start | bytes 1179652
  14.0 12.2 %collective-permute-start.2 = (f32[128,768]{1,0:T(8,128)S(1)}, f32[128,768]{1,0:T(8,128)S(1)}, u32[]{:S(2)}, u32[]{:S(2)}) collective-permute-start(f32[128,768]{1,0:T(8,128)S(1)} %slice_dynamic-update-slice_fusion.12), channel_id=1, source_target_pairs={{0,16},{2,18},{4,20},{6,22},{8,24},{10,26},{12,28},{14,30},{16,0},... | collective-permute-start | bytes 1179656 | tf_op jit(solution)/shard_map/ppermute | solution.py:61
  14.4 24.3 %all-to-all-start = ((f32[64,4,512]{2,1,0:T(4,128)}), f32[64,4,512]{2,1,0:T(4,128)S(1)}, u32[]{:S(2)}, u32[]{:S(2)}) async-start(f32[64,4,512]{2,1,0:T(4,128)} %pack_runs.2), calls=%async_computation | async-start | bytes 1048576 | tf_op jit(solution)/shard_map/all_to_all | solution.py:427
  24.7 13.9 %collective-permute-start.1 = (f32[128,768]{1,0:T(8,128)S(1)}, f32[128,768]{1,0:T(8,128)S(1)}, u32[]{:S(2)}, u32[]{:S(2)}) collective-permute-start(f32[128,768]{1,0:T(8,128)S(1)} %slice_dynamic-update-slice_fusion.12), channel_id=1, source_target_pairs={{0,4},{2,34},{4,8},{6,38},{8,12},{10,42},{12,0},{14,46},{16,20},{1... | collective-permute-start | bytes 1179656 | tf_op jit(solution)/shard_map/ppermute | solution.py:61
  26.2 23.0 %copy-start.12 = (f32[128,768]{1,0:T(8,128)}, f32[128,768]{1,0:T(8,128)S(1)}, u32[]{:S(2)}) copy-start(f32[128,768]{1,0:T(8,128)S(1)} %collective-permute-done.2) | copy-start | bytes 1179652
  26.2 12.5 %collective-permute-start.3 = (f32[128,768]{1,0:T(8,128)S(1)}, f32[128,768]{1,0:T(8,128)S(1)}, u32[]{:S(2)}, u32[]{:S(2)}) collective-permute-start(f32[128,768]{1,0:T(8,128)S(1)} %collective-permute-done.2), channel_id=1, source_target_pairs={{0,12},{2,98},{4,0},{6,102},{8,4},{10,106},{12,8},{14,110},{16,28}... | collective-permute-start | bytes 1179656 | tf_op jit(solution)/shard_map/ppermute | solution.py:61
  27.7 21.5 %collective-permute-start.7 = (f32[128,768]{1,0:T(8,128)S(1)}, f32[128,768]{1,0:T(8,128)S(1)}, u32[]{:S(2)}, u32[]{:S(2)}) collective-permute-start(f32[128,768]{1,0:T(8,128)S(1)} %slice_dynamic-update-slice_fusion.12), channel_id=1, source_target_pairs={{0,12},{2,98},{4,0},{6,102},{8,4},{10,106},{12,8},{14,110},{16,28}... | collective-permute-start | bytes 1179656 | tf_op jit(solution)/shard_map/ppermute | solution.py:61
  29.1 20.2 %collective-permute-start.6 = (f32[128,768]{1,0:T(8,128)S(1)}, f32[128,768]{1,0:T(8,128)S(1)}, u32[]{:S(2)}, u32[]{:S(2)}) collective-permute-start(f32[128,768]{1,0:T(8,128)S(1)} %collective-permute-done.2), channel_id=1, source_target_pairs={{0,4},{2,34},{4,8},{6,38},{8,12},{10,42},{12,0},{14,46},{16,20},{1... | collective-permute-start | bytes 1179656 | tf_op jit(solution)/shard_map/ppermute | solution.py:61
  38.6 10.6 %copy-start.13 = (f32[128,768]{1,0:T(8,128)}, f32[128,768]{1,0:T(8,128)S(1)}, u32[]{:S(2)}) copy-start(f32[128,768]{1,0:T(8,128)S(1)} %collective-permute-done.1) | copy-start | bytes 1179652
  38.6 10.6 %copy-start.4 = (f32[64,4,512]{2,1,0:T(4,128)}, f32[64,4,512]{2,1,0:T(4,128)S(1)}, u32[]{:S(2)}) copy-start(f32[64,4,512]{2,1,0:T(4,128)S(1)} %all-to-all-done) | copy-start | bytes 1572868
  38.6 10.6 %copy-start.14 = (f32[128,768]{1,0:T(8,128)}, f32[128,768]{1,0:T(8,128)S(1)}, u32[]{:S(2)}) copy-start(f32[128,768]{1,0:T(8,128)S(1)} %collective-permute-done.3) | copy-start | bytes 1179652
  38.7 10.6 %collective-permute-start.4 = (f32[128,768]{1,0:T(8,128)S(1)}, f32[128,768]{1,0:T(8,128)S(1)}, u32[]{:S(2)}, u32[]{:S(2)}) collective-permute-start(f32[128,768]{1,0:T(8,128)S(1)} %collective-permute-done.1), channel_id=1, source_target_pairs={{0,4},{2,34},{4,8},{6,38},{8,12},{10,42},{12,0},{14,46},{16,20},{1... | collective-permute-start | bytes 1179656 | tf_op jit(solution)/shard_map/ppermute | solution.py:61
  39.0 11.1 %collective-permute-start.5 = (f32[128,768]{1,0:T(8,128)S(1)}, f32[128,768]{1,0:T(8,128)}, u32[]{:S(2)}, u32[]{:S(2)}) collective-permute-start(f32[128,768]{1,0:T(8,128)S(1)} %collective-permute-done.3), channel_id=1, source_target_pairs={{0,12},{2,98},{4,0},{6,102},{8,4},{10,106},{12,8},{14,110},{16,28}... | collective-permute-start | bytes 1179656 | tf_op jit(solution)/shard_map/ppermute | solution.py:61
  49.2 0.7 copy-start.15
  49.2 0.9 copy-start.16
  51.9 67.1 %copy-start.1 = (f32[512,768]{1,0:T(8,128)}, f32[512,768]{1,0:T(8,128)S(1)}, u32[]{:S(2)}) copy-start(f32[512,768]{1,0:T(8,128)S(1)} %get-tuple-element.34.refs_0_) | copy-start | bytes 4718596
  51.9 67.1 %copy-start.2 = (f32[512,768]{1,0:T(8,128)}, f32[512,768]{1,0:T(8,128)S(1)}, u32[]{:S(2)}) copy-start(f32[512,768]{1,0:T(8,128)S(1)} %get-tuple-element.35.refs_4_) | copy-start | bytes 4718596
  51.9 20.9 %collective-permute-start.8 = (f32[512,768]{1,0:T(8,128)S(1)}, f32[512,768]{1,0:T(8,128)}, u32[]{:S(2)}, u32[]{:S(2)}) collective-permute-start(f32[512,768]{1,0:T(8,128)S(1)} %get-tuple-element.34.refs_0_), channel_id=1, source_target_pairs={{0,32},{2,6},{4,36},{6,10},{8,40},{10,14},{12,44},{14,2},{16,48},{... | collective-permute-start | bytes 4718600 | tf_op jit(solution)/shard_map/ppermute | solution.py:61
  52.9 20.0 %collective-permute-start.10 = (f32[512,768]{1,0:T(8,128)S(1)}, f32[512,768]{1,0:T(8,128)}, u32[]{:S(2)}, u32[]{:S(2)}) collective-permute-start(f32[512,768]{1,0:T(8,128)S(1)} %get-tuple-element.35.refs_4_), channel_id=1, source_target_pairs={{0,96},{2,14},{4,100},{6,2},{8,104},{10,6},{12,108},{14,10},{16,11... | collective-permute-start | bytes 4718600 | tf_op jit(solution)/shard_map/ppermute | solution.py:61
  54.7 34.6 %collective-permute-start.13 = (f32[512,768]{1,0:T(8,128)S(1)}, f32[512,768]{1,0:T(8,128)S(1)}, u32[]{:S(2)}, u32[]{:S(2)}) collective-permute-start(f32[512,768]{1,0:T(8,128)S(1)} %get-tuple-element.34.refs_0_), channel_id=1, source_target_pairs={{0,96},{2,14},{4,100},{6,2},{8,104},{10,6},{12,108},{14,10},{16,11... | collective-permute-start | bytes 4718600 | tf_op jit(solution)/shard_map/ppermute | solution.py:61
  55.9 35.5 %collective-permute-start.12 = (f32[512,768]{1,0:T(8,128)S(1)}, f32[512,768]{1,0:T(8,128)S(1)}, u32[]{:S(2)}, u32[]{:S(2)}) collective-permute-start(f32[512,768]{1,0:T(8,128)S(1)} %get-tuple-element.35.refs_4_), channel_id=1, source_target_pairs={{0,32},{2,6},{4,36},{6,10},{8,40},{10,14},{12,44},{14,2},{16,48},{... | collective-permute-start | bytes 4718600 | tf_op jit(solution)/shard_map/ppermute | solution.py:61
  72.9 33.7 %collective-permute-start.9 = (f32[512,768]{1,0:T(8,128)}, f32[512,768]{1,0:T(8,128)}, u32[]{:S(2)}, u32[]{:S(2)}) collective-permute-start(f32[512,768]{1,0:T(8,128)} %collective-permute-done.8.refs_1_), channel_id=1, source_target_pairs={{0,32},{2,6},{4,36},{6,10},{8,40},{10,14},{12,44},{14,2},{16,48},{... | collective-permute-start | bytes 4718600 | tf_op jit(solution)/shard_map/ppermute | solution.py:61
  72.9 39.1 %collective-permute-start.11 = (f32[512,768]{1,0:T(8,128)}, f32[512,768]{1,0:T(8,128)}, u32[]{:S(2)}, u32[]{:S(2)}) collective-permute-start(f32[512,768]{1,0:T(8,128)} %collective-permute-done.10.refs_6_), channel_id=1, source_target_pairs={{0,96},{2,14},{4,100},{6,2},{8,104},{10,6},{12,108},{14,10},{16,11... | collective-permute-start | bytes 4718600 | tf_op jit(solution)/shard_map/ppermute | solution.py:61
  75.6 40.1 %collective-permute-start.14 = (f32[512,768]{1,0:T(8,128)S(1)}, f32[512,768]{1,0:T(8,128)}, u32[]{:S(2)}, u32[]{:S(2)}) collective-permute-start(f32[512,768]{1,0:T(8,128)S(1)} %get-tuple-element.34.refs_0_), channel_id=1, source_target_pairs={{0,2},{2,0},{4,6},{6,4},{8,10},{10,8},{12,14},{14,12},{16,18},{18,... | collective-permute-start | bytes 4718600 | tf_op jit(solution)/shard_map/ppermute | solution.py:61
  89.3 2.0 copy-start.7
  89.3 26.4 %collective-permute-start.18 = (f32[512,768]{1,0:T(8,128)S(1)}, f32[512,768]{1,0:T(8,128)}, u32[]{:S(2)}, u32[]{:S(2)}) collective-permute-start(f32[512,768]{1,0:T(8,128)S(1)} %get-tuple-element.35.refs_4_), channel_id=1, source_target_pairs={{0,2},{2,0},{4,6},{6,4},{8,10},{10,8},{12,14},{14,12},{16,18},{18,... | collective-permute-start | bytes 4718600 | tf_op jit(solution)/shard_map/ppermute | solution.py:61
  91.3 1.2 copy-start.8
  92.5 23.6 %collective-permute-start.15 = (f32[512,768]{1,0:T(8,128)}, f32[512,768]{1,0:T(8,128)}, u32[]{:S(2)}, u32[]{:S(2)}) collective-permute-start(f32[512,768]{1,0:T(8,128)} %collective-permute-done.8.refs_1_), channel_id=1, source_target_pairs={{0,2},{2,0},{4,6},{6,4},{8,10},{10,8},{12,14},{14,12},{16,18},{18,... | collective-permute-start | bytes 4718600 | tf_op jit(solution)/shard_map/ppermute | solution.py:61
  106.6 7.1 %collective-permute-start.24 = (f32[128,384]{1,0:T(8,128)}, f32[128,384]{1,0:T(8,128)S(1)}, u32[]{:S(2)}, u32[]{:S(2)}) collective-permute-start(f32[128,384]{1,0:T(8,128)} %copy-done.9), channel_id=1, source_target_pairs={{0,1},{1,0},{2,3},{3,2},{4,5},{5,4},{6,7},{7,6},{8,9},{9,8},{10,11... | collective-permute-start | bytes 589832 | tf_op jit(solution)/shard_map/ppermute | solution.py:450
  112.0 7.1 %collective-permute-start.20 = (f32[512,768]{1,0:T(8,128)}, f32[512,768]{1,0:T(8,128)}, u32[]{:S(2)}, u32[]{:S(2)}) collective-permute-start(f32[512,768]{1,0:T(8,128)} %collective-permute-done.10.refs_6_), channel_id=1, source_target_pairs={{0,2},{2,0},{4,6},{6,4},{8,10},{10,8},{12,14},{14,12},{16,18},{18,... | collective-permute-start | bytes 4718600 | tf_op jit(solution)/shard_map/ppermute | solution.py:61
  113.7 2.4 copy-start.19
  113.7 6.5 %collective-permute-start.16 = (f32[512,768]{1,0:T(8,128)}, f32[512,768]{1,0:T(8,128)}, u32[]{:S(2)}, u32[]{:S(2)}) collective-permute-start(f32[512,768]{1,0:T(8,128)} %copy-done.7), channel_id=1, source_target_pairs={{0,2},{2,0},{4,6},{6,4},{8,10},{10,8},{12,14},{14,12},{16,18},{18,... | collective-permute-start | bytes 4718600 | tf_op jit(solution)/shard_map/ppermute | solution.py:61
  115.6 6.0 %collective-permute-start.17 = (f32[512,768]{1,0:T(8,128)}, f32[512,768]{1,0:T(8,128)}, u32[]{:S(2)}, u32[]{:S(2)}) collective-permute-start(f32[512,768]{1,0:T(8,128)} %collective-permute-done.9.refs_3_), channel_id=1, source_target_pairs={{0,2},{2,0},{4,6},{6,4},{8,10},{10,8},{12,14},{14,12},{16,18},{18,... | collective-permute-start | bytes 4718600 | tf_op jit(solution)/shard_map/ppermute | solution.py:61
  115.7 8.1 %collective-permute-start.19 = (f32[512,768]{1,0:T(8,128)}, f32[512,768]{1,0:T(8,128)}, u32[]{:S(2)}, u32[]{:S(2)}) collective-permute-start(f32[512,768]{1,0:T(8,128)} %copy-done.8), channel_id=1, source_target_pairs={{0,2},{2,0},{4,6},{6,4},{8,10},{10,8},{12,14},{14,12},{16,18},{18,... | collective-permute-start | bytes 4718600 | tf_op jit(solution)/shard_map/ppermute | solution.py:61
  116.1 9.9 %collective-permute-start.21 = (f32[512,768]{1,0:T(8,128)}, f32[512,768]{1,0:T(8,128)}, u32[]{:S(2)}, u32[]{:S(2)}) collective-permute-start(f32[512,768]{1,0:T(8,128)} %collective-permute-done.11.refs_7_), channel_id=1, source_target_pairs={{0,2},{2,0},{4,6},{6,4},{8,10},{10,8},{12,14},{14,12},{16,18},{18,... | collective-permute-start | bytes 4718600 | tf_op jit(solution)/shard_map/ppermute | solution.py:61
  119.1 12.1 %collective-permute-start.23 = (f32[256,384]{1,0:T(8,128)}, f32[256,384]{1,0:T(8,128)S(1)}, u32[]{:S(2)}, u32[]{:S(2)}) collective-permute-start(f32[256,384]{1,0:T(8,128)} %slice.111), channel_id=1, source_target_pairs={{0,1},{1,0},{2,3},{3,2},{4,5},{5,4},{6,7},{7,6},{8,9},{9,8},{10,11... | collective-permute-start | bytes 1179656 | tf_op jit(solution)/shard_map/ppermute | solution.py:449
  129.2 12.1 %collective-permute-start.22 = (f32[768,128]{1,0:T(8,128)}, f32[768,128]{1,0:T(8,128)S(1)}, u32[]{:S(2)}, u32[]{:S(2)}) collective-permute-start(f32[768,128]{1,0:T(8,128)} %get-tuple-element.40), channel_id=1, source_target_pairs={{0,1},{1,0},{2,3},{3,2},{4,5},{5,4},{6,7},{7,6},{8,9},{9,8},{10,11... | collective-permute-start | bytes 1179656 | tf_op jit(solution)/shard_map/ppermute | solution.py:458
  131.3 10.1 %copy-start.10 = (f32[128,768]{1,0:T(8,128)}, f32[128,768]{1,0:T(8,128)S(1)}, u32[]{:S(2)}) copy-start(f32[128,768]{1,0:T(8,128)S(1)} %slice_dynamic-update-slice_fusion.6) | copy-start | bytes 1179652
  131.3 10.1 %copy-start.17 = (f32[256,384]{1,0:T(8,128)}, f32[256,384]{1,0:T(8,128)S(1)}, u32[]{:S(2)}) copy-start(f32[256,384]{1,0:T(8,128)S(1)} %collective-permute-done.23) | copy-start | bytes 1179652
  141.4 0.7 copy-start.21
  142.1 108.7 %all-to-all-start.1 = ((f32[64,4,8192]{2,1,0:T(4,128)}), f32[64,4,8192]{2,1,0:T(4,128)}, u32[]{:S(2)}, u32[]{:S(2)}) async-start(f32[64,4,8192]{2,1,0:T(4,128)} %pack_runs.3), calls=%async_computation.1 | async-start | bytes 16777216 | tf_op jit(solution)/shard_map/all_to_all | solution.py:427
  148.6 44.6 %copy-start.3 = (f32[256,512]{1,0:T(8,128)S(1)}, f32[256,512]{1,0:T(8,128)}, u32[]{:S(2)}) copy-start(f32[256,512]{1,0:T(8,128)} %reshape.86) | copy-start | bytes 1572868
  148.6 44.6 %copy-start.18 = (f32[256,384]{1,0:T(8,128)S(1)}, f32[256,384]{1,0:T(8,128)}, u32[]{:S(2)}) copy-start(f32[256,384]{1,0:T(8,128)} %copy-done.17) | copy-start | bytes 1179652
  193.3 1.0 copy-start.6
  193.3 1.1 copy-start.11
  193.3 1.9 copy-start
  193.3 1.9 copy-start.20

commit v8 on v7

--- a/solution.py
+++ b/solution.py
@@ -442,10 +442,10 @@
 
     near, across, small = ring(mine, move(mine, "y"), "first", small)
     sent_rows, goes = small.reshape(PW, HEAD + BW)[:, :HEAD], small.reshape(PW, HEAD + BW)[:, HEAD]
+    near, across, targets, own = lax.optimization_barrier(
+        (jnp.concatenate(near, axis=0), jnp.concatenate(across, axis=0), targets, own)
+    )
     outgoing = pack_runs(targets, front_matrix, 0, width, 2048)
-    near, across, outgoing, own = lax.optimization_barrier(
-        (jnp.concatenate(near, axis=0), jnp.concatenate(across, axis=0), outgoing, own)
-    )
     panel_beside = lax.ppermute(sent_rows, "col", swap)
     theirs = weave(others, lax.ppermute(own, "col", swap), col)
     near, across, _ = ring(near, across, "second")

time: 265 us -> 270 us (1.019)
  waiting for transfers between devices: 90.7 us -> 94.2 us
    ppermute x1, waiting for transfers between devices: 0.01 us -> 5.81 us  [local(): panel_beside = lax.ppermute(sent_rows, 'col', swap)]
    unnamed x61 -> x63, local copies, waits for them, and re-layouts: 5.78 us -> 4.95 us
  transfers between devices with their start and end apart: 27 -> 27, of which waited for: 9 -> 10; matrix products, arithmetic and copies ran while one was open for 8% -> 8% of each run, Pallas kernels for 30% -> 30%
where the time goes in v8:
time: 270 us; the launch traced here: 267 us
  waiting for transfers between devices  94.2 us (35%)
  Pallas kernels  90.7 us (34%)
  starting transfers between devices  50.9 us (19%)
  local copies, waits for them, and re-layouts  11.9 us (4%)
  other arithmetic  9.36 us (3%)
  matrix products  8.32 us (3%)
    ppermute x21, waiting for transfers between devices, move(): return lax.ppermute(value, 'row', pairs_of(kind, step))  54.5 us
    pallas_call x1, Pallas kernels, inverse_factor(): pl.pallas_call(factor_kernel, out_shape=jax.ShapeDtypeStruct((PANEL, PANE...  44.6 us
    all_to_all x2, waiting for transfers between devices, send(): return lax.all_to_all(runs, 'row', split_axis=0, concat_axis=0, tiled=True)  25.5 us
    ppermute x21, starting transfers between devices, move(): return lax.ppermute(value, 'row', pairs_of(kind, step))  24 us
    pallas_call x1, Pallas kernels, update_of(): pl.pallas_call(update_kernel, out_shape=jax.ShapeDtypeStruct((PW, width),...  21.7 us
    all_to_all x2, starting transfers between devices, send(): return lax.all_to_all(runs, 'row', split_axis=0, concat_axis=0, tiled=True)  18.9 us
    pallas_call x1, Pallas kernels, place_rows(): pl.pallas_call(functools.partial(place_kernel, tile), out_shape=jax.Shape...  10.8 us
    pallas_call x2, Pallas kernels, pack_runs(): pl.pallas_call(pack_kernel, out_shape=jax.ShapeDtypeStruct((N_ROW, CAP, w...  10.5 us
  transfers between devices with their start and end apart: 27, of which 10 were waited for; matrix products, arithmetic and copies ran while one was open for 8% of the time, Pallas kernels for 30%

profile of v8, /device:TPU:1, one launch (start us, length us, event | category | flops | bytes accessed | tf_op | source)
XLA Modules:
  0.0 266.5 jit_solution(9344113125095213354)
XLA Ops:
  0.6 1.0 constant_dynamic-slice_fusion.1
  1.6 3.8 %collective-permute-start = (f32[128,384]{1,0:T(8,128)S(1)}, f32[128,384]{1,0:T(8,128)S(1)}, u32[]{:S(2)}, u32[]{:S(2)}) collective-permute-start(f32[128,384]{1,0:T(8,128)S(1)} %constant_dynamic-slice_fusion.1), channel_id=1, source_target_pairs={{0,1},{1,0},{2,3},{3,2},{4,5},{5,4},{6,7},{7,6},{8,9},{9,8},{10,11... | collective-permute-start | bytes 589832 | tf_op jit(solution)/shard_map/ppermute | solution.py:439
  5.5 0.5 broadcast.94
  6.0 1.3 reduce.5
  7.3 0.7 fusion.9
  8.3 0.9 pad_maximum_fusion.2.rows_ref
  9.2 0.5 and_select_fusion.1.slot_ref
  9.7 2.5 pack_runs.2
  12.3 1.0 broadcast_select_fusion.6
  13.4 0.6 copy-done.9
  13.9 0.4 collective-permute-start.2
  14.3 10.3 %all-to-all-start = ((f32[64,4,512]{2,1,0:T(4,128)}), f32[64,4,512]{2,1,0:T(4,128)S(1)}, u32[]{:S(2)}, u32[]{:S(2)}) async-start(f32[64,4,512]{2,1,0:T(4,128)} %pack_runs.2), calls=%async_computation | async-start | bytes 1048576 | tf_op jit(solution)/shard_map/all_to_all | solution.py:427
  24.7 1.5 collective-permute-start.1
  26.1 1.5 collective-permute-start.3
  27.6 1.4 collective-permute-start.7
  29.1 9.5 %collective-permute-done.1 = f32[128,768]{1,0:T(8,128)S(1)} collective-permute-done((f32[128,768]{1,0:T(8,128)S(1)}, f32[128,768]{1,0:T(8,128)S(1)}, u32[]{:S(2)}, u32[]{:S(2)}) %collective-permute-start.1) | collective-permute-done | bytes 393248 | tf_op jit(solution)/shard_map/ppermute | solution.py:61
  38.6 0.3 collective-permute-start.4
  38.9 2.4 collective-permute-start.5
  41.3 0.3 collective-permute-done.7
  41.7 0.8 collective-permute-done.6
  42.5 4.5 %collective-permute-done.4 = f32[128,768]{1,0:T(8,128)S(1)} collective-permute-done((f32[128,768]{1,0:T(8,128)S(1)}, f32[128,768]{1,0:T(8,128)S(1)}, u32[]{:S(2)}, u32[]{:S(2)}) %collective-permute-start.4) | collective-permute-done | bytes 393248 | tf_op jit(solution)/shard_map/ppermute | solution.py:61
  47.1 1.7 pad_maximum_fusion
  48.8 1.0 collective-permute-start.8
  49.7 1.8 collective-permute-start.10
  51.5 1.2 collective-permute-start.13
  52.7 0.3 collective-permute-start.12
  53.0 16.7 %collective-permute-done.8.refs_1_ = f32[512,768]{1,0:T(8,128)} collective-permute-done((f32[512,768]{1,0:T(8,128)S(1)}, f32[512,768]{1,0:T(8,128)}, u32[]{:S(2)}, u32[]{:S(2)}) %collective-permute-start.8) | collective-permute-done | bytes 1572896 | tf_op jit(solution)/shard_map/ppermute | solution.py:61
  69.7 2.7 %collective-permute-start.11 = (f32[512,768]{1,0:T(8,128)}, f32[512,768]{1,0:T(8,128)}, u32[]{:S(2)}, u32[]{:S(2)}) collective-permute-start(f32[512,768]{1,0:T(8,128)} %collective-permute-done.10.refs_6_), channel_id=1, source_target_pairs={{0,96},{2,14},{4,100},{6,2},{8,104},{10,6},{12,108},{14,10},{16,11... | collective-permute-start | bytes 4718600 | tf_op jit(solution)/shard_map/ppermute | solution.py:61
  72.4 2.1 collective-permute-start.14
  74.5 11.7 %collective-permute-done.13.refs_2_ = f32[512,768]{1,0:T(8,128)S(1)} collective-permute-done((f32[512,768]{1,0:T(8,128)S(1)}, f32[512,768]{1,0:T(8,128)S(1)}, u32[]{:S(2)}, u32[]{:S(2)}) %collective-permute-start.13) | collective-permute-done | bytes 1572896 | tf_op jit(solution)/shard_map/ppermute | solution.py:61
  86.2 2.1 collective-permute-start.18
  88.3 1.2 copy-done.8
  89.5 1.1 collective-permute-start.15
  90.6 0.7 constant_dynamic-slice_fusion
  91.3 0.6 fusion.5
  91.9 0.6 slice_bitcast_fusion.order_ref
  92.5 10.9 %collective-permute-done.9.refs_3_ = f32[512,768]{1,0:T(8,128)} collective-permute-done((f32[512,768]{1,0:T(8,128)}, f32[512,768]{1,0:T(8,128)}, u32[]{:S(2)}, u32[]{:S(2)}) %collective-permute-start.9) | collective-permute-done | bytes 1572896 | tf_op jit(solution)/shard_map/ppermute | solution.py:61
  103.4 1.1 collective-permute-start.24
  104.5 0.6 slice_bitcast_fusion.1.place_ref
  105.1 2.0 reshape.86
  107.1 1.8 slice.111
  108.9 1.8 collective-permute-start.20
  110.7 1.8 collective-permute-start.16
  112.5 0.4 collective-permute-start.19
  113.1 0.9 slice_convert_fusion
  114.1 0.7 fusion.4.place_ref
  114.8 7.9 %pack_runs.3 = f32[64,4,8192]{2,1,0:T(4,128)} custom-call(s32[64]{0:T(128)} %and_select_fusion.1.slot_ref, f32[256,8192]{1,0:T(8,128)} %rows_ref.1), custom_call_target="tpu_custom_call" | custom-call | bytes 16777216 | tf_op jit(solution)/shard_map/pack_runs/pallas_call | solution.py:108
  122.8 1.0 broadcast_select_fusion.4
  123.8 1.1 collective-permute-start.23
  125.0 3.1 %head_rows.1 = (f32[384,768]{1,0:T(8,128)}, f32[768,128]{1,0:T(8,128)}) custom-call(s32[8]{0:T(128)} %slice_bitcast_fusion.1.place_ref, s32[1]{0:T(128)} %bitcast.2.col_ref, f32[512,768]{1,0:T(8,128)} %copy-done.1, f32[512,768]{1,0:T(8,128)} %collective-permute-done.8.refs_1_, f32[512,768]{1,0:T(8,128)} %copy-done.7, ...), custom_call_target="tpu_custom_call" | custom-call | bytes 4000000 | tf_op jit(solution)/shard_map/head_rows/pallas_call | solution.py:154
  128.1 2.0 collective-permute-start.22
  130.1 5.8 %collective-permute-done.23 = f32[256,384]{1,0:T(8,128)S(1)} collective-permute-done((f32[256,384]{1,0:T(8,128)}, f32[256,384]{1,0:T(8,128)S(1)}, u32[]{:S(2)}, u32[]{:S(2)}) %collective-permute-start.23) | collective-permute-done | bytes 393248 | tf_op jit(solution)/shard_map/ppermute | solution.py:449
  136.0 8.4 %collective-permute-done.22.lower_ref = f32[768,128]{1,0:T(8,128)S(1)} collective-permute-done((f32[768,128]{1,0:T(8,128)}, f32[768,128]{1,0:T(8,128)S(1)}, u32[]{:S(2)}, u32[]{:S(2)}) %collective-permute-start.22) | collective-permute-done | bytes 393248 | tf_op jit(solution)/shard_map/ppermute | solution.py:458
  144.4 0.7 copy-done.22
  145.1 8.5 %all-to-all-start.1 = ((f32[64,4,8192]{2,1,0:T(4,128)}), f32[64,4,8192]{2,1,0:T(4,128)}, u32[]{:S(2)}, u32[]{:S(2)}) async-start(f32[64,4,8192]{2,1,0:T(4,128)} %pack_runs.3), calls=%async_computation.1 | async-start | bytes 16777216 | tf_op jit(solution)/shard_map/all_to_all | solution.py:427
  153.7 44.6 %inverse_factor.1 = f32[768,768]{1,0:T(8,128)} custom-call(s32[1]{0:T(128)} %bitcast.2.col_ref, f32[384,768]{1,0:T(8,128)} %get-tuple-element.44.rows_ref, f32[768,128]{1,0:T(8,128)} %copy-done.22), custom_call_target="tpu_custom_call" | custom-call | flops 199999995904 | bytes 5000000 | tf_op jit(solution)/shard_map/inverse_factor/pallas_call | solution.py:269
  198.6 0.8 copy-done.6
  199.5 0.8 copy-done
  200.3 3.1 %convolution_select_fusion = f32[256,768]{1,0:T(8,128)} fusion(f32[768,768]{1,0:T(8,128)S(1)} %copy-done, f32[128,768]{1,0:T(8,128)S(1)} %get-tuple-element.53, f32[128,768]{1,0:T(8,128)S(1)} %get-tuple-element.52, pred[768]{0:T(1024)(128)(4,1)S(1)} %copy-done.21), kind=kOutput, calls=%fused_computation.2 | convolution fusion | flops 1812332544 | bytes 3932928 | tf_op jit(solution)/shard_map/dot_general | solution.py:27
  203.3 2.2 fusion.12
  205.5 3.1 %fusion.13.x_ref = f32[256,768]{1,0:T(8,128)} fusion(f32[256,768]{1,0:T(8,128)S(1)} %fusion.12, f32[768,768]{1,0:T(8,128)S(1)} %copy-done), kind=kOutput, calls=%fused_computation.63 | convolution fusion | flops 1811939328 | bytes 3932160 | tf_op jit(solution)/shard_map/dot_general | solution.py:33
  208.6 21.7 %update_of.1.update_ref = f32[256,8192]{1,0:T(8,128)} custom-call(s32[64]{0:T(128)} %slice_bitcast_fusion.order_ref, f32[256,768]{1,0:T(8,128)} %fusion.13.x_ref, f32[512,768]{1,0:T(8,128)} %copy-done.1, f32[512,768]{1,0:T(8,128)} %collective-permute-done.8.refs_1_, f32[512,768]{1,0:T(8,128)} %copy-done.7, f32[512,768]{1,0:T(8,128)} %collective-permute-done.9.refs_3_, ...), custom_call_target="tpu_custom_call" | custom-call | flops 9663676416 | bytes 34000000 | tf_op jit(solution)/shard_map/update_of/pallas_call | solution.py:351
  230.3 25.5 %all-to-all-done.1.arrived_ref = f32[64,4,8192]{2,1,0:T(4,128)} async-done(((f32[64,4,8192]{2,1,0:T(4,128)}), f32[64,4,8192]{2,1,0:T(4,128)}, u32[]{:S(2)}, u32[]{:S(2)}) %all-to-all-start.1) | async-done | bytes 8388640 | tf_op jit(solution)/shard_map/all_to_all | solution.py:427
  255.7 10.8 %place_rows.1 = f32[256,8192]{1,0:T(8,128)} custom-call(bf16[256,256]{1,0:T(8,128)(2,1)} %fusion.4.place_ref, f32[64,4,8192]{2,1,0:T(4,128)} %all-to-all-done.1.arrived_ref, f32[256,8192]{1,0:T(8,128)} %update_of.1.update_ref), custom_call_target="tpu_custom_call" | custom-call | flops 2147483648 | bytes 25165824 | tf_op jit(solution)/shard_map/place_rows/pallas_call | solution.py:392
  (90 shorter events, 1.3 us)
Async XLA Ops:
  0.6 7.7 %slice-start = ((f32[256,8192]{1,0:T(8,128)}), f32[256,384]{1,0:T(8,128)S(1)}, s32[]{:S(2)}) async-start(f32[256,8192]{1,0:T(8,128)} %rows_ref.1), calls=%async_computation.2 | async-start | bytes 786432 | tf_op jit(solution)/shard_map/slice | solution.py:436
  1.6 10.6 %collective-permute-start = (f32[128,384]{1,0:T(8,128)S(1)}, f32[128,384]{1,0:T(8,128)S(1)}, u32[]{:S(2)}, u32[]{:S(2)}) collective-permute-start(f32[128,384]{1,0:T(8,128)S(1)} %constant_dynamic-slice_fusion.1), channel_id=1, source_target_pairs={{0,1},{1,0},{2,3},{3,2},{4,5},{5,4},{6,7},{7,6},{8,9},{9,8},{10,11... | collective-permute-start | bytes 589832 | tf_op jit(solution)/shard_map/ppermute | solution.py:439
  13.2 0.7 copy-start.9
  13.9 34.8 %copy-start.5 = (f32[128,768]{1,0:T(8,128)}, f32[128,768]{1,0:T(8,128)S(1)}, u32[]{:S(2)}) copy-start(f32[128,768]{1,0:T(8,128)S(1)} %slice_dynamic-update-slice_fusion.12) | copy-start | bytes 1179652
  13.9 12.2 %collective-permute-start.2 = (f32[128,768]{1,0:T(8,128)S(1)}, f32[128,768]{1,0:T(8,128)S(1)}, u32[]{:S(2)}, u32[]{:S(2)}) collective-permute-start(f32[128,768]{1,0:T(8,128)S(1)} %slice_dynamic-update-slice_fusion.12), channel_id=1, source_target_pairs={{0,16},{2,18},{4,20},{6,22},{8,24},{10,26},{12,28},{14,30},{16,0},... | collective-permute-start | bytes 1179656 | tf_op jit(solution)/shard_map/ppermute | solution.py:61
  14.3 24.3 %all-to-all-start = ((f32[64,4,512]{2,1,0:T(4,128)}), f32[64,4,512]{2,1,0:T(4,128)S(1)}, u32[]{:S(2)}, u32[]{:S(2)}) async-start(f32[64,4,512]{2,1,0:T(4,128)} %pack_runs.2), calls=%async_computation | async-start | bytes 1048576 | tf_op jit(solution)/shard_map/all_to_all | solution.py:427
  24.7 13.9 %collective-permute-start.1 = (f32[128,768]{1,0:T(8,128)S(1)}, f32[128,768]{1,0:T(8,128)S(1)}, u32[]{:S(2)}, u32[]{:S(2)}) collective-permute-start(f32[128,768]{1,0:T(8,128)S(1)} %slice_dynamic-update-slice_fusion.12), channel_id=1, source_target_pairs={{0,4},{2,34},{4,8},{6,38},{8,12},{10,42},{12,0},{14,46},{16,20},{1... | collective-permute-start | bytes 1179656 | tf_op jit(solution)/shard_map/ppermute | solution.py:61
  26.1 20.9 %copy-start.12 = (f32[128,768]{1,0:T(8,128)}, f32[128,768]{1,0:T(8,128)S(1)}, u32[]{:S(2)}) copy-start(f32[128,768]{1,0:T(8,128)S(1)} %collective-permute-done.2) | copy-start | bytes 1179652
  26.1 12.5 %collective-permute-start.3 = (f32[128,768]{1,0:T(8,128)S(1)}, f32[128,768]{1,0:T(8,128)S(1)}, u32[]{:S(2)}, u32[]{:S(2)}) collective-permute-start(f32[128,768]{1,0:T(8,128)S(1)} %collective-permute-done.2), channel_id=1, source_target_pairs={{0,12},{2,98},{4,0},{6,102},{8,4},{10,106},{12,8},{14,110},{16,28}... | collective-permute-start | bytes 1179656 | tf_op jit(solution)/shard_map/ppermute | solution.py:61
  27.6 14.0 %collective-permute-start.7 = (f32[128,768]{1,0:T(8,128)S(1)}, f32[128,768]{1,0:T(8,128)S(1)}, u32[]{:S(2)}, u32[]{:S(2)}) collective-permute-start(f32[128,768]{1,0:T(8,128)S(1)} %slice_dynamic-update-slice_fusion.12), channel_id=1, source_target_pairs={{0,12},{2,98},{4,0},{6,102},{8,4},{10,106},{12,8},{14,110},{16,28}... | collective-permute-start | bytes 1179656 | tf_op jit(solution)/shard_map/ppermute | solution.py:61
  29.0 13.5 %collective-permute-start.6 = (f32[128,768]{1,0:T(8,128)S(1)}, f32[128,768]{1,0:T(8,128)S(1)}, u32[]{:S(2)}, u32[]{:S(2)}) collective-permute-start(f32[128,768]{1,0:T(8,128)S(1)} %collective-permute-done.2), channel_id=1, source_target_pairs={{0,4},{2,34},{4,8},{6,38},{8,12},{10,42},{12,0},{14,46},{16,20},{1... | collective-permute-start | bytes 1179656 | tf_op jit(solution)/shard_map/ppermute | solution.py:61
  38.6 8.4 %copy-start.13 = (f32[128,768]{1,0:T(8,128)}, f32[128,768]{1,0:T(8,128)S(1)}, u32[]{:S(2)}) copy-start(f32[128,768]{1,0:T(8,128)S(1)} %collective-permute-done.1) | copy-start | bytes 1179652
  38.6 8.4 %copy-start.4 = (f32[64,4,512]{2,1,0:T(4,128)}, f32[64,4,512]{2,1,0:T(4,128)S(1)}, u32[]{:S(2)}) copy-start(f32[64,4,512]{2,1,0:T(4,128)S(1)} %all-to-all-done) | copy-start | bytes 1572868
  38.6 8.4 %copy-start.14 = (f32[128,768]{1,0:T(8,128)}, f32[128,768]{1,0:T(8,128)S(1)}, u32[]{:S(2)}) copy-start(f32[128,768]{1,0:T(8,128)S(1)} %collective-permute-done.3) | copy-start | bytes 1179652
  38.6 8.4 %collective-permute-start.4 = (f32[128,768]{1,0:T(8,128)S(1)}, f32[128,768]{1,0:T(8,128)S(1)}, u32[]{:S(2)}, u32[]{:S(2)}) collective-permute-start(f32[128,768]{1,0:T(8,128)S(1)} %collective-permute-done.1), channel_id=1, source_target_pairs={{0,4},{2,34},{4,8},{6,38},{8,12},{10,42},{12,0},{14,46},{16,20},{1... | collective-permute-start | bytes 1179656 | tf_op jit(solution)/shard_map/ppermute | solution.py:61
  38.9 8.1 %collective-permute-start.5 = (f32[128,768]{1,0:T(8,128)S(1)}, f32[128,768]{1,0:T(8,128)S(1)}, u32[]{:S(2)}, u32[]{:S(2)}) collective-permute-start(f32[128,768]{1,0:T(8,128)S(1)} %collective-permute-done.3), channel_id=1, source_target_pairs={{0,12},{2,98},{4,0},{6,102},{8,4},{10,106},{12,8},{14,110},{16,28}... | collective-permute-start | bytes 1179656 | tf_op jit(solution)/shard_map/ppermute | solution.py:61
  41.7 5.4 %copy-start.15 = (f32[128,768]{1,0:T(8,128)}, f32[128,768]{1,0:T(8,128)S(1)}, u32[]{:S(2)}) copy-start(f32[128,768]{1,0:T(8,128)S(1)} %collective-permute-done.7) | copy-start | bytes 1179652
  42.5 4.5 %copy-start.16 = (f32[128,768]{1,0:T(8,128)}, f32[128,768]{1,0:T(8,128)S(1)}, u32[]{:S(2)}) copy-start(f32[128,768]{1,0:T(8,128)S(1)} %collective-permute-done.6) | copy-start | bytes 1179652
  48.7 74.0 %copy-start.1 = (f32[512,768]{1,0:T(8,128)}, f32[512,768]{1,0:T(8,128)S(1)}, u32[]{:S(2)}) copy-start(f32[512,768]{1,0:T(8,128)S(1)} %get-tuple-element.34.refs_0_) | copy-start | bytes 4718596
  48.8 74.0 %copy-start.2 = (f32[512,768]{1,0:T(8,128)}, f32[512,768]{1,0:T(8,128)S(1)}, u32[]{:S(2)}) copy-start(f32[512,768]{1,0:T(8,128)S(1)} %get-tuple-element.35.refs_4_) | copy-start | bytes 4718596
  48.8 20.9 %collective-permute-start.8 = (f32[512,768]{1,0:T(8,128)S(1)}, f32[512,768]{1,0:T(8,128)}, u32[]{:S(2)}, u32[]{:S(2)}) collective-permute-start(f32[512,768]{1,0:T(8,128)S(1)} %get-tuple-element.34.refs_0_), channel_id=1, source_target_pairs={{0,32},{2,6},{4,36},{6,10},{8,40},{10,14},{12,44},{14,2},{16,48},{... | collective-permute-start | bytes 4718600 | tf_op jit(solution)/shard_map/ppermute | solution.py:61
  49.7 20.0 %collective-permute-start.10 = (f32[512,768]{1,0:T(8,128)S(1)}, f32[512,768]{1,0:T(8,128)}, u32[]{:S(2)}, u32[]{:S(2)}) collective-permute-start(f32[512,768]{1,0:T(8,128)S(1)} %get-tuple-element.35.refs_4_), channel_id=1, source_target_pairs={{0,96},{2,14},{4,100},{6,2},{8,104},{10,6},{12,108},{14,10},{16,11... | collective-permute-start | bytes 4718600 | tf_op jit(solution)/shard_map/ppermute | solution.py:61
  51.5 34.6 %collective-permute-start.13 = (f32[512,768]{1,0:T(8,128)S(1)}, f32[512,768]{1,0:T(8,128)S(1)}, u32[]{:S(2)}, u32[]{:S(2)}) collective-permute-start(f32[512,768]{1,0:T(8,128)S(1)} %get-tuple-element.34.refs_0_), channel_id=1, source_target_pairs={{0,96},{2,14},{4,100},{6,2},{8,104},{10,6},{12,108},{14,10},{16,11... | collective-permute-start | bytes 4718600 | tf_op jit(solution)/shard_map/ppermute | solution.py:61
  52.7 35.6 %collective-permute-start.12 = (f32[512,768]{1,0:T(8,128)S(1)}, f32[512,768]{1,0:T(8,128)S(1)}, u32[]{:S(2)}, u32[]{:S(2)}) collective-permute-start(f32[512,768]{1,0:T(8,128)S(1)} %get-tuple-element.35.refs_4_), channel_id=1, source_target_pairs={{0,32},{2,6},{4,36},{6,10},{8,40},{10,14},{12,44},{14,2},{16,48},{... | collective-permute-start | bytes 4718600 | tf_op jit(solution)/shard_map/ppermute | solution.py:61
  69.7 33.7 %collective-permute-start.9 = (f32[512,768]{1,0:T(8,128)}, f32[512,768]{1,0:T(8,128)}, u32[]{:S(2)}, u32[]{:S(2)}) collective-permute-start(f32[512,768]{1,0:T(8,128)} %collective-permute-done.8.refs_1_), channel_id=1, source_target_pairs={{0,32},{2,6},{4,36},{6,10},{8,40},{10,14},{12,44},{14,2},{16,48},{... | collective-permute-start | bytes 4718600 | tf_op jit(solution)/shard_map/ppermute | solution.py:61
  69.7 39.2 %collective-permute-start.11 = (f32[512,768]{1,0:T(8,128)}, f32[512,768]{1,0:T(8,128)}, u32[]{:S(2)}, u32[]{:S(2)}) collective-permute-start(f32[512,768]{1,0:T(8,128)} %collective-permute-done.10.refs_6_), channel_id=1, source_target_pairs={{0,96},{2,14},{4,100},{6,2},{8,104},{10,6},{12,108},{14,10},{16,11... | collective-permute-start | bytes 4718600 | tf_op jit(solution)/shard_map/ppermute | solution.py:61
  72.4 40.1 %collective-permute-start.14 = (f32[512,768]{1,0:T(8,128)S(1)}, f32[512,768]{1,0:T(8,128)}, u32[]{:S(2)}, u32[]{:S(2)}) collective-permute-start(f32[512,768]{1,0:T(8,128)S(1)} %get-tuple-element.34.refs_0_), channel_id=1, source_target_pairs={{0,2},{2,0},{4,6},{6,4},{8,10},{10,8},{12,14},{14,12},{16,18},{18,... | collective-permute-start | bytes 4718600 | tf_op jit(solution)/shard_map/ppermute | solution.py:61
  86.2 2.1 copy-start.7
  86.2 26.4 %collective-permute-start.18 = (f32[512,768]{1,0:T(8,128)S(1)}, f32[512,768]{1,0:T(8,128)}, u32[]{:S(2)}, u32[]{:S(2)}) collective-permute-start(f32[512,768]{1,0:T(8,128)S(1)} %get-tuple-element.35.refs_4_), channel_id=1, source_target_pairs={{0,2},{2,0},{4,6},{6,4},{8,10},{10,8},{12,14},{14,12},{16,18},{18,... | collective-permute-start | bytes 4718600 | tf_op jit(solution)/shard_map/ppermute | solution.py:61
  88.3 1.2 copy-start.8
  89.5 23.5 %collective-permute-start.15 = (f32[512,768]{1,0:T(8,128)}, f32[512,768]{1,0:T(8,128)}, u32[]{:S(2)}, u32[]{:S(2)}) collective-permute-start(f32[512,768]{1,0:T(8,128)} %collective-permute-done.8.refs_1_), channel_id=1, source_target_pairs={{0,2},{2,0},{4,6},{6,4},{8,10},{10,8},{12,14},{14,12},{16,18},{18,... | collective-permute-start | bytes 4718600 | tf_op jit(solution)/shard_map/ppermute | solution.py:61
  103.4 7.3 %collective-permute-start.24 = (f32[128,384]{1,0:T(8,128)}, f32[128,384]{1,0:T(8,128)S(1)}, u32[]{:S(2)}, u32[]{:S(2)}) collective-permute-start(f32[128,384]{1,0:T(8,128)} %copy-done.9), channel_id=1, source_target_pairs={{0,1},{1,0},{2,3},{3,2},{4,5},{5,4},{6,7},{7,6},{8,9},{9,8},{10,11... | collective-permute-start | bytes 589832 | tf_op jit(solution)/shard_map/ppermute | solution.py:450
  108.9 14.9 %collective-permute-start.20 = (f32[512,768]{1,0:T(8,128)}, f32[512,768]{1,0:T(8,128)}, u32[]{:S(2)}, u32[]{:S(2)}) collective-permute-start(f32[512,768]{1,0:T(8,128)} %collective-permute-done.10.refs_6_), channel_id=1, source_target_pairs={{0,2},{2,0},{4,6},{6,4},{8,10},{10,8},{12,14},{14,12},{16,18},{18,... | collective-permute-start | bytes 4718600 | tf_op jit(solution)/shard_map/ppermute | solution.py:61
  110.7 2.3 copy-start.19
  110.7 14.3 %collective-permute-start.16 = (f32[512,768]{1,0:T(8,128)}, f32[512,768]{1,0:T(8,128)}, u32[]{:S(2)}, u32[]{:S(2)}) collective-permute-start(f32[512,768]{1,0:T(8,128)} %copy-done.7), channel_id=1, source_target_pairs={{0,2},{2,0},{4,6},{6,4},{8,10},{10,8},{12,14},{14,12},{16,18},{18,... | collective-permute-start | bytes 4718600 | tf_op jit(solution)/shard_map/ppermute | solution.py:61
  112.5 12.5 %collective-permute-start.17 = (f32[512,768]{1,0:T(8,128)}, f32[512,768]{1,0:T(8,128)}, u32[]{:S(2)}, u32[]{:S(2)}) collective-permute-start(f32[512,768]{1,0:T(8,128)} %collective-permute-done.9.refs_3_), channel_id=1, source_target_pairs={{0,2},{2,0},{4,6},{6,4},{8,10},{10,8},{12,14},{14,12},{16,18},{18,... | collective-permute-start | bytes 4718600 | tf_op jit(solution)/shard_map/ppermute | solution.py:61
  112.5 12.4 %collective-permute-start.19 = (f32[512,768]{1,0:T(8,128)}, f32[512,768]{1,0:T(8,128)}, u32[]{:S(2)}, u32[]{:S(2)}) collective-permute-start(f32[512,768]{1,0:T(8,128)} %copy-done.8), channel_id=1, source_target_pairs={{0,2},{2,0},{4,6},{6,4},{8,10},{10,8},{12,14},{14,12},{16,18},{18,... | collective-permute-start | bytes 4718600 | tf_op jit(solution)/shard_map/ppermute | solution.py:61
  113.0 12.0 %collective-permute-start.21 = (f32[512,768]{1,0:T(8,128)}, f32[512,768]{1,0:T(8,128)}, u32[]{:S(2)}, u32[]{:S(2)}) collective-permute-start(f32[512,768]{1,0:T(8,128)} %collective-permute-done.11.refs_7_), channel_id=1, source_target_pairs={{0,2},{2,0},{4,6},{6,4},{8,10},{10,8},{12,14},{14,12},{16,18},{18,... | collective-permute-start | bytes 4718600 | tf_op jit(solution)/shard_map/ppermute | solution.py:61
  114.8 7.9 %copy-start.20 = (f32[128,384]{1,0:T(8,128)S(1)}, f32[128,384]{1,0:T(8,128)}, u32[]{:S(2)}) copy-start(f32[128,384]{1,0:T(8,128)} %copy-done.19) | copy-start | bytes 589828
  123.8 12.1 %collective-permute-start.23 = (f32[256,384]{1,0:T(8,128)}, f32[256,384]{1,0:T(8,128)S(1)}, u32[]{:S(2)}, u32[]{:S(2)}) collective-permute-start(f32[256,384]{1,0:T(8,128)} %slice.111), channel_id=1, source_target_pairs={{0,1},{1,0},{2,3},{3,2},{4,5},{5,4},{6,7},{7,6},{8,9},{9,8},{10,11... | collective-permute-start | bytes 1179656 | tf_op jit(solution)/shard_map/ppermute | solution.py:449
  128.1 16.2 %collective-permute-start.22 = (f32[768,128]{1,0:T(8,128)}, f32[768,128]{1,0:T(8,128)S(1)}, u32[]{:S(2)}, u32[]{:S(2)}) collective-permute-start(f32[768,128]{1,0:T(8,128)} %get-tuple-element.40), channel_id=1, source_target_pairs={{0,1},{1,0},{2,3},{3,2},{4,5},{5,4},{6,7},{7,6},{8,9},{9,8},{10,11... | collective-permute-start | bytes 1179656 | tf_op jit(solution)/shard_map/ppermute | solution.py:458
  130.1 14.2 %copy-start.10 = (f32[128,768]{1,0:T(8,128)}, f32[128,768]{1,0:T(8,128)S(1)}, u32[]{:S(2)}) copy-start(f32[128,768]{1,0:T(8,128)S(1)} %slice_dynamic-update-slice_fusion.6) | copy-start | bytes 1179652
  136.0 8.4 %copy-start.17 = (f32[256,384]{1,0:T(8,128)}, f32[256,384]{1,0:T(8,128)S(1)}, u32[]{:S(2)}) copy-start(f32[256,384]{1,0:T(8,128)S(1)} %collective-permute-done.23) | copy-start | bytes 1179652
  144.4 0.7 copy-start.22
  145.1 110.6 %all-to-all-start.1 = ((f32[64,4,8192]{2,1,0:T(4,128)}), f32[64,4,8192]{2,1,0:T(4,128)}, u32[]{:S(2)}, u32[]{:S(2)}) async-start(f32[64,4,8192]{2,1,0:T(4,128)} %pack_runs.3), calls=%async_computation.1 | async-start | bytes 16777216 | tf_op jit(solution)/shard_map/all_to_all | solution.py:427
  153.7 44.7 %copy-start.3 = (f32[256,512]{1,0:T(8,128)S(1)}, f32[256,512]{1,0:T(8,128)}, u32[]{:S(2)}) copy-start(f32[256,512]{1,0:T(8,128)} %reshape.86) | copy-start | bytes 1572868
  153.7 44.7 %copy-start.18 = (f32[256,384]{1,0:T(8,128)S(1)}, f32[256,384]{1,0:T(8,128)}, u32[]{:S(2)}) copy-start(f32[256,384]{1,0:T(8,128)} %copy-done.17) | copy-start | bytes 1179652
  198.3 1.0 copy-start.6
  198.3 1.1 copy-start.11
  198.4 1.9 copy-start
  198.4 1.9 copy-start.21
